TPU v7x, 256 devices: a whole 4x4x8 slice. The times are simulated.
256 devices in a mesh: dp: 8 (over z_lo, y), frame: 8 (over x, core), row: 4 (over z_hi).
Axes of the slice: x: 4, y: 4, z: 8 (z_hi: 4, z_lo: 2; z = z_hi * 2 + z_lo), core: 2. Of those that a mesh axis runs over, the one named last changes fastest.
Arguments:
- latents: bfloat16 [8, 8, 32, 32, 640], P('dp', 'frame', 'row'), may hold values from -6 to 6
- space_kernel: bfloat16 [3, 3, 640, 640], replicated, may hold values from -0.078125 to 0.078125
- time_kernel: bfloat16 [1920, 640], P('dp'), may hold values from -0.125 to 0.125
- qkv_weight: bfloat16 [640, 1920], P('dp'), may hold values from -4 to 4
- out_weight: bfloat16 [640, 640], P('dp'), may hold values from -0.25 to 0.25
- norm_gain: float32 [640], replicated, may hold values from 0.25 to 1.75
- grad_out: bfloat16 [8, 8, 32, 32, 640], P('dp', 'frame', 'row'), may hold values from -6 to 6
Outputs:
- grad_latents: bfloat16 [8, 8, 32, 32, 640], P('dp', 'frame', 'row')
- grad_qkv: float32 [640, 1920], P('dp', ('frame', 'row'))
- grad_outproj: float32 [640, 640], P('dp', ('frame', 'row'))
All inputs are finite; a program needn't handle non-finite values.
Results may differ from a plain program's by a relative error of at most 0.04.
Values may be sent and summed in bfloat16 or wider, within the bound.
No kernel may reach another device: no remote copies, remote signals or barrier semaphores. Data moves between devices by JAX's collectives and lax.ppermute only.
A program may use at most 128 MiB of HBM per device.

v0:
```python
import functools

import jax
import jax.numpy as jnp
from jax import lax
from jax.experimental import pallas as pl
from jax.experimental.pallas import tpu as pltpu
from jax.sharding import Mesh
from jax.sharding import PartitionSpec as P

HEAD_DIM = 64
C = 640
F32 = jnp.float32
BF16 = jnp.bfloat16
VIDEO = ("zl", "y")
FRAME = ("x", "c")
MIB = 1 << 20


def sds(shape, dtype=BF16):
    return jax.ShapeDtypeStruct(shape, dtype)


AXES = ("zl", "y", "x", "c", "zh")


def call(body, outs, n_vmem, n_any, scratch=(), limit=12, flops=0, moved=0):
    def placed_body(*refs):
        body([lax.axis_index(name) for name in AXES], *refs)

    specs = [pl.BlockSpec(memory_space=pltpu.VMEM)] * n_vmem
    specs += [pl.BlockSpec(memory_space=pl.ANY)] * n_any
    return pl.pallas_call(
        placed_body,
        out_shape=outs,
        in_specs=specs,
        out_specs=[pl.BlockSpec(memory_space=pltpu.VMEM)] * len(outs),
        scratch_shapes=list(scratch),
        compiler_params=pltpu.CompilerParams(vmem_limit_bytes=limit * MIB),
        cost_estimate=pl.CostEstimate(flops=flops, bytes_accessed=moved, transcendentals=0),
    )


def mm(a, b):
    return lax.dot_general(a, b, (((1,), (0,)), ((), ())), preferred_element_type=F32)


def mm_nt(a, b):
    return lax.dot_general(a, b, (((1,), (1,)), ((), ())), preferred_element_type=F32)


def mm_tn(a, b):
    return lax.dot_general(a, b, (((0,), (0,)), ((), ())), preferred_element_type=F32)


def shifted_columns(images_ref, low_ref, high_ref, zh, shifts_ref, order):
    low = low_ref[...].astype(F32) * jnp.where(zh > 0, 1.0, 0.0)
    high = high_ref[...].astype(F32) * jnp.where(zh < 3, 1.0, 0.0)
    whole = jnp.concatenate([low, images_ref[...].astype(F32), high], axis=0)
    flat = whole.reshape(320, C)
    column = lax.broadcasted_iota(jnp.int32, (320, C), 0) % 32
    before = jnp.where(column == 0, 0.0, pltpu.roll(flat, 1, 0))
    after = jnp.where(column == 31, 0.0, pltpu.roll(flat, 319, 0))
    views = (before, flat, after)
    for j, which in enumerate(order):
        shifts_ref[:, j * C : (j + 1) * C] = views[which].astype(BF16)


def kernel_copies(kernel_hbm, kernel_ref, sems):
    return [
        pltpu.make_async_copy(kernel_hbm.at[pl.ds(dy, 1)], kernel_ref.at[pl.ds(dy, 1)], sems.at[dy])
        for dy in range(3)
    ]


def conv_forward_body(pos, images, low, high, grad_out, kernel_hbm, out, *rest):
    kernel_ref, shifts, sems = rest
    copies = kernel_copies(kernel_hbm, kernel_ref, sems)
    for copy in copies:
        copy.start()
    shifted_columns(images, low, high, pos[4], shifts, (0, 1, 2))
    total = images[...].astype(F32).reshape(256, C)
    for dy in range(3):
        copies[dy].wait()
        taps = kernel_ref[dy].reshape(3 * C, C)
        total = total + mm(shifts[32 * dy : 32 * dy + 256, :], taps)
    out[:, 0] = total.astype(BF16).reshape(8, 32, C)
    out[:, 1] = grad_out[...]


def conv_backward_body(pos, images, low, high, kernel_hbm, out, token, kernel_ref, shifts, sems):
    token[...] = jnp.zeros((8, 128), F32)
    copies = kernel_copies(kernel_hbm, kernel_ref, sems)
    for copy in copies:
        copy.start()
    shifted_columns(images, low, high, pos[4], shifts, (2, 1, 0))
    total = images[...].astype(F32).reshape(256, C)
    for dy in range(3):
        copies[dy].wait()
        at = 32 * (2 - dy)
        for dx in range(3):
            total = total + mm_nt(shifts[at : at + 256, dx * C : (dx + 1) * C], kernel_ref[dy, dx])
    out[...] = total.astype(BF16).reshape(8, 32, C)


CONV_SCRATCH = (pltpu.VMEM((3, 3, C, C), BF16), pltpu.VMEM((320, 3 * C), BF16))


def conv_forward(images, low, high, grad_out, kernel):
    return call(
        conv_forward_body,
        [sds((8, 2, 32, C))],
        4,
        1,
        CONV_SCRATCH + (pltpu.SemaphoreType.DMA((3,)),),
        limit=48,
        flops=2 * 256 * 9 * C * C,
        moved=9 * C * C * 2,
    )(images, low, high, grad_out, kernel)[0]


def conv_backward(images, low, high, kernel):
    return call(
        conv_backward_body,
        [sds((8, 32, C)), sds((8, 128), F32)],
        3,
        1,
        CONV_SCRATCH + (pltpu.SemaphoreType.DMA((3,)),),
        limit=48,
        flops=2 * 256 * 9 * C * C,
        moved=9 * C * C * 2,
    )(images, low, high, kernel)


def half_body(pos, time, half, sem):
    rows = time.at[pl.ds(pl.multiple_of(112 * pos[3], 16), 128)]
    copy = pltpu.make_async_copy(rows, half, sem)
    copy.start()
    copy.wait()


def half_time(time):
    dma = (pltpu.SemaphoreType.DMA,)
    return call(half_body, [sds((128, C))], 0, 1, dma, limit=62)(time)[0]


def half_projections_body(pos, qkv, out, *refs):
    core, (half, sems) = pos[3], refs[3:]

    def run(first, second):
        copies = [
            pltpu.make_async_copy(first, half.at[0:80], sems.at[0]),
            pltpu.make_async_copy(second, half.at[80:160], sems.at[1]),
        ]
        for copy in copies:
            copy.start()
        for copy in copies:
            copy.wait()

    @pl.when(core == 0)
    def _():
        run(qkv.at[:, 0:C], qkv.at[:, C : 2 * C])

    @pl.when(core == 1)
    def _():
        run(qkv.at[:, 2 * C : 3 * C], out)


def half_projections(qkv, out, after):
    dma = (pltpu.SemaphoreType.DMA((2,)),)
    return call(half_projections_body, [sds((160, C))], 0, 5, dma, limit=62)(qkv, out, *after)[0]


def gate(value, after):
    return pl.pallas_call(
        lambda a, b, c: None,
        out_shape=sds(value.shape, value.dtype),
        in_specs=[pl.BlockSpec(memory_space=pl.ANY)] * 2,
        out_specs=pl.BlockSpec(memory_space=pl.ANY),
        input_output_aliases={0: 0},
    )(value, after)


def four_body(pos, own, *refs):
    others, out = refs[:3], refs[-1]
    out[pos[1]] = own[...]
    for k in range(3):
        out[(pos[1] + 3 - k) % 4] = others[k][...]


def four(own, others, after):
    return call(four_body, [sds((4,) + own.shape)], 4, 1)(own, *others, after)[0]


def across(own):
    pairs = []
    for z in range(8):
        for core in range(2):
            to = (z + 7 + 2 * core) % 8
            pairs.append(tuple(((at % 2) * 2 + core) * 4 + at // 2 for at in (z, to)))
    return lax.ppermute(own, ("zl", "c", "zh"), pairs)


def swapped(value):
    return lax.ppermute(value, "c", [(0, 1), (1, 0)])


def time_copies(pos, pieces, target, sem):
    zl, core = pos[0], pos[3]
    copies = []
    for i, piece in enumerate(pieces):
        blocks = pl.ds(4 * (zl if i % 2 == 0 else 1 - zl), 4)
        half = core if i < 2 else 1 - core
        source = piece.at[:, pl.ds(pl.multiple_of(16 * half, 16), 112)]
        place = target.at[blocks, pl.ds(pl.multiple_of(128 * half, 16), 112)]
        copies.append(pltpu.make_async_copy(source, place, sem.at[i]))
        if i < 2:
            source = piece.at[:, pl.ds(pl.multiple_of(112 * (1 - half), 16), 16)]
            place = target.at[blocks, pl.ds(112, 16)]
            copies.append(pltpu.make_async_copy(source, place, sem.at[4 + i]))
    return copies


def projection_copies(pos, pieces, target, sem):
    zl, core = pos[0], pos[3]
    copies = []
    for i, piece in enumerate(pieces):
        blocks = pl.ds(4 * (zl if i % 2 == 0 else 1 - zl), 4)
        half = core if i < 2 else 1 - core
        for j in range(2):
            lanes = pl.ds(pl.multiple_of(1280 * half + 640 * j, 128), 640)
            source = piece.at[:, 80 * j : 80 * j + 80]
            copies.append(pltpu.make_async_copy(source, target.at[blocks, :, lanes], sem.at[2 * i + j]))
    return copies


def gathered(own, after):
    far = gate(across(own), after)
    return [own, far, swapped(own), swapped(far)]


def temporal_body(pos, tile, gain, *refs):
    time_pieces, (temporal_out, normal_out) = refs[:4], refs[4:6]
    time_ref, padded, sem = refs[6:]
    copies = time_copies(pos, time_pieces, time_ref, sem)
    for copy in copies:
        copy.start()
    value = tile[:, 0].astype(F32)
    padded[0] = jnp.zeros((32, C), BF16)
    padded[1:9] = (value * jax.nn.sigmoid(value)).astype(BF16)
    padded[9] = jnp.zeros((32, C), BF16)
    total = value.reshape(256, C)
    for copy in copies:
        copy.wait()
    taps = time_ref[...].reshape(3 * C, C)
    for k in range(3):
        total = total + mm(padded[k : k + 8].reshape(256, C), taps[k * C : (k + 1) * C, :])
    temporal = total.astype(BF16)
    temporal_out[...] = temporal
    value = temporal.astype(F32)
    scale = lax.rsqrt(jnp.mean(value * value, axis=-1, keepdims=True) + 1e-06)
    normal_out[...] = (value * scale * gain[...]).astype(BF16)


TIME_SCRATCH = (pltpu.VMEM((8, 240, C), BF16), pltpu.VMEM((10, 32, C), BF16))


def temporal_step(tile, gain, time_pieces):
    return call(
        temporal_body,
        [sds((256, C)), sds((256, C))],
        2,
        4,
        TIME_SCRATCH + (pltpu.SemaphoreType.DMA((6,)),),
        limit=20,
        flops=2 * 256 * 3 * C * C,
        moved=3 * C * C * 2,
    )(tile, gain, *time_pieces)


def attention_body(pos, normal, tile, *refs):
    weight_pieces, (grad_packed, keep, send) = refs[:4], refs[4:7]
    weight_ref, packed, grad_blend, blended, sem = refs[7:]
    copies = projection_copies(pos, weight_pieces, weight_ref, sem)
    for copy in copies:
        copy.start()
    for copy in copies:
        copy.wait()
    weight = weight_ref[...].reshape(C, 4 * C)
    packed[...] = mm(normal[...], weight[:, : 3 * C]).astype(BF16).reshape(8, 2, 16, 3 * C)
    arriving = tile[:, 1].reshape(256, C)
    grad_blend[...] = mm_nt(arriving, weight[:, 3 * C :]).astype(BF16).reshape(8, 2, 16, C)
    first_head = lax.broadcasted_iota(jnp.int32, (128, 128), 1) < HEAD_DIM
    row_pixel = lax.broadcasted_iota(jnp.int32, (256, 128), 0) % 16
    column_pixel = lax.broadcasted_iota(jnp.int32, (256, 128), 1) % 16
    same_pixel = row_pixel == column_pixel
    nothing = jnp.zeros((128, 128), BF16)

    def two_heads(block):
        return jnp.concatenate(
            [jnp.where(first_head, block, nothing), jnp.where(first_head, nothing, block)], axis=0
        )

    def merged(both):
        return jnp.where(first_head, both[:128], both[128:]).astype(BF16)

    for half in range(2):
        for pair in range(5):
            at = pair * 128

            def part(ref, offset):
                return ref[:, half, :, offset + at : offset + at + 128].reshape(128, 128)

            queries = two_heads(part(packed, 0))
            keys = part(packed, C)
            values = part(packed, 2 * C)
            scores = jnp.where(same_pixel, mm_nt(queries, keys) * HEAD_DIM**-0.5, -1e30)
            expons = jnp.exp(scores - jnp.max(scores, axis=-1, keepdims=True))
            probs = expons * (1.0 / jnp.sum(expons, axis=-1, keepdims=True))
            rounded = probs.astype(BF16)
            blended[:, half, :, at : at + 128] = merged(mm(rounded, values)).reshape(8, 16, 128)
            upper = two_heads(part(grad_blend, 0))
            grad_probs = mm_nt(upper, values)
            inner = jnp.sum(grad_probs * probs, axis=-1, keepdims=True)
            grad_scores = (probs * (grad_probs - inner) * HEAD_DIM**-0.5).astype(BF16)
            results = (
                merged(mm(grad_scores, keys)),
                mm_tn(grad_scores, queries).astype(BF16),
                mm_tn(rounded, upper).astype(BF16),
            )
            for i, result in enumerate(results):
                lanes = slice(i * C + at, i * C + at + 128)
                grad_packed[:, half, :, lanes] = result.reshape(8, 16, 128)

    core = pos[3]
    whole = grad_packed[...].reshape(256, 3 * C)

    def columns(array, width, which):
        starts = [(2 * x + which) * width for x in range(4)]
        return jnp.concatenate([array[:, s : s + width] for s in starts], axis=1)

    mixed = blended[...].reshape(256, C)
    qkv_parts = [columns(whole, 240, which) for which in range(2)]
    out_parts = [columns(arriving, 80, which) for which in range(2)]
    for target, swap in ((send, 0), (keep, 1)):
        first = core == swap
        qkv_side = jnp.where(first, qkv_parts[1], qkv_parts[0])
        out_side = jnp.where(first, out_parts[1], out_parts[0])
        target[:, 0:960] = mm_tn(normal[...], qkv_side).astype(BF16)
        target[:, 960:1280] = mm_tn(mixed, out_side).astype(BF16)


def attention_step(normal, tile, weight_pieces):
    return call(
        attention_body,
        [sds((8, 2, 16, 3 * C)), sds((C, 1280)), sds((C, 1280))],
        2,
        4,
        (
            pltpu.VMEM((8, 80, 4 * C), BF16),
            pltpu.VMEM((8, 2, 16, 3 * C), BF16),
            pltpu.VMEM((8, 2, 16, C), BF16),
            pltpu.VMEM((8, 2, 16, C), BF16),
            pltpu.SemaphoreType.DMA((8,)),
        ),
        limit=36,
        flops=2 * 256 * 10 * C * C,
        moved=4 * C * C * 2,
    )(normal, tile, *weight_pieces)


def tile_gradient_body(pos, *refs):
    grad_packed, temporal, tile, gain = refs[:4]
    weight_pieces, time_pieces, out = refs[4:8], refs[8:12], refs[13]
    weight_ref, time_ref, padded, sem, time_sem = refs[14:]
    copies = projection_copies(pos, weight_pieces, weight_ref, sem)
    later_copies = time_copies(pos, time_pieces, time_ref, time_sem)
    for copy in copies + later_copies:
        copy.start()
    for copy in copies:
        copy.wait()
    weight = weight_ref[...].reshape(C, 4 * C)[:, : 3 * C]
    grad_normal = mm_nt(grad_packed[...].reshape(256, 3 * C), weight)
    value = temporal[...].astype(F32)
    scale = lax.rsqrt(jnp.mean(value * value, axis=-1, keepdims=True) + 1e-06)
    scaled = grad_normal * gain[...]
    inner = jnp.mean(value * scaled, axis=-1, keepdims=True)
    through_norm = scale * scaled - value * (scale * scale * scale * inner)
    grad_temporal = (tile[:, 1].astype(F32).reshape(256, C) + through_norm).astype(BF16)
    padded[0] = jnp.zeros((32, C), BF16)
    padded[1:9] = grad_temporal.reshape(8, 32, C)
    padded[9] = jnp.zeros((32, C), BF16)
    for copy in later_copies:
        copy.wait()
    taps = time_ref[...].reshape(3 * C, C)
    grad_act = jnp.zeros((256, C), F32)
    for k in range(3):
        later = padded[2 - k : 10 - k].reshape(256, C)
        grad_act = grad_act + mm_nt(later, taps[k * C : (k + 1) * C, :])
    as_float = tile[:, 0].astype(F32).reshape(256, C)
    logistic = jax.nn.sigmoid(as_float)
    grad_spatial = grad_temporal.astype(F32) + grad_act * logistic * (
        1.0 + as_float * (1.0 - logistic)
    )
    out[...] = grad_spatial.astype(BF16).reshape(8, 32, C)


def tile_gradient(grad_packed, temporal, tile, gain, weights, times, after):
    return call(
        tile_gradient_body,
        [sds((8, 32, C))],
        4,
        9,
        (pltpu.VMEM((8, 80, 4 * C), BF16),)
        + TIME_SCRATCH
        + (pltpu.SemaphoreType.DMA((8,)), pltpu.SemaphoreType.DMA((6,))),
        limit=28,
        flops=2 * 256 * 6 * C * C,
        moved=7 * C * C * 2,
    )(grad_packed, temporal, tile, gain, *weights, *times, after)[0]


def pair_sum_body(pos, keep, other, own, *sends):
    y = pos[1]

    def block(index):
        return keep[:, index].astype(F32) + other[:, index].astype(F32)

    own[...] = block(y)
    for k in range(3):
        sends[k][...] = block((y + k + 1) % 4).astype(BF16)


def video_sum_body(pos, held, *refs):
    others, own, sends, scratch = refs[:3], refs[3], refs[4:7], refs[7]
    total = held[...]
    for other in others:
        total = total + other[...].astype(F32)
    for x in range(4):
        scratch[x, :, :, 0:240] = total[:, :, 240 * x : 240 * x + 240]
        scratch[x, :, :, 240:320] = total[:, :, 960 + 80 * x : 960 + 80 * x + 80]
    own[...] = scratch[pos[2]]
    for k in range(3):
        sends[k][...] = scratch[(pos[2] + k + 1) % 4].astype(BF16)


def frame_sum_body(pos, held, first, second, third, out):
    total = held[...]
    for other in (first, second, third):
        total = total + other[...].astype(F32)
    for row in range(4):
        out[row, :, :, 0:60] = total[:, :, 60 * row : 60 * row + 60].astype(BF16)
        out[row, :, :, 60:80] = total[:, :, 240 + 20 * row : 240 + 20 * row + 20].astype(BF16)


def row_sum_body(pos, parts, after, own, send, scratch):
    scratch[...] = jnp.sum(parts[...].astype(F32), axis=0)
    own[...] = scratch[pos[0]]
    send[...] = scratch[1 - pos[0]].astype(BF16)


def last_sum_body(pos, held, other, qkv_out, out_out):
    total = held[...] + other[...].astype(F32)
    qkv_out[...] = total[:, 0:60]
    out_out[...] = total[:, 60:80]


def round_trip(sends, axis):
    return [
        lax.ppermute(sends[k], axis, [(i, (i + k + 1) % 4) for i in range(4)]) for k in range(3)
    ]


def pair_sum(keep, send):
    shape = (2, 4, 80, 1280)
    step = (2, 80, 1280)
    return call(pair_sum_body, [sds(step, F32)] + [sds(step)] * 3, 2, 0, limit=20)(
        keep.reshape(shape), swapped(send).reshape(shape)
    )


def reduce_grads(own, sends, after):
    step = (2, 80, 320)
    own, *sends = call(
        video_sum_body,
        [sds(step, F32)] + [sds(step)] * 3,
        4,
        0,
        (pltpu.VMEM((4,) + step, F32),),
        limit=20,
    )(own, *round_trip(sends, "y"))
    parts = call(frame_sum_body, [sds((4, 2, 80, 80))], 4, 0)(
        own, *round_trip(sends, "x")
    )[0]
    parts = lax.all_to_all(parts, "zh", split_axis=0, concat_axis=0, tiled=True)
    own, send = call(
        row_sum_body, [sds((80, 80), F32), sds((80, 80))], 1, 1, (pltpu.VMEM((2, 80, 80), F32),)
    )(parts, after)
    other = lax.ppermute(send, "zl", [(0, 1), (1, 0)])
    return call(last_sum_body, [sds((80, 60), F32), sds((80, 20), F32)], 2, 0)(own, other)


def edges(images):
    low = lax.ppermute(images[7:8], "zh", [(i, (i + 1) % 4) for i in range(4)])
    high = lax.ppermute(images[0:1], "zh", [(i, (i + 3) % 4) for i in range(4)])
    return low, high


def exchange(rows):
    return lax.all_to_all(rows, FRAME, split_axis=0, concat_axis=0, tiled=True)


def shards(latents, space_kernel, time_kernel, qkv_weight, out_weight, norm_gain, grad_out):
    images, incoming = latents[0, 0], grad_out[0, 0]
    gain = norm_gain.reshape(1, C)
    low, high = edges(images)
    half = half_time(time_kernel)
    others = round_trip([half] * 3, "y")
    other_half = half_projections(qkv_weight, out_weight, others)
    other_others = round_trip([other_half] * 3, "y")
    rows = conv_forward(images, low, high, incoming, space_kernel)
    tile = exchange(rows)
    times = gathered(four(half, others, half), tile)
    weights = gathered(four(other_half, other_others, rows), tile)
    temporal, normal = temporal_step(tile, gain, times)
    grad_packed, keep, send = attention_step(normal, tile, weights)
    own, *sends = pair_sum(keep, send)
    grad_spatial = exchange(
        tile_gradient(grad_packed, temporal, tile, gain, weights, times, sends[0])
    )
    low, high = edges(grad_spatial)
    grad_latents, token = conv_backward(grad_spatial, low, high, space_kernel)
    grad_qkv, grad_outproj = reduce_grads(own, sends, token)
    return grad_latents[None, None], grad_qkv, grad_outproj


def solution(mesh):
    inner = Mesh(mesh.devices.reshape(2, 4, 4, 2, 4), ("zl", "y", "x", "c", "zh"))
    tiles = P(VIDEO, FRAME, "zh", None, None)
    weight = P(VIDEO, None)
    grads = P(VIDEO, ("x", "c", "zh"))
    return jax.shard_map(
        shards,
        mesh=inner,
        in_specs=(tiles, P(), weight, weight, weight, P(), tiles),
        out_specs=(tiles, grads, grads),
        check_vma=False,
    )
```

profile of v0, /device:TPU:6, one launch (start us, length us, event | category | flops | bytes accessed | tf_op | source)
XLA Modules:
  0.0 131.4 jit_solution(10371813450079686879)
XLA Ops:
  0.7 1.7 %shard_map.95.refs_0_.refs_4_ = bf16[128,640]{1,0:T(8,128)(2,1)} custom-call(bf16[240,640]{1,0:T(8,128)(2,1)} %refs_0_.2), custom_call_target="tpu_custom_call" | custom-call | tf_op jit(solution)/shard_map/pallas_call | solution.py:144
  2.3 3.1 %collective-permute-start.4 = (bf16[128,640]{1,0:T(8,128)(2,1)}, bf16[128,640]{1,0:T(8,128)(2,1)S(1)}, u32[]{:S(2)}, u32[]{:S(2)}) collective-permute-start(bf16[128,640]{1,0:T(8,128)(2,1)} %shard_map.95.refs_0_.refs_4_), channel_id=1, source_target_pairs={{0,96},{32,0},{64,32},{96,64},{1,97},{33,1},{65,33},{97,65},{2,98}... | collective-permute-start | bytes 491528 | tf_op jit(solution)/shard_map/ppermute | solution.py:470
  6.1 1.0 collective-permute-start.2
  7.0 0.8 slice_bitcast_fusion
  7.8 6.4 %collective-permute-start.1 = (bf16[1,32,640]{2,1,0:T(8,128)(2,1)S(1)}, bf16[1,32,640]{2,1,0:T(8,128)(2,1)S(1)}, u32[]{:S(2)}, u32[]{:S(2)}) collective-permute-start(bf16[1,32,640]{2,1,0:T(8,128)(2,1)S(1)} %get-tuple-element.46), channel_id=1, source_target_pairs={{0,3},{1,0},{2,1},{3,2},{4,7},{5,4},{6,5},{7,6},{8,11},{9,8},{10,9... | collective-permute-start | bytes 122888 | tf_op jit(solution)/shard_map/ppermute | solution.py:505
  14.3 2.0 %collective-permute-done.2.refs_1_.refs_2_ = bf16[128,640]{1,0:T(8,128)(2,1)S(1)} collective-permute-done((bf16[128,640]{1,0:T(8,128)(2,1)}, bf16[128,640]{1,0:T(8,128)(2,1)S(1)}, u32[]{:S(2)}, u32[]{:S(2)}) %collective-permute-start.2) | collective-permute-done | bytes 163872 | tf_op jit(solution)/shard_map/ppermute | solution.py:470
  17.0 1.6 %shard_map.99.refs_0_ = bf16[160,640]{1,0:T(8,128)(2,1)} custom-call(bf16[80,1920]{1,0:T(8,128)(2,1)} %refs_0_.3, bf16[80,640]{1,0:T(8,128)(2,1)} %refs_1_.1, bf16[128,640]{1,0:T(8,128)(2,1)} %copy-done.13, bf16[128,640]{1,0:T(8,128)(2,1)} %copy-done.11, bf16[128,640]{1,0:T(8,128)(2,1)} %copy-done.9), custom_call_target="tpu_custom_call" | custom-call | tf_op jit(solution)/shard_map/pallas_call | solution.py:171
  18.6 1.0 collective-permute-start.10
  19.6 1.7 %collective-permute-start.9 = (bf16[160,640]{1,0:T(8,128)(2,1)}, bf16[160,640]{1,0:T(8,128)(2,1)S(1)}, u32[]{:S(2)}, u32[]{:S(2)}) collective-permute-start(bf16[160,640]{1,0:T(8,128)(2,1)} %shard_map.99.refs_0_), channel_id=1, source_target_pairs={{0,64},{32,96},{64,0},{96,32},{1,65},{33,97},{65,1},{97,33},{2,66}... | collective-permute-start | bytes 614408 | tf_op jit(solution)/shard_map/ppermute | solution.py:470
  21.3 5.6 %shard_map.94.refs_4_ = bf16[8,2,32,640]{3,2,1,0:T(8,128)(2,1)} custom-call(bf16[8,32,640]{2,1,0:T(8,128)(2,1)S(1)} %bitcast.11, bf16[1,32,640]{2,1,0:T(8,128)(2,1)S(1)} %collective-permute-done.refs_1_, bf16[1,32,640]{2,1,0:T(8,128)(2,1)S(1)} %collective-permute-done.1.refs_2_, bf16[8,32,640]{2,1,0:T(8,128)(2,1)S(1)} %bitcast.12, ...), custom_call_target="tpu_custom_call" | custom-call | flops 1887436800 | bytes 7372800 | tf_op jit(solution)/shard_map/pallas_call | solution.py:110
  27.0 2.4 %collective-permute-done.9.refs_2_ = bf16[160,640]{1,0:T(8,128)(2,1)S(1)} collective-permute-done((bf16[160,640]{1,0:T(8,128)(2,1)}, bf16[160,640]{1,0:T(8,128)(2,1)S(1)}, u32[]{:S(2)}, u32[]{:S(2)}) %collective-permute-start.9) | collective-permute-done | bytes 204832 | tf_op jit(solution)/shard_map/ppermute | solution.py:470
  29.4 2.6 %collective-permute-done.8.refs_1_ = bf16[160,640]{1,0:T(8,128)(2,1)S(1)} collective-permute-done((bf16[160,640]{1,0:T(8,128)(2,1)}, bf16[160,640]{1,0:T(8,128)(2,1)S(1)}, u32[]{:S(2)}, u32[]{:S(2)}) %collective-permute-start.8) | collective-permute-done | bytes 204832 | tf_op jit(solution)/shard_map/ppermute | solution.py:470
  32.0 5.9 %collective-permute-start.11 = (bf16[4,160,640]{2,1,0:T(8,128)(2,1)S(1)}, bf16[4,160,640]{2,1,0:T(8,128)(2,1)}, u32[]{:S(2)}, u32[]{:S(2)}) collective-permute-start(bf16[4,160,640]{2,1,0:T(8,128)(2,1)S(1)} %shard_map.100.refs_2_.refs_4_), channel_id=1, source_target_pairs={{0,131},{4,132},{128,0},{132,5},{1,128},{5,133},{129,1},{133,6},{2... | collective-permute-start | bytes 2457608 | tf_op jit(solution)/shard_map/ppermute | solution.py:201
  37.9 4.8 %all-to-all-start = ((bf16[8,2,32,640]{3,2,1,0:T(8,128)(2,1)}), bf16[8,2,32,640]{3,2,1,0:T(8,128)(2,1)S(1)}, u32[]{:S(2)}, u32[]{:S(2)}) async-start(bf16[8,2,32,640]{3,2,1,0:T(8,128)(2,1)} %shard_map.94.refs_4_), calls=%async_computation | async-start | bytes 1310720 | tf_op jit(solution)/shard_map/all_to_all | solution.py:510
  42.8 1.1 collective-permute-start.5
  43.9 8.5 %all-to-all-done.b.refs_0_.refs_1_.refs_2_ = bf16[8,2,32,640]{3,2,1,0:T(8,128)(2,1)S(1)} async-done(((bf16[8,2,32,640]{3,2,1,0:T(8,128)(2,1)}), bf16[8,2,32,640]{3,2,1,0:T(8,128)(2,1)S(1)}, u32[]{:S(2)}, u32[]{:S(2)}) %all-to-all-start) | async-done | bytes 655392 | tf_op jit(solution)/shard_map/all_to_all | solution.py:510
  52.4 0.8 copy-done
  53.7 1.1 collective-permute-done.5.a
  54.8 0.9 copy-done.2
  56.3 1.7 %collective-permute-done.7.refs_5_.refs_11_ = bf16[4,128,640]{2,1,0:T(8,128)(2,1)S(1)} collective-permute-done((bf16[4,128,640]{2,1,0:T(8,128)(2,1)}, bf16[4,128,640]{2,1,0:T(8,128)(2,1)S(1)}, u32[]{:S(2)}, u32[]{:S(2)}) %collective-permute-start.7) | collective-permute-done | bytes 655392 | tf_op jit(solution)/shard_map/ppermute | solution.py:205
  58.0 1.1 copy-done.3
  59.1 1.6 %shard_map.98 = (bf16[256,640]{1,0:T(8,128)(2,1)S(1)}, bf16[256,640]{1,0:T(8,128)(2,1)S(1)}) custom-call(bf16[8,2,32,640]{3,2,1,0:T(8,128)(2,1)S(1)} %copy-done.1, f32[1,640]{1,0:T(1,128)S(1)} %reshape.17.refs_1_.refs_3_, bf16[4,128,640]{2,1,0:T(8,128)(2,1)S(1)} %shard_map.96.refs_2_.refs_8_, bf16[4,128,640]{2,1,0:T(8,128)(2,1)S(1)} %copy-done.3, ...), custom_call_target="tpu_custom_call" | custom-call | flops 629145600 | bytes 2457600 | tf_op jit(solution)/shard_map/pallas_call | solution.py:269
  60.7 9.6 %shard_map.102 = (bf16[8,2,16,1920]{3,2,1,0:T(8,128)(2,1)S(1)}, bf16[640,1280]{1,0:T(8,128)(2,1)S(1)}, bf16[640,1280]{1,0:T(8,128)(2,1)S(1)}) custom-call(bf16[256,640]{1,0:T(8,128)(2,1)S(1)} %get-tuple-element.22.refs_0_, bf16[8,2,32,640]{3,2,1,0:T(8,128)(2,1)S(1)} %copy-done.1, bf16[4,160,640]{2,1,0:T(8,128)(2,1)S(1)} %shard_map.100.refs_2_.refs_4_, ...), custom_call_target="tpu_custom_call" | custom-call | flops 2097152000 | bytes 3276800 | tf_op jit(solution)/shard_map/pallas_call | solution.py:354
  70.6 3.4 %collective-permute-done.14 = bf16[640,1280]{1,0:T(8,128)(2,1)S(1)} collective-permute-done((bf16[640,1280]{1,0:T(8,128)(2,1)S(1)}, bf16[640,1280]{1,0:T(8,128)(2,1)S(1)}, u32[]{:S(2)}, u32[]{:S(2)}) %collective-permute-start.14) | collective-permute-done | bytes 1638432 | tf_op jit(solution)/shard_map/ppermute | solution.py:205
  74.0 1.3 %shard_map.103 = (f32[2,80,1280]{2,1,0:T(8,128)S(1)}, bf16[2,80,1280]{2,1,0:T(8,128)(2,1)}, bf16[2,80,1280]{2,1,0:T(8,128)(2,1)}, bf16[2,80,1280]{2,1,0:T(8,128)(2,1)}) custom-call(bf16[2,4,80,1280]{3,2,1,0:T(8,128)(2,1)S(1)} %bitcast.9, bf16[2,4,80,1280]{3,2,1,0:T(8,128)(2,1)S(1)} %bitcast.10), custom_call_target="tpu_custom_call" | custom-call | tf_op jit(solution)/shard_map/pallas_call | solution.py:477
  75.3 0.9 copy-done.7
  76.5 1.2 collective-permute-start.19
  77.7 0.9 collective-permute-start.17
  78.5 5.6 %shard_map.104 = bf16[8,32,640]{2,1,0:T(8,128)(2,1)} custom-call(bf16[8,2,16,1920]{3,2,1,0:T(8,128)(2,1)S(1)} %get-tuple-element.23.refs_0_, bf16[256,640]{1,0:T(8,128)(2,1)S(1)} %get-tuple-element.24.refs_1_, bf16[8,2,32,640]{3,2,1,0:T(8,128)(2,1)S(1)} %copy-done.1, f32[1,640]{1,0:T(1,128)S(1)} %reshape.17.refs_1_.refs_3_, ...), custom_call_target="tpu_custom_call" | custom-call | flops 1258291200 | bytes 5734400 | tf_op jit(solution)/shard_map/pallas_call | solution.py:409
  84.2 5.1 %all-to-all-start.1 = ((bf16[8,32,640]{2,1,0:T(8,128)(2,1)}), bf16[8,32,640]{2,1,0:T(8,128)(2,1)S(1)}, u32[]{:S(2)}, u32[]{:S(2)}) async-start(bf16[8,32,640]{2,1,0:T(8,128)(2,1)} %shard_map.104), calls=%async_computation.1 | async-start | bytes 655360 | tf_op jit(solution)/shard_map/all_to_all | solution.py:510
  89.3 1.0 collective-permute-done.18.refs_2_
  90.3 6.5 %collective-permute-done.19.refs_3_ = bf16[2,80,1280]{2,1,0:T(8,128)(2,1)} collective-permute-done((bf16[2,80,1280]{2,1,0:T(8,128)(2,1)}, bf16[2,80,1280]{2,1,0:T(8,128)(2,1)}, u32[]{:S(2)}, u32[]{:S(2)}) %collective-permute-start.19) | collective-permute-done | bytes 409632 | tf_op jit(solution)/shard_map/ppermute | solution.py:470
  96.8 1.6 %collective-permute-done.17.refs_1_ = bf16[2,80,1280]{2,1,0:T(8,128)(2,1)} collective-permute-done((bf16[2,80,1280]{2,1,0:T(8,128)(2,1)}, bf16[2,80,1280]{2,1,0:T(8,128)(2,1)}, u32[]{:S(2)}, u32[]{:S(2)}) %collective-permute-start.17) | collective-permute-done | bytes 409632 | tf_op jit(solution)/shard_map/ppermute | solution.py:470
  98.3 1.1 copy-done.8
  99.5 1.6 %shard_map.106 = (f32[2,80,320]{2,1,0:T(8,128)S(1)}, bf16[2,80,320]{2,1,0:T(8,128)(2,1)S(1)}, bf16[2,80,320]{2,1,0:T(8,128)(2,1)S(1)}, bf16[2,80,320]{2,1,0:T(8,128)(2,1)S(1)}) custom-call(f32[2,80,1280]{2,1,0:T(8,128)S(1)} %copy-done.8, bf16[2,80,1280]{2,1,0:T(8,128)(2,1)} %collective-permute-done.17.refs_1_, ...), custom_call_target="tpu_custom_call" | custom-call | tf_op jit(solution)/shard_map/pallas_call | solution.py:484
  101.1 1.8 %collective-permute-start.20 = (bf16[2,80,320]{2,1,0:T(8,128)(2,1)S(1)}, bf16[2,80,320]{2,1,0:T(8,128)(2,1)S(1)}, u32[]{:S(2)}, u32[]{:S(2)}) collective-permute-start(bf16[2,80,320]{2,1,0:T(8,128)(2,1)S(1)} %get-tuple-element.33), channel_id=1, source_target_pairs={{0,8},{8,16},{16,24},{24,0},{1,9},{9,17},{17,25},{25,1},{2,10},{10... | collective-permute-start | bytes 307208 | tf_op jit(solution)/shard_map/ppermute | solution.py:470
  102.9 1.1 collective-permute-start.21
  104.3 2.7 %collective-permute-start.16 = (bf16[1,32,640]{2,1,0:T(8,128)(2,1)S(1)}, bf16[1,32,640]{2,1,0:T(8,128)(2,1)S(1)}, u32[]{:S(2)}, u32[]{:S(2)}) collective-permute-start(bf16[1,32,640]{2,1,0:T(8,128)(2,1)S(1)} %get-tuple-element.44), channel_id=1, source_target_pairs={{0,3},{1,0},{2,1},{3,2},{4,7},{5,4},{6,5},{7,6},{8,11},{9,8},{10,9... | collective-permute-start | bytes 122888 | tf_op jit(solution)/shard_map/ppermute | solution.py:505
  107.3 3.3 %collective-permute-done.21.refs_2_ = bf16[2,80,320]{2,1,0:T(8,128)(2,1)S(1)} collective-permute-done((bf16[2,80,320]{2,1,0:T(8,128)(2,1)S(1)}, bf16[2,80,320]{2,1,0:T(8,128)(2,1)S(1)}, u32[]{:S(2)}, u32[]{:S(2)}) %collective-permute-start.21) | collective-permute-done | bytes 102432 | tf_op jit(solution)/shard_map/ppermute | solution.py:470
  110.6 1.4 %collective-permute-done.22.refs_3_ = bf16[2,80,320]{2,1,0:T(8,128)(2,1)S(1)} collective-permute-done((bf16[2,80,320]{2,1,0:T(8,128)(2,1)S(1)}, bf16[2,80,320]{2,1,0:T(8,128)(2,1)S(1)}, u32[]{:S(2)}, u32[]{:S(2)}) %collective-permute-start.22) | collective-permute-done | bytes 102432 | tf_op jit(solution)/shard_map/ppermute | solution.py:470
  112.0 0.9 shard_map.107
  112.9 3.8 %all-to-all-start.2 = ((bf16[4,2,80,80]{3,2,1,0:T(8,128)(2,1)}), bf16[4,2,80,80]{3,2,1,0:T(8,128)(2,1)S(1)}, u32[]{:S(2)}, u32[]{:S(2)}) async-start(bf16[4,2,80,80]{3,2,1,0:T(8,128)(2,1)} %shard_map.107), calls=%async_computation.2 | async-start | bytes 327680 | tf_op jit(solution)/shard_map/all_to_all | solution.py:495
  116.7 5.8 %shard_map.105 = (bf16[8,32,640]{2,1,0:T(8,128)(2,1)}, f32[8,128]{1,0:T(8,128)S(1)}) custom-call(bf16[8,32,640]{2,1,0:T(8,128)(2,1)S(1)} %all-to-all-done.1.refs_0_, bf16[1,32,640]{2,1,0:T(8,128)(2,1)S(1)} %collective-permute-done.15.refs_1_, bf16[1,32,640]{2,1,0:T(8,128)(2,1)S(1)} %collective-permute-done.16.refs_2_, bf16[3,3,640,640]{3,2,1,0:T(8,128)(2,1)} %refs_3_.1), custom_call_target="tpu_custom_call" | custom-call | flops 1887436800 | bytes 7372800 | tf_op jit(solution)/shard_map/pallas_call | solution.py:123
  122.5 3.5 %all-to-all-done.2.refs_0_ = bf16[4,2,80,80]{3,2,1,0:T(8,128)(2,1)S(1)} async-done(((bf16[4,2,80,80]{3,2,1,0:T(8,128)(2,1)}), bf16[4,2,80,80]{3,2,1,0:T(8,128)(2,1)S(1)}, u32[]{:S(2)}, u32[]{:S(2)}) %all-to-all-start.2) | async-done | bytes 102432 | tf_op jit(solution)/shard_map/all_to_all | solution.py:495
  126.1 0.8 collective-permute-start.23
  126.9 3.1 %collective-permute-done.23.refs_1_ = bf16[80,80]{1,0:T(8,128)(2,1)S(1)} collective-permute-done((bf16[80,80]{1,0:T(8,128)(2,1)S(1)}, bf16[80,80]{1,0:T(8,128)(2,1)S(1)}, u32[]{:S(2)}, u32[]{:S(2)}) %collective-permute-start.23) | collective-permute-done | bytes 12832 | tf_op jit(solution)/shard_map/ppermute | solution.py:499
  130.0 0.7 copy.12
  130.7 0.7 copy.13
  (63 shorter events, 4.0 us)
Async XLA Ops:
  0.6 20.7 %copy-start.15 = (bf16[1,1,8,32,640]{4,3,2,1,0:T(8,128)(2,1)S(1)}, bf16[1,1,8,32,640]{4,3,2,1,0:T(8,128)(2,1)}, u32[]{:S(2)}) copy-start(bf16[1,1,8,32,640]{4,3,2,1,0:T(8,128)(2,1)} %param.7) | copy-start | bytes 983044
  0.6 20.7 %copy-start.16 = (bf16[1,1,8,32,640]{4,3,2,1,0:T(8,128)(2,1)S(1)}, bf16[1,1,8,32,640]{4,3,2,1,0:T(8,128)(2,1)}, u32[]{:S(2)}) copy-start(bf16[1,1,8,32,640]{4,3,2,1,0:T(8,128)(2,1)} %param.13) | copy-start | bytes 983044
  2.3 11.9 %collective-permute-start.4 = (bf16[128,640]{1,0:T(8,128)(2,1)}, bf16[128,640]{1,0:T(8,128)(2,1)S(1)}, u32[]{:S(2)}, u32[]{:S(2)}) collective-permute-start(bf16[128,640]{1,0:T(8,128)(2,1)} %shard_map.95.refs_0_.refs_4_), channel_id=1, source_target_pairs={{0,96},{32,0},{64,32},{96,64},{1,97},{33,1},{65,33},{97,65},{2,98}... | collective-permute-start | bytes 491528 | tf_op jit(solution)/shard_map/ppermute | solution.py:470
  5.4 8.9 %collective-permute-start.3 = (bf16[128,640]{1,0:T(8,128)(2,1)}, bf16[128,640]{1,0:T(8,128)(2,1)S(1)}, u32[]{:S(2)}, u32[]{:S(2)}) collective-permute-start(bf16[128,640]{1,0:T(8,128)(2,1)} %shard_map.95.refs_0_.refs_4_), channel_id=1, source_target_pairs={{0,64},{32,96},{64,0},{96,32},{1,65},{33,97},{65,1},{97,33},{2,66}... | collective-permute-start | bytes 491528 | tf_op jit(solution)/shard_map/ppermute | solution.py:470
  6.1 10.3 %collective-permute-start.2 = (bf16[128,640]{1,0:T(8,128)(2,1)}, bf16[128,640]{1,0:T(8,128)(2,1)S(1)}, u32[]{:S(2)}, u32[]{:S(2)}) collective-permute-start(bf16[128,640]{1,0:T(8,128)(2,1)} %shard_map.95.refs_0_.refs_4_), channel_id=1, source_target_pairs={{0,32},{32,64},{64,96},{96,0},{1,33},{33,65},{65,97},{97,1},{2,34}... | collective-permute-start | bytes 491528 | tf_op jit(solution)/shard_map/ppermute | solution.py:470
  7.8 13.5 %collective-permute-start.1 = (bf16[1,32,640]{2,1,0:T(8,128)(2,1)S(1)}, bf16[1,32,640]{2,1,0:T(8,128)(2,1)S(1)}, u32[]{:S(2)}, u32[]{:S(2)}) collective-permute-start(bf16[1,32,640]{2,1,0:T(8,128)(2,1)S(1)} %get-tuple-element.46), channel_id=1, source_target_pairs={{0,3},{1,0},{2,1},{3,2},{4,7},{5,4},{6,5},{7,6},{8,11},{9,8},{10,9... | collective-permute-start | bytes 122888 | tf_op jit(solution)/shard_map/ppermute | solution.py:505
  14.2 7.1 %collective-permute-start = (bf16[1,32,640]{2,1,0:T(8,128)(2,1)S(1)}, bf16[1,32,640]{2,1,0:T(8,128)(2,1)S(1)}, u32[]{:S(2)}, u32[]{:S(2)}) collective-permute-start(bf16[1,32,640]{2,1,0:T(8,128)(2,1)S(1)} %get-tuple-element.47), channel_id=1, source_target_pairs={{0,1},{1,2},{2,3},{3,0},{4,5},{5,6},{6,7},{7,4},{8,9},{9,10},{10,1... | collective-permute-start | bytes 122888 | tf_op jit(solution)/shard_map/ppermute | solution.py:504
  14.2 2.1 %copy-start.9 = (bf16[128,640]{1,0:T(8,128)(2,1)}, bf16[128,640]{1,0:T(8,128)(2,1)S(1)}, u32[]{:S(2)}) copy-start(bf16[128,640]{1,0:T(8,128)(2,1)S(1)} %collective-permute-done.4.refs_3_.refs_4_) | copy-start | bytes 491524
  14.3 2.0 %copy-start.11 = (bf16[128,640]{1,0:T(8,128)(2,1)}, bf16[128,640]{1,0:T(8,128)(2,1)S(1)}, u32[]{:S(2)}) copy-start(bf16[128,640]{1,0:T(8,128)(2,1)S(1)} %collective-permute-done.3.refs_2_.refs_3_) | copy-start | bytes 491524
  16.3 0.7 copy-start.13
  18.6 8.3 %collective-permute-start.10 = (bf16[160,640]{1,0:T(8,128)(2,1)}, bf16[160,640]{1,0:T(8,128)(2,1)S(1)}, u32[]{:S(2)}, u32[]{:S(2)}) collective-permute-start(bf16[160,640]{1,0:T(8,128)(2,1)} %shard_map.99.refs_0_), channel_id=1, source_target_pairs={{0,96},{32,0},{64,32},{96,64},{1,97},{33,1},{65,33},{97,65},{2,98}... | collective-permute-start | bytes 614408 | tf_op jit(solution)/shard_map/ppermute | solution.py:470
  19.6 9.8 %collective-permute-start.9 = (bf16[160,640]{1,0:T(8,128)(2,1)}, bf16[160,640]{1,0:T(8,128)(2,1)S(1)}, u32[]{:S(2)}, u32[]{:S(2)}) collective-permute-start(bf16[160,640]{1,0:T(8,128)(2,1)} %shard_map.99.refs_0_), channel_id=1, source_target_pairs={{0,64},{32,96},{64,0},{96,32},{1,65},{33,97},{65,1},{97,33},{2,66}... | collective-permute-start | bytes 614408 | tf_op jit(solution)/shard_map/ppermute | solution.py:470
  21.3 10.6 %collective-permute-start.8 = (bf16[160,640]{1,0:T(8,128)(2,1)}, bf16[160,640]{1,0:T(8,128)(2,1)S(1)}, u32[]{:S(2)}, u32[]{:S(2)}) collective-permute-start(bf16[160,640]{1,0:T(8,128)(2,1)} %shard_map.99.refs_0_), channel_id=1, source_target_pairs={{0,32},{32,64},{64,96},{96,0},{1,33},{33,65},{65,97},{97,1},{2,34}... | collective-permute-start | bytes 614408 | tf_op jit(solution)/shard_map/ppermute | solution.py:470
  21.3 10.6 %copy-start.6 = (bf16[160,640]{1,0:T(8,128)(2,1)S(1)}, bf16[160,640]{1,0:T(8,128)(2,1)}, u32[]{:S(2)}) copy-start(bf16[160,640]{1,0:T(8,128)(2,1)} %shard_map.99.refs_0_) | copy-start | bytes 614404
  26.9 15.8 %copy-start.5 = (bf16[128,640]{1,0:T(8,128)(2,1)S(1)}, bf16[128,640]{1,0:T(8,128)(2,1)}, u32[]{:S(2)}) copy-start(bf16[128,640]{1,0:T(8,128)(2,1)} %shard_map.95.refs_0_.refs_4_) | copy-start | bytes 491524
  26.9 15.8 %copy-start.10 = (bf16[128,640]{1,0:T(8,128)(2,1)S(1)}, bf16[128,640]{1,0:T(8,128)(2,1)}, u32[]{:S(2)}) copy-start(bf16[128,640]{1,0:T(8,128)(2,1)} %copy-done.9) | copy-start | bytes 491524
  26.9 15.8 %copy-start.12 = (bf16[128,640]{1,0:T(8,128)(2,1)S(1)}, bf16[128,640]{1,0:T(8,128)(2,1)}, u32[]{:S(2)}) copy-start(bf16[128,640]{1,0:T(8,128)(2,1)} %copy-done.11) | copy-start | bytes 491524
  27.0 15.8 %copy-start.14 = (bf16[128,640]{1,0:T(8,128)(2,1)S(1)}, bf16[128,640]{1,0:T(8,128)(2,1)}, u32[]{:S(2)}) copy-start(bf16[128,640]{1,0:T(8,128)(2,1)} %copy-done.13) | copy-start | bytes 491524
  32.0 20.4 %collective-permute-start.11 = (bf16[4,160,640]{2,1,0:T(8,128)(2,1)S(1)}, bf16[4,160,640]{2,1,0:T(8,128)(2,1)}, u32[]{:S(2)}, u32[]{:S(2)}) collective-permute-start(bf16[4,160,640]{2,1,0:T(8,128)(2,1)S(1)} %shard_map.100.refs_2_.refs_4_), channel_id=1, source_target_pairs={{0,131},{4,132},{128,0},{132,5},{1,128},{5,133},{129,1},{133,6},{2... | collective-permute-start | bytes 2457608 | tf_op jit(solution)/shard_map/ppermute | solution.py:201
  37.9 14.5 %all-to-all-start = ((bf16[8,2,32,640]{3,2,1,0:T(8,128)(2,1)}), bf16[8,2,32,640]{3,2,1,0:T(8,128)(2,1)S(1)}, u32[]{:S(2)}, u32[]{:S(2)}) async-start(bf16[8,2,32,640]{3,2,1,0:T(8,128)(2,1)} %shard_map.94.refs_4_), calls=%async_computation | async-start | bytes 1310720 | tf_op jit(solution)/shard_map/all_to_all | solution.py:510
  42.8 12.9 %copy-start.17 = (f32[640]{0:T(1024)S(1)}, f32[640]{0:T(1024)}, u32[]{:S(2)}) copy-start(f32[640]{0:T(1024)} %param.12) | copy-start | bytes 7684
  42.8 12.0 %collective-permute-start.5 = (bf16[4,128,640]{2,1,0:T(8,128)(2,1)S(1)}, bf16[4,128,640]{2,1,0:T(8,128)(2,1)S(1)}, u32[]{:S(2)}, u32[]{:S(2)}) collective-permute-start(bf16[4,128,640]{2,1,0:T(8,128)(2,1)S(1)} %shard_map.96.refs_2_.refs_8_), channel_id=1, source_target_pairs={{0,131},{4,132},{128,0},{132,5},{1,128},{5,133},{129,1},{133,6},{2... | collective-permute-start | bytes 1966088 | tf_op jit(solution)/shard_map/ppermute | solution.py:201
  43.9 16.8 %collective-permute-start.12 = (bf16[4,160,640]{2,1,0:T(8,128)(2,1)S(1)}, bf16[4,160,640]{2,1,0:T(8,128)(2,1)}, u32[]{:S(2)}, u32[]{:S(2)}) collective-permute-start(bf16[4,160,640]{2,1,0:T(8,128)(2,1)S(1)} %shard_map.100.refs_2_.refs_4_), channel_id=1, source_target_pairs={{0,4},{4,0},{1,5},{5,1},{2,6},{6,2},{3,7},{7,3},{8,12},{12,8},{9,1... | collective-permute-start | bytes 2457608 | tf_op jit(solution)/shard_map/ppermute | solution.py:205
  52.4 0.8 copy-start
  53.2 4.7 %copy-start.1 = (bf16[8,2,32,640]{3,2,1,0:T(8,128)(2,1)S(1)}, bf16[8,2,32,640]{3,2,1,0:T(8,128)(2,1)}, u32[]{:S(2)}) copy-start(bf16[8,2,32,640]{3,2,1,0:T(8,128)(2,1)} %copy-done) | copy-start | bytes 1966084
  53.2 7.5 %collective-permute-start.13 = (bf16[4,160,640]{2,1,0:T(8,128)(2,1)}, bf16[4,160,640]{2,1,0:T(8,128)(2,1)}, u32[]{:S(2)}, u32[]{:S(2)}) collective-permute-start(bf16[4,160,640]{2,1,0:T(8,128)(2,1)} %shard_map.101.refs_3_.refs_5_), channel_id=1, source_target_pairs={{0,4},{4,0},{1,5},{5,1},{2,6},{6,2},{3,7},{7,3},{8,12},{12,8},{9,1... | collective-permute-start | bytes 2457608 | tf_op jit(solution)/shard_map/ppermute | solution.py:205
  53.2 3.1 %collective-permute-start.6 = (bf16[4,128,640]{2,1,0:T(8,128)(2,1)S(1)}, bf16[4,128,640]{2,1,0:T(8,128)(2,1)S(1)}, u32[]{:S(2)}, u32[]{:S(2)}) collective-permute-start(bf16[4,128,640]{2,1,0:T(8,128)(2,1)S(1)} %shard_map.96.refs_2_.refs_8_), channel_id=1, source_target_pairs={{0,4},{4,0},{1,5},{5,1},{2,6},{6,2},{3,7},{7,3},{8,12},{12,8},{9,1... | collective-permute-start | bytes 1966088 | tf_op jit(solution)/shard_map/ppermute | solution.py:205
  54.8 0.9 copy-start.2
  55.7 2.3 %collective-permute-start.7 = (bf16[4,128,640]{2,1,0:T(8,128)(2,1)}, bf16[4,128,640]{2,1,0:T(8,128)(2,1)S(1)}, u32[]{:S(2)}, u32[]{:S(2)}) collective-permute-start(bf16[4,128,640]{2,1,0:T(8,128)(2,1)} %shard_map.97.refs_3_.refs_9_), channel_id=1, source_target_pairs={{0,4},{4,0},{1,5},{5,1},{2,6},{6,2},{3,7},{7,3},{8,12},{12,8},{9,1... | collective-permute-start | bytes 1966088 | tf_op jit(solution)/shard_map/ppermute | solution.py:205
  58.0 1.1 copy-start.3
  70.4 3.6 %collective-permute-start.14 = (bf16[640,1280]{1,0:T(8,128)(2,1)S(1)}, bf16[640,1280]{1,0:T(8,128)(2,1)S(1)}, u32[]{:S(2)}, u32[]{:S(2)}) collective-permute-start(bf16[640,1280]{1,0:T(8,128)(2,1)S(1)} %get-tuple-element.26), channel_id=1, source_target_pairs={{0,4},{4,0},{1,5},{5,1},{2,6},{6,2},{3,7},{7,3},{8,12},{12,8},{9,1... | collective-permute-start | bytes 4915208 | tf_op jit(solution)/shard_map/ppermute | solution.py:205
  74.0 4.5 %copy-start.4 = (bf16[4,128,640]{2,1,0:T(8,128)(2,1)S(1)}, bf16[4,128,640]{2,1,0:T(8,128)(2,1)}, u32[]{:S(2)}) copy-start(bf16[4,128,640]{2,1,0:T(8,128)(2,1)} %shard_map.97.refs_3_.refs_9_) | copy-start | bytes 1966084
  75.3 0.9 copy-start.7
  76.2 14.1 %collective-permute-start.18 = (bf16[2,80,1280]{2,1,0:T(8,128)(2,1)}, bf16[2,80,1280]{2,1,0:T(8,128)(2,1)S(1)}, u32[]{:S(2)}, u32[]{:S(2)}) collective-permute-start(bf16[2,80,1280]{2,1,0:T(8,128)(2,1)} %get-tuple-element.30), channel_id=1, source_target_pairs={{0,64},{32,96},{64,0},{96,32},{1,65},{33,97},{65,1},{97,33},{2,66}... | collective-permute-start | bytes 1228808 | tf_op jit(solution)/shard_map/ppermute | solution.py:470
  76.5 20.3 %collective-permute-start.19 = (bf16[2,80,1280]{2,1,0:T(8,128)(2,1)}, bf16[2,80,1280]{2,1,0:T(8,128)(2,1)}, u32[]{:S(2)}, u32[]{:S(2)}) collective-permute-start(bf16[2,80,1280]{2,1,0:T(8,128)(2,1)} %get-tuple-element.31), channel_id=1, source_target_pairs={{0,96},{32,0},{64,32},{96,64},{1,97},{33,1},{65,33},{97,65},{2,98}... | collective-permute-start | bytes 1228808 | tf_op jit(solution)/shard_map/ppermute | solution.py:470
  77.7 20.7 %collective-permute-start.17 = (bf16[2,80,1280]{2,1,0:T(8,128)(2,1)}, bf16[2,80,1280]{2,1,0:T(8,128)(2,1)}, u32[]{:S(2)}, u32[]{:S(2)}) collective-permute-start(bf16[2,80,1280]{2,1,0:T(8,128)(2,1)} %get-tuple-element.27.refs_12_), channel_id=1, source_target_pairs={{0,32},{32,64},{64,96},{96,0},{1,33},{33,65},{65,97},{97,1},{2,34}... | collective-permute-start | bytes 1228808 | tf_op jit(solution)/shard_map/ppermute | solution.py:470
  84.2 20.1 %all-to-all-start.1 = ((bf16[8,32,640]{2,1,0:T(8,128)(2,1)}), bf16[8,32,640]{2,1,0:T(8,128)(2,1)S(1)}, u32[]{:S(2)}, u32[]{:S(2)}) async-start(bf16[8,32,640]{2,1,0:T(8,128)(2,1)} %shard_map.104), calls=%async_computation.1 | async-start | bytes 655360 | tf_op jit(solution)/shard_map/all_to_all | solution.py:510
  98.3 1.1 copy-start.8
  101.1 6.3 %collective-permute-start.20 = (bf16[2,80,320]{2,1,0:T(8,128)(2,1)S(1)}, bf16[2,80,320]{2,1,0:T(8,128)(2,1)S(1)}, u32[]{:S(2)}, u32[]{:S(2)}) collective-permute-start(bf16[2,80,320]{2,1,0:T(8,128)(2,1)S(1)} %get-tuple-element.33), channel_id=1, source_target_pairs={{0,8},{8,16},{16,24},{24,0},{1,9},{9,17},{17,25},{25,1},{2,10},{10... | collective-permute-start | bytes 307208 | tf_op jit(solution)/shard_map/ppermute | solution.py:470
  102.9 7.7 %collective-permute-start.21 = (bf16[2,80,320]{2,1,0:T(8,128)(2,1)S(1)}, bf16[2,80,320]{2,1,0:T(8,128)(2,1)S(1)}, u32[]{:S(2)}, u32[]{:S(2)}) collective-permute-start(bf16[2,80,320]{2,1,0:T(8,128)(2,1)S(1)} %get-tuple-element.34), channel_id=1, source_target_pairs={{0,16},{8,24},{16,0},{24,8},{1,17},{9,25},{17,1},{25,9},{2,18},{10... | collective-permute-start | bytes 307208 | tf_op jit(solution)/shard_map/ppermute | solution.py:470
  104.0 8.0 %collective-permute-start.22 = (bf16[2,80,320]{2,1,0:T(8,128)(2,1)S(1)}, bf16[2,80,320]{2,1,0:T(8,128)(2,1)S(1)}, u32[]{:S(2)}, u32[]{:S(2)}) collective-permute-start(bf16[2,80,320]{2,1,0:T(8,128)(2,1)S(1)} %get-tuple-element.35), channel_id=1, source_target_pairs={{0,24},{8,0},{16,8},{24,16},{1,25},{9,1},{17,9},{25,17},{2,26},{10... | collective-permute-start | bytes 307208 | tf_op jit(solution)/shard_map/ppermute | solution.py:470
  104.3 12.4 %collective-permute-start.16 = (bf16[1,32,640]{2,1,0:T(8,128)(2,1)S(1)}, bf16[1,32,640]{2,1,0:T(8,128)(2,1)S(1)}, u32[]{:S(2)}, u32[]{:S(2)}) collective-permute-start(bf16[1,32,640]{2,1,0:T(8,128)(2,1)S(1)} %get-tuple-element.44), channel_id=1, source_target_pairs={{0,3},{1,0},{2,1},{3,2},{4,7},{5,4},{6,5},{7,6},{8,11},{9,8},{10,9... | collective-permute-start | bytes 122888 | tf_op jit(solution)/shard_map/ppermute | solution.py:505
  107.0 9.7 %collective-permute-start.15 = (bf16[1,32,640]{2,1,0:T(8,128)(2,1)S(1)}, bf16[1,32,640]{2,1,0:T(8,128)(2,1)S(1)}, u32[]{:S(2)}, u32[]{:S(2)}) collective-permute-start(bf16[1,32,640]{2,1,0:T(8,128)(2,1)S(1)} %get-tuple-element.45), channel_id=1, source_target_pairs={{0,1},{1,2},{2,3},{3,0},{4,5},{5,6},{6,7},{7,4},{8,9},{9,10},{10,1... | collective-permute-start | bytes 122888 | tf_op jit(solution)/shard_map/ppermute | solution.py:504
  112.9 13.1 %all-to-all-start.2 = ((bf16[4,2,80,80]{3,2,1,0:T(8,128)(2,1)}), bf16[4,2,80,80]{3,2,1,0:T(8,128)(2,1)S(1)}, u32[]{:S(2)}, u32[]{:S(2)}) async-start(bf16[4,2,80,80]{3,2,1,0:T(8,128)(2,1)} %shard_map.107), calls=%async_computation.2 | async-start | bytes 327680 | tf_op jit(solution)/shard_map/all_to_all | solution.py:495
  126.1 3.9 %collective-permute-start.23 = (bf16[80,80]{1,0:T(8,128)(2,1)S(1)}, bf16[80,80]{1,0:T(8,128)(2,1)S(1)}, u32[]{:S(2)}, u32[]{:S(2)}) collective-permute-start(bf16[80,80]{1,0:T(8,128)(2,1)S(1)} %get-tuple-element.38), channel_id=1, source_target_pairs={{0,128},{128,0},{1,129},{129,1},{2,130},{130,2},{3,131},{131,3},{4... | collective-permute-start | bytes 38408 | tf_op jit(solution)/shard_map/ppermute | solution.py:499
where the time goes:
time: 132 us; the launch traced here: 131 us
  starting transfers between devices  44.6 us (34%)
  waiting for transfers between devices  42.5 us (32%)
  Pallas kernels  35.7 us (27%)
  local copies, waits for them, and re-layouts  7.75 us (6%)
    ppermute x12, waiting for transfers between devices, round_trip(): lax.ppermute(sends[k], axis, [(i, (i + k + 1) % 4) for i in range(4)])  20.7 us
    ppermute x12, starting transfers between devices, round_trip(): lax.ppermute(sends[k], axis, [(i, (i + k + 1) % 4) for i in range(4)])  12.9 us
    all_to_all x2, starting transfers between devices, exchange(): return lax.all_to_all(rows, FRAME, split_axis=0, concat_axis=0, tiled=True)  9.91 us
    pallas_call x1, Pallas kernels, attention_step(): call(attention_body, [sds((8, 2, 16, 3 * C)), sds((C, 1280)), sds((C, 128...  9.64 us
    ppermute x2, starting transfers between devices, edges(): high = lax.ppermute(images[0:1], 'zh', [(i, (i + 3) % 4) for i in range(4)])  9.09 us
    all_to_all x2, waiting for transfers between devices, exchange(): return lax.all_to_all(rows, FRAME, split_axis=0, concat_axis=0, tiled=True)  8.49 us
    ppermute x2, starting transfers between devices, across(): return lax.ppermute(own, ('zl', 'c', 'zh'), pairs)  7.02 us
    unnamed x38, local copies, waits for them, and re-layouts  6.93 us
  transfers between devices with their start and end apart: 27, of which 16 were waited for; matrix products, arithmetic and copies ran while one was open for 1% of the time, Pallas kernels for 17%

commit v1 on v0

--- a/solution.py
+++ b/solution.py
@@ -15,6 +15,7 @@
 VIDEO = ("zl", "y")
 FRAME = ("x", "c")
 MIB = 1 << 20
+BLOCKS = (4, 4, 80, C)
 
 
 def sds(shape, dtype=BF16):
@@ -132,25 +133,15 @@
     )(images, low, high, kernel)
 
 
-def half_body(pos, time, half, sem):
-    rows = time.at[pl.ds(pl.multiple_of(112 * pos[3], 16), 128)]
-    copy = pltpu.make_async_copy(rows, half, sem)
-    copy.start()
-    copy.wait()
-
-
-def half_time(time):
-    dma = (pltpu.SemaphoreType.DMA,)
-    return call(half_body, [sds((128, C))], 0, 1, dma, limit=62)(time)[0]
-
-
-def half_projections_body(pos, qkv, out, *refs):
-    core, (half, sems) = pos[3], refs[3:]
+def halves_body(pos, time, qkv, out, half, sems):
+    core = pos[3]
+    rows = time.at[pl.ds(pl.multiple_of(112 * core, 16), 128)]
 
     def run(first, second):
         copies = [
-            pltpu.make_async_copy(first, half.at[0:80], sems.at[0]),
-            pltpu.make_async_copy(second, half.at[80:160], sems.at[1]),
+            pltpu.make_async_copy(rows, half.at[0:128], sems.at[0]),
+            pltpu.make_async_copy(first, half.at[128:208], sems.at[1]),
+            pltpu.make_async_copy(second, half.at[208:288], sems.at[2]),
         ]
         for copy in copies:
             copy.start()
@@ -166,9 +157,9 @@
         run(qkv.at[:, 2 * C : 3 * C], out)
 
 
-def half_projections(qkv, out, after):
-    dma = (pltpu.SemaphoreType.DMA((2,)),)
-    return call(half_projections_body, [sds((160, C))], 0, 5, dma, limit=62)(qkv, out, *after)[0]
+def halves_of(time, qkv, out):
+    dma = (pltpu.SemaphoreType.DMA((3,)),)
+    return call(halves_body, [sds((288, C))], 0, 3, dma, limit=62)(time, qkv, out)[0]
 
 
 def gate(value, after):
@@ -182,14 +173,16 @@
 
 
 def four_body(pos, own, *refs):
-    others, out = refs[:3], refs[-1]
-    out[pos[1]] = own[...]
+    others, four, three = refs[:3], refs[-2], refs[-1]
+    four[pos[1]] = own[...]
     for k in range(3):
-        out[(pos[1] + 3 - k) % 4] = others[k][...]
-
-
-def four(own, others, after):
-    return call(four_body, [sds((4,) + own.shape)], 4, 1)(own, *others, after)[0]
+        four[(pos[1] + 3 - k) % 4] = others[k][...]
+        three[k] = others[k][...]
+
+
+def four_of(own, others, *after):
+    outs = [sds((4,) + own.shape), sds((3,) + own.shape)]
+    return call(four_body, outs, 4, len(after))(own, *others, *after)
 
 
 def across(own):
@@ -205,43 +198,48 @@
     return lax.ppermute(value, "c", [(0, 1), (1, 0)])
 
 
+def placed_pieces(pos, pieces):
+    zl, y, core = pos[0], pos[1], pos[3]
+    own, own_swapped, near, near_swapped, three, three_swapped = pieces
+    placed = [(own, pl.ds(4 * zl, 4), core), (own_swapped, pl.ds(4 * zl, 4), 1 - core)]
+    for half, one, others in ((core, near, three), (1 - core, near_swapped, three_swapped)):
+        placed.append((one, 4 * (1 - zl) + y, half))
+        for k in range(3):
+            placed.append((others.at[k], 4 * (1 - zl) + (y + 3 - k) % 4, half))
+    return placed
+
+
 def time_copies(pos, pieces, target, sem):
-    zl, core = pos[0], pos[3]
     copies = []
-    for i, piece in enumerate(pieces):
-        blocks = pl.ds(4 * (zl if i % 2 == 0 else 1 - zl), 4)
-        half = core if i < 2 else 1 - core
-        source = piece.at[:, pl.ds(pl.multiple_of(16 * half, 16), 112)]
-        place = target.at[blocks, pl.ds(pl.multiple_of(128 * half, 16), 112)]
-        copies.append(pltpu.make_async_copy(source, place, sem.at[i]))
-        if i < 2:
-            source = piece.at[:, pl.ds(pl.multiple_of(112 * (1 - half), 16), 16)]
-            place = target.at[blocks, pl.ds(112, 16)]
-            copies.append(pltpu.make_async_copy(source, place, sem.at[4 + i]))
+    for i, (piece, blocks, half) in enumerate(placed_pieces(pos, pieces)):
+        lead = (slice(None),) if i < 2 else ()
+
+        def part(first, last, n, i=i, piece=piece, blocks=blocks, lead=lead):
+            source = piece.at[lead + (pl.ds(pl.multiple_of(first, 16), n),)]
+            place = target.at[blocks, pl.ds(pl.multiple_of(last, 16), n)]
+            copies.append(pltpu.make_async_copy(source, place, sem.at[len(copies)]))
+
+        part(16 * half, 128 * half, 112)
+        if i == 0 or 2 <= i < 6:
+            part(112 * (1 - half), 112, 16)
     return copies
 
 
 def projection_copies(pos, pieces, target, sem):
-    zl, core = pos[0], pos[3]
     copies = []
-    for i, piece in enumerate(pieces):
-        blocks = pl.ds(4 * (zl if i % 2 == 0 else 1 - zl), 4)
-        half = core if i < 2 else 1 - core
+    for i, (piece, blocks, half) in enumerate(placed_pieces(pos, pieces)):
+        lead = (slice(None),) if i < 2 else ()
         for j in range(2):
             lanes = pl.ds(pl.multiple_of(1280 * half + 640 * j, 128), 640)
-            source = piece.at[:, 80 * j : 80 * j + 80]
-            copies.append(pltpu.make_async_copy(source, target.at[blocks, :, lanes], sem.at[2 * i + j]))
+            source = piece.at[lead + (pl.ds(128 + 80 * j, 80),)]
+            place = target.at[blocks, :, lanes]
+            copies.append(pltpu.make_async_copy(source, place, sem.at[2 * i + j]))
     return copies
 
 
-def gathered(own, after):
-    far = gate(across(own), after)
-    return [own, far, swapped(own), swapped(far)]
-
-
 def temporal_body(pos, tile, gain, *refs):
-    time_pieces, (temporal_out, normal_out) = refs[:4], refs[4:6]
-    time_ref, padded, sem = refs[6:]
+    time_pieces, (temporal_out, normal_out) = refs[:6], refs[6:8]
+    time_ref, padded, sem = refs[8:]
     copies = time_copies(pos, time_pieces, time_ref, sem)
     for copy in copies:
         copy.start()
@@ -270,8 +268,8 @@
         temporal_body,
         [sds((256, C)), sds((256, C))],
         2,
-        4,
-        TIME_SCRATCH + (pltpu.SemaphoreType.DMA((6,)),),
+        6,
+        TIME_SCRATCH + (pltpu.SemaphoreType.DMA((15,)),),
         limit=20,
         flops=2 * 256 * 3 * C * C,
         moved=3 * C * C * 2,
@@ -279,8 +277,8 @@
 
 
 def attention_body(pos, normal, tile, *refs):
-    weight_pieces, (grad_packed, keep, send) = refs[:4], refs[4:7]
-    weight_ref, packed, grad_blend, blended, sem = refs[7:]
+    weight_pieces, (grad_packed, mixed_out, send) = refs[:6], refs[6:9]
+    weight_ref, packed, grad_blend, blended, sem = refs[9:]
     copies = projection_copies(pos, weight_pieces, weight_ref, sem)
     for copy in copies:
         copy.start()
@@ -288,8 +286,7 @@
         copy.wait()
     weight = weight_ref[...].reshape(C, 4 * C)
     packed[...] = mm(normal[...], weight[:, : 3 * C]).astype(BF16).reshape(8, 2, 16, 3 * C)
-    arriving = tile[:, 1].reshape(256, C)
-    grad_blend[...] = mm_nt(arriving, weight[:, 3 * C :]).astype(BF16).reshape(8, 2, 16, C)
+    grad_blend[...] = mm_nt(tile[:, 1].reshape(256, C), weight[:, 3 * C :]).astype(BF16).reshape(8, 2, 16, C)
     first_head = lax.broadcasted_iota(jnp.int32, (128, 128), 1) < HEAD_DIM
     row_pixel = lax.broadcasted_iota(jnp.int32, (256, 128), 0) % 16
     column_pixel = lax.broadcasted_iota(jnp.int32, (256, 128), 1) % 16
@@ -332,49 +329,99 @@
                 lanes = slice(i * C + at, i * C + at + 128)
                 grad_packed[:, half, :, lanes] = result.reshape(8, 16, 128)
 
-    core = pos[3]
-    whole = grad_packed[...].reshape(256, 3 * C)
-
-    def columns(array, width, which):
-        starts = [(2 * x + which) * width for x in range(4)]
-        return jnp.concatenate([array[:, s : s + width] for s in starts], axis=1)
-
-    mixed = blended[...].reshape(256, C)
-    qkv_parts = [columns(whole, 240, which) for which in range(2)]
-    out_parts = [columns(arriving, 80, which) for which in range(2)]
-    for target, swap in ((send, 0), (keep, 1)):
-        first = core == swap
-        qkv_side = jnp.where(first, qkv_parts[1], qkv_parts[0])
-        out_side = jnp.where(first, out_parts[1], out_parts[0])
-        target[:, 0:960] = mm_tn(normal[...], qkv_side).astype(BF16)
-        target[:, 960:1280] = mm_tn(mixed, out_side).astype(BF16)
+    mixed_out[...] = blended[...].reshape(256, C)
+    weight_gradient(1 - pos[3], normal, mixed_out, tile, grad_packed, send)
+
+
+def gradient_pair(first, second):
+    def gap(n):
+        return jnp.zeros((256, n), BF16)
+
+    def placed(left, *parts):
+        return mm_tn(left, jnp.concatenate(parts, axis=1))
+
+    a = placed(first[0], first[2], gap(16))
+    b = placed(first[1], gap(112), first[3], gap(64))
+    c = placed(second[0], gap(64), second[2], gap(80))
+    d = placed(second[1], gap(48), second[3])
+    groups = (
+        a[:, :128],
+        a[:, 128:] + b[:, :128],
+        b[:, 128:] + c[:, :128],
+        c[:, 128:256],
+        c[:, 256:] + d,
+    )
+    return jnp.concatenate(groups, axis=1).astype(BF16)
+
+
+def weight_gradient(core, normal, mixed, tile, grad_packed, target):
+    for which in range(2):
+
+        @pl.when(core == which)
+        def _(which=which):
+            packed = grad_packed[...].reshape(256, 3 * C)
+            arriving = tile[:, 1].reshape(256, C)
+            left, right = normal[...], mixed[...]
+
+            def sides(x):
+                at = 2 * x + which
+                return packed[:, 240 * at : 240 * at + 240], arriving[:, 80 * at : 80 * at + 80]
+
+            if which == 0:
+                for half in range(2):
+                    a, b = [(left, right) + sides(2 * half + i) for i in range(2)]
+                    both = gradient_pair(a, b).reshape(2, 4, 80, C)
+                    for zl in range(2):
+                        target[:, 2 * zl + half] = both[zl]
+            else:
+                lefts = left[:, :320], left[:, 320:]
+                rights = right[:, :320], right[:, 320:]
+                for x in range(4):
+                    a, b = [(lefts[zl], rights[zl]) + sides(x) for zl in range(2)]
+                    target[x] = gradient_pair(a, b).reshape(4, 80, C)
+
+
+def own_gradient_body(pos, normal, mixed, tile, grad_packed, keep):
+    weight_gradient(pos[3], normal, mixed, tile, grad_packed, keep)
+
+
+def own_gradient(normal, mixed, tile, grad_packed):
+    return call(
+        own_gradient_body,
+        [sds(BLOCKS)],
+        4,
+        0,
+        limit=24,
+        flops=2 * 256 * 2 * C * C,
+        moved=2 * C * C * 2,
+    )(normal, mixed, tile, grad_packed)[0]
 
 
 def attention_step(normal, tile, weight_pieces):
     return call(
         attention_body,
-        [sds((8, 2, 16, 3 * C)), sds((C, 1280)), sds((C, 1280))],
+        [sds((8, 2, 16, 3 * C)), sds((256, C)), sds(BLOCKS)],
         2,
-        4,
+        6,
         (
             pltpu.VMEM((8, 80, 4 * C), BF16),
             pltpu.VMEM((8, 2, 16, 3 * C), BF16),
             pltpu.VMEM((8, 2, 16, C), BF16),
             pltpu.VMEM((8, 2, 16, C), BF16),
-            pltpu.SemaphoreType.DMA((8,)),
+            pltpu.SemaphoreType.DMA((20,)),
         ),
         limit=36,
-        flops=2 * 256 * 10 * C * C,
+        flops=2 * 256 * 8 * C * C,
         moved=4 * C * C * 2,
     )(normal, tile, *weight_pieces)
 
 
 def tile_gradient_body(pos, *refs):
     grad_packed, temporal, tile, gain = refs[:4]
-    weight_pieces, time_pieces, out = refs[4:8], refs[8:12], refs[13]
-    weight_ref, time_ref, padded, sem, time_sem = refs[14:]
-    copies = projection_copies(pos, weight_pieces, weight_ref, sem)
-    later_copies = time_copies(pos, time_pieces, time_ref, time_sem)
+    pieces, out = refs[4:10], refs[11]
+    weight_ref, time_ref, padded, sem, time_sem = refs[12:]
+    copies = projection_copies(pos, pieces, weight_ref, sem)
+    later_copies = time_copies(pos, pieces, time_ref, time_sem)
     for copy in copies + later_copies:
         copy.start()
     for copy in copies:
@@ -405,46 +452,54 @@
     out[...] = grad_spatial.astype(BF16).reshape(8, 32, C)
 
 
-def tile_gradient(grad_packed, temporal, tile, gain, weights, times, after):
+def tile_gradient(grad_packed, temporal, tile, gain, weights, after):
     return call(
         tile_gradient_body,
         [sds((8, 32, C))],
         4,
-        9,
+        7,
         (pltpu.VMEM((8, 80, 4 * C), BF16),)
         + TIME_SCRATCH
-        + (pltpu.SemaphoreType.DMA((8,)), pltpu.SemaphoreType.DMA((6,))),
+        + (pltpu.SemaphoreType.DMA((20,)), pltpu.SemaphoreType.DMA((15,))),
         limit=28,
         flops=2 * 256 * 6 * C * C,
         moved=7 * C * C * 2,
-    )(grad_packed, temporal, tile, gain, *weights, *times, after)[0]
+    )(grad_packed, temporal, tile, gain, *weights, after)[0]
 
 
 def pair_sum_body(pos, keep, other, own, *sends):
-    y = pos[1]
+    me = jnp.where(pos[3] == 0, pos[1], pos[2])
 
     def block(index):
-        return keep[:, index].astype(F32) + other[:, index].astype(F32)
-
-    own[...] = block(y)
+        return keep[index].astype(F32) + other[index].astype(F32)
+
+    own[...] = block(me)
     for k in range(3):
-        sends[k][...] = block((y + k + 1) % 4).astype(BF16)
-
-
-def video_sum_body(pos, held, *refs):
-    others, own, sends, scratch = refs[:3], refs[3], refs[4:7], refs[7]
+        sends[k][...] = block((me + k + 1) % 4).astype(BF16)
+
+
+def second_sum_body(pos, held, *refs):
+    others, own, sends, scratch = refs[0:3], refs[3], refs[4:7], refs[7]
     total = held[...]
     for other in others:
         total = total + other[...].astype(F32)
-    for x in range(4):
-        scratch[x, :, :, 0:240] = total[:, :, 240 * x : 240 * x + 240]
-        scratch[x, :, :, 240:320] = total[:, :, 960 + 80 * x : 960 + 80 * x + 80]
-    own[...] = scratch[pos[2]]
+
+    for which in range(2):
+
+        @pl.when(pos[3] == which)
+        def _(which=which):
+            for i in range(4):
+                for zl in range(2):
+                    block, at = (2 * zl + i // 2, i % 2) if which == 0 else (i, zl)
+                    scratch[i, zl] = total[block, :, 320 * at : 320 * at + 320]
+
+    me = jnp.where(pos[3] == 0, pos[2], pos[1])
+    own[...] = scratch[me]
     for k in range(3):
-        sends[k][...] = scratch[(pos[2] + k + 1) % 4].astype(BF16)
-
-
-def frame_sum_body(pos, held, first, second, third, out):
+        sends[k][...] = scratch[(me + k + 1) % 4].astype(BF16)
+
+
+def third_sum_body(pos, held, first, second, third, out):
     total = held[...]
     for other in (first, second, third):
         total = total + other[...].astype(F32)
@@ -460,9 +515,9 @@
 
 
 def last_sum_body(pos, held, other, qkv_out, out_out):
-    total = held[...] + other[...].astype(F32)
-    qkv_out[...] = total[:, 0:60]
-    out_out[...] = total[:, 60:80]
+    total = (held[...] + other[...].astype(F32)).T
+    qkv_out[...] = total[0:60]
+    out_out[...] = total[60:80]
 
 
 def round_trip(sends, axis):
@@ -471,33 +526,50 @@
     ]
 
 
+def crosswise(sends, first):
+    def target(y, x, core, k):
+        if (core == 0) == first:
+            return (y + k + 1) % 4, x
+        return y, (x + k + 1) % 4
+
+    moved = []
+    for k in range(3):
+        pairs = []
+        for y in range(4):
+            for x in range(4):
+                for core in range(2):
+                    ty, tx = target(y, x, core, k)
+                    pairs.append(((y * 4 + x) * 2 + core, (ty * 4 + tx) * 2 + core))
+        moved.append(lax.ppermute(sends[k], ("y", "x", "c"), pairs))
+    return moved
+
+
 def pair_sum(keep, send):
-    shape = (2, 4, 80, 1280)
-    step = (2, 80, 1280)
+    step = BLOCKS[1:]
     return call(pair_sum_body, [sds(step, F32)] + [sds(step)] * 3, 2, 0, limit=20)(
-        keep.reshape(shape), swapped(send).reshape(shape)
+        keep, swapped(send)
     )
 
 
-def reduce_grads(own, sends, after):
+def reduce_grads(summed, after):
+    own, *sends = summed
     step = (2, 80, 320)
     own, *sends = call(
-        video_sum_body,
+        second_sum_body,
         [sds(step, F32)] + [sds(step)] * 3,
         4,
         0,
         (pltpu.VMEM((4,) + step, F32),),
         limit=20,
-    )(own, *round_trip(sends, "y"))
-    parts = call(frame_sum_body, [sds((4, 2, 80, 80))], 4, 0)(
-        own, *round_trip(sends, "x")
-    )[0]
+    )(own, *crosswise(sends, True))
+    parts = call(third_sum_body, [sds((4, 2, 80, 80))], 4, 0)(own, *crosswise(sends, False))[0]
     parts = lax.all_to_all(parts, "zh", split_axis=0, concat_axis=0, tiled=True)
     own, send = call(
         row_sum_body, [sds((80, 80), F32), sds((80, 80))], 1, 1, (pltpu.VMEM((2, 80, 80), F32),)
     )(parts, after)
     other = lax.ppermute(send, "zl", [(0, 1), (1, 0)])
-    return call(last_sum_body, [sds((80, 60), F32), sds((80, 20), F32)], 2, 0)(own, other)
+    grads = call(last_sum_body, [sds((60, 80), F32), sds((20, 80), F32)], 2, 0)(own, other)
+    return [grad.T for grad in grads]
 
 
 def edges(images):
@@ -514,23 +586,24 @@
     images, incoming = latents[0, 0], grad_out[0, 0]
     gain = norm_gain.reshape(1, C)
     low, high = edges(images)
-    half = half_time(time_kernel)
+    half = halves_of(time_kernel, qkv_weight, out_weight)
     others = round_trip([half] * 3, "y")
-    other_half = half_projections(qkv_weight, out_weight, others)
-    other_others = round_trip([other_half] * 3, "y")
+    near = across(half)
     rows = conv_forward(images, low, high, incoming, space_kernel)
     tile = exchange(rows)
-    times = gathered(four(half, others, half), tile)
-    weights = gathered(four(other_half, other_others, rows), tile)
-    temporal, normal = temporal_step(tile, gain, times)
-    grad_packed, keep, send = attention_step(normal, tile, weights)
-    own, *sends = pair_sum(keep, send)
+    own, three = four_of(half, others, rows, near)
+    far = gate(across(three), tile)
+    weights = [own, swapped(own), near, swapped(near), far, swapped(far)]
+    temporal, normal = temporal_step(tile, gain, weights)
+    grad_packed, mixed, send = attention_step(normal, tile, weights)
+    keep = own_gradient(normal, mixed, tile, grad_packed)
+    summed = pair_sum(keep, send)
     grad_spatial = exchange(
-        tile_gradient(grad_packed, temporal, tile, gain, weights, times, sends[0])
+        tile_gradient(grad_packed, temporal, tile, gain, weights, summed[0])
     )
     low, high = edges(grad_spatial)
     grad_latents, token = conv_backward(grad_spatial, low, high, space_kernel)
-    grad_qkv, grad_outproj = reduce_grads(own, sends, token)
+    grad_qkv, grad_outproj = reduce_grads(summed, token)
     return grad_latents[None, None], grad_qkv, grad_outproj
 
 

time: 132 us -> 118 us (0.89)
  waiting for transfers between devices: 42.5 us -> 32.7 us
  starting transfers between devices: 44.6 us -> 39.9 us
  local copies, waits for them, and re-layouts: 7.75 us -> 5.99 us
    ppermute x12 -> x3, waiting for transfers between devices: 20.7 us -> 0.01 us  [round_trip(): lax.ppermute(sends[k], axis, [(i, (i + k + 1) % 4) for i in range(4)])]
    ppermute x12 -> x3, starting transfers between devices: 12.9 us -> 4.61 us  [round_trip(): lax.ppermute(sends[k], axis, [(i, (i + k + 1) % 4) for i in range(4)])]
    ppermute x0 -> x6, starting transfers between devices: none -> 7.22 us  [crosswise(): moved.append(lax.ppermute(sends[k], ('y', 'x', 'c'), pairs))]
    ppermute x2, waiting for transfers between devices: 0.01 us -> 6.11 us  [edges(): low = lax.ppermute(images[7:8], 'zh', [(i, (i + 1) % 4) for i in range(4)])]
    ppermute x2, starting transfers between devices: 9.09 us -> 3.5 us  [edges(): high = lax.ppermute(images[0:1], 'zh', [(i, (i + 3) % 4) for i in range(4)])]
    all_to_all x2, waiting for transfers between devices: 8.49 us -> 12.1 us  [exchange(): return lax.all_to_all(rows, FRAME, split_axis=0, concat_axis=0, tiled=True)]
    ppermute x2, waiting for transfers between devices: 0.01 us -> 3.45 us  [edges(): high = lax.ppermute(images[0:1], 'zh', [(i, (i + 3) % 4) for i in range(4)])]
    pallas_call x10 -> x9, Pallas kernels: 22.9 us -> 24.9 us  [the longest x1 9.1 us: attention_step(): call(attention_body, [sds((8, 2, 16, 3 * C)), sds((256, C)), sds(BLOCKS)]...]
  transfers between devices with their start and end apart: 27 -> 23, of which waited for: 16 -> 9; matrix products, arithmetic and copies ran while one was open for 1% -> 1% of each run, Pallas kernels for 17% -> 17%
where the time goes in v1:
time: 118 us; the launch traced here: 116 us
  starting transfers between devices  39.9 us (34%)
  Pallas kernels  36.7 us (31%)
  waiting for transfers between devices  32.7 us (28%)
  local copies, waits for them, and re-layouts  5.99 us (5%)
    all_to_all x2, waiting for transfers between devices, exchange(): return lax.all_to_all(rows, FRAME, split_axis=0, concat_axis=0, tiled=True)  12.1 us
    all_to_all x2, starting transfers between devices, exchange(): return lax.all_to_all(rows, FRAME, split_axis=0, concat_axis=0, tiled=True)  10.2 us
    pallas_call x1, Pallas kernels, attention_step(): call(attention_body, [sds((8, 2, 16, 3 * C)), sds((256, C)), sds(BLOCKS)]...  9.1 us
    ppermute x2, starting transfers between devices, across(): return lax.ppermute(own, ('zl', 'c', 'zh'), pairs)  7.27 us
    ppermute x6, starting transfers between devices, crosswise(): moved.append(lax.ppermute(sends[k], ('y', 'x', 'c'), pairs))  7.22 us
    pallas_call x1, Pallas kernels, tile_gradient(): call(tile_gradient_body, [sds((8, 32, C))], 4, 7, (pltpu.VMEM((8, 80, 4 *...  6.19 us
    ppermute x2, waiting for transfers between devices, edges(): low = lax.ppermute(images[7:8], 'zh', [(i, (i + 1) % 4) for i in range(4)])  6.11 us
    pallas_call x1, Pallas kernels, conv_backward(): call(conv_backward_body, [sds((8, 32, C)), sds((8, 128), F32)], 3, 1, CON...  5.83 us
  transfers between devices with their start and end apart: 23, of which 9 were waited for; matrix products, arithmetic and copies ran while one was open for 1% of the time, Pallas kernels for 17%

profile of v1, /device:TPU:6, one launch (start us, length us, event | category | flops | bytes accessed | tf_op | source)
XLA Modules:
  0.0 116.1 jit_solution(11019611361390764404)
XLA Ops:
  0.7 1.9 %shard_map.95.refs_0_ = bf16[288,640]{1,0:T(8,128)(2,1)} custom-call(bf16[240,640]{1,0:T(8,128)(2,1)} %refs_0_.1, bf16[80,1920]{1,0:T(8,128)(2,1)} %refs_1_.1, bf16[80,640]{1,0:T(8,128)(2,1)} %refs_2_.1), custom_call_target="tpu_custom_call" | custom-call | tf_op jit(solution)/shard_map/pallas_call | solution.py:162
  2.5 5.9 %collective-permute-start.5 = (bf16[288,640]{1,0:T(8,128)(2,1)}, bf16[288,640]{1,0:T(8,128)(2,1)S(1)}, u32[]{:S(2)}, u32[]{:S(2)}) collective-permute-start(bf16[288,640]{1,0:T(8,128)(2,1)} %shard_map.95.refs_0_), channel_id=1, source_target_pairs={{0,131},{4,132},{128,0},{132,5},{1,128},{5,133},{129,1},{133,6},{2... | collective-permute-start | bytes 1105928 | tf_op jit(solution)/shard_map/ppermute | solution.py:194
  8.4 3.0 %collective-permute-start.4 = (bf16[288,640]{1,0:T(8,128)(2,1)}, bf16[288,640]{1,0:T(8,128)(2,1)S(1)}, u32[]{:S(2)}, u32[]{:S(2)}) collective-permute-start(bf16[288,640]{1,0:T(8,128)(2,1)} %shard_map.95.refs_0_), channel_id=1, source_target_pairs={{0,96},{32,0},{64,32},{96,64},{1,97},{33,1},{65,33},{97,65},{2,98}... | collective-permute-start | bytes 1105928 | tf_op jit(solution)/shard_map/ppermute | solution.py:525
  11.5 0.6 collective-permute-start.3
  12.1 1.0 collective-permute-start.2
  13.1 0.8 slice_bitcast_fusion
  13.9 1.5 %collective-permute-start.1 = (bf16[1,32,640]{2,1,0:T(8,128)(2,1)S(1)}, bf16[1,32,640]{2,1,0:T(8,128)(2,1)S(1)}, u32[]{:S(2)}, u32[]{:S(2)}) collective-permute-start(bf16[1,32,640]{2,1,0:T(8,128)(2,1)S(1)} %get-tuple-element.47), channel_id=1, source_target_pairs={{0,3},{1,0},{2,1},{3,2},{4,7},{5,4},{6,5},{7,6},{8,11},{9,8},{10,9... | collective-permute-start | bytes 122888 | tf_op jit(solution)/shard_map/ppermute | solution.py:577
  15.4 3.4 %collective-permute-done.1.refs_2_ = bf16[1,32,640]{2,1,0:T(8,128)(2,1)S(1)} collective-permute-done((bf16[1,32,640]{2,1,0:T(8,128)(2,1)S(1)}, bf16[1,32,640]{2,1,0:T(8,128)(2,1)S(1)}, u32[]{:S(2)}, u32[]{:S(2)}) %collective-permute-start.1) | collective-permute-done | bytes 40992 | tf_op jit(solution)/shard_map/ppermute | solution.py:577
  18.8 6.1 %collective-permute-done.refs_1_ = bf16[1,32,640]{2,1,0:T(8,128)(2,1)S(1)} collective-permute-done((bf16[1,32,640]{2,1,0:T(8,128)(2,1)S(1)}, bf16[1,32,640]{2,1,0:T(8,128)(2,1)S(1)}, u32[]{:S(2)}, u32[]{:S(2)}) %collective-permute-start) | collective-permute-done | bytes 40992 | tf_op jit(solution)/shard_map/ppermute | solution.py:576
  25.0 4.8 %shard_map.94.refs_4_ = bf16[8,2,32,640]{3,2,1,0:T(8,128)(2,1)S(1)} custom-call(bf16[8,32,640]{2,1,0:T(8,128)(2,1)S(1)} %bitcast.9, bf16[1,32,640]{2,1,0:T(8,128)(2,1)S(1)} %collective-permute-done.refs_1_, bf16[1,32,640]{2,1,0:T(8,128)(2,1)S(1)} %collective-permute-done.1.refs_2_, bf16[8,32,640]{2,1,0:T(8,128)(2,1)S(1)} %bitcast.10, ...), custom_call_target="tpu_custom_call" | custom-call | flops 1887436800 | bytes 7372800 | tf_op jit(solution)/shard_map/pallas_call | solution.py:111
  29.8 1.3 %shard_map.96 = (bf16[4,288,640]{2,1,0:T(8,128)(2,1)S(1)}, bf16[3,288,640]{2,1,0:T(8,128)(2,1)}) custom-call(bf16[288,640]{1,0:T(8,128)(2,1)S(1)} %copy-done.10, bf16[288,640]{1,0:T(8,128)(2,1)S(1)} %collective-permute-done.2.refs_1_, bf16[288,640]{1,0:T(8,128)(2,1)S(1)} %collective-permute-done.3.refs_2_, ...), custom_call_target="tpu_custom_call" | custom-call | tf_op jit(solution)/shard_map/pallas_call | solution.py:185
  31.1 1.3 %collective-permute-start.8 = (bf16[3,288,640]{2,1,0:T(8,128)(2,1)}, bf16[3,288,640]{2,1,0:T(8,128)(2,1)S(1)}, u32[]{:S(2)}, u32[]{:S(2)}) collective-permute-start(bf16[3,288,640]{2,1,0:T(8,128)(2,1)} %get-tuple-element.25), channel_id=1, source_target_pairs={{0,131},{4,132},{128,0},{132,5},{1,128},{5,133},{129,1},{133,6},{2... | collective-permute-start | bytes 3317768 | tf_op jit(solution)/shard_map/ppermute | solution.py:194
  32.4 4.8 %all-to-all-start = ((bf16[8,2,32,640]{3,2,1,0:T(8,128)(2,1)}), bf16[8,2,32,640]{3,2,1,0:T(8,128)(2,1)S(1)}, u32[]{:S(2)}, u32[]{:S(2)}) async-start(bf16[8,2,32,640]{3,2,1,0:T(8,128)(2,1)} %copy-done.6), calls=%async_computation | async-start | bytes 1310720 | tf_op jit(solution)/shard_map/all_to_all | solution.py:582
  37.2 0.1 collective-permute-start.6
  37.4 9.5 %all-to-all-done.b.refs_0_.refs_1_.refs_2_ = bf16[8,2,32,640]{3,2,1,0:T(8,128)(2,1)S(1)} async-done(((bf16[8,2,32,640]{3,2,1,0:T(8,128)(2,1)}), bf16[8,2,32,640]{3,2,1,0:T(8,128)(2,1)S(1)}, u32[]{:S(2)}, u32[]{:S(2)}) %all-to-all-start) | async-done | bytes 655392 | tf_op jit(solution)/shard_map/all_to_all | solution.py:582
  46.9 0.8 copy-done
  47.7 1.0 copy-done.3
  48.7 0.5 collective-permute-start.7
  49.2 3.0 %collective-permute-done.7.refs_5_.refs_7_ = bf16[288,640]{1,0:T(8,128)(2,1)S(1)} collective-permute-done((bf16[288,640]{1,0:T(8,128)(2,1)}, bf16[288,640]{1,0:T(8,128)(2,1)S(1)}, u32[]{:S(2)}, u32[]{:S(2)}) %collective-permute-start.7) | collective-permute-done | bytes 368672 | tf_op jit(solution)/shard_map/ppermute | solution.py:198
  52.2 1.1 copy-done.1
  53.3 1.2 %copy-done.4 = bf16[3,288,640]{2,1,0:T(8,128)(2,1)S(1)} copy-done((bf16[3,288,640]{2,1,0:T(8,128)(2,1)S(1)}, bf16[3,288,640]{2,1,0:T(8,128)(2,1)}, u32[]{:S(2)}) %copy-start.4) | copy-done | bytes 1105944
  54.5 1.0 copy-done.8
  55.5 3.2 %shard_map.98 = (bf16[256,640]{1,0:T(8,128)(2,1)S(1)}, bf16[256,640]{1,0:T(8,128)(2,1)S(1)}) custom-call(bf16[8,2,32,640]{3,2,1,0:T(8,128)(2,1)S(1)} %copy-done.1, f32[1,640]{1,0:T(1,128)S(1)} %reshape.11.refs_1_.refs_3_, bf16[4,288,640]{2,1,0:T(8,128)(2,1)S(1)} %get-tuple-element.24.refs_2_.refs_4_, ...), custom_call_target="tpu_custom_call" | custom-call | flops 629145600 | bytes 2457600 | tf_op jit(solution)/shard_map/pallas_call | solution.py:267
  58.7 9.1 %shard_map.99 = (bf16[8,2,16,1920]{3,2,1,0:T(8,128)(2,1)S(1)}, bf16[256,640]{1,0:T(8,128)(2,1)S(1)}, bf16[4,4,80,640]{3,2,1,0:T(8,128)(2,1)S(1)}) custom-call(bf16[256,640]{1,0:T(8,128)(2,1)S(1)} %get-tuple-element.26.refs_0_, bf16[8,2,32,640]{3,2,1,0:T(8,128)(2,1)S(1)} %copy-done.2, bf16[4,288,640]{2,1,0:T(8,128)(2,1)S(1)} %get-tuple-element.24.refs_2_.refs_4_, ...), custom_call_target="tpu_custom_call" | custom-call | flops 1677721600 | bytes 3276800 | tf_op jit(solution)/shard_map/pallas_call | solution.py:401
  67.8 0.1 collective-permute-start.10
  67.9 1.1 shard_map.100.refs_0_
  69.1 2.4 %collective-permute-done.10.refs_1_ = bf16[4,4,80,640]{3,2,1,0:T(8,128)(2,1)S(1)} collective-permute-done((bf16[4,4,80,640]{3,2,1,0:T(8,128)(2,1)S(1)}, bf16[4,4,80,640]{3,2,1,0:T(8,128)(2,1)S(1)}, u32[]{:S(2)}, u32[]{:S(2)}) %collective-permute-start.10) | collective-permute-done | bytes 1638432 | tf_op jit(solution)/shard_map/ppermute | solution.py:198
  71.4 1.1 shard_map.101
  72.6 1.6 %collective-permute-start.13 = (bf16[4,80,640]{2,1,0:T(8,128)(2,1)}, bf16[4,80,640]{2,1,0:T(8,128)(2,1)S(1)}, u32[]{:S(2)}, u32[]{:S(2)}) collective-permute-start(bf16[4,80,640]{2,1,0:T(8,128)(2,1)} %get-tuple-element.33), channel_id=1, source_target_pairs={{0,32},{4,12},{8,40},{12,20},{16,48},{20,28},{24,56},{28,4},{32,64... | collective-permute-start | bytes 1228808 | tf_op jit(solution)/shard_map/ppermute | solution.py:543
  74.1 1.8 %collective-permute-start.14 = (bf16[4,80,640]{2,1,0:T(8,128)(2,1)}, bf16[4,80,640]{2,1,0:T(8,128)(2,1)S(1)}, u32[]{:S(2)}, u32[]{:S(2)}) collective-permute-start(bf16[4,80,640]{2,1,0:T(8,128)(2,1)} %get-tuple-element.34), channel_id=1, source_target_pairs={{0,64},{4,20},{8,72},{12,28},{16,80},{20,4},{24,88},{28,12},{32,96... | collective-permute-start | bytes 1228808 | tf_op jit(solution)/shard_map/ppermute | solution.py:543
  76.0 0.8 collective-permute-start.15
  76.8 6.2 %shard_map.102 = bf16[8,32,640]{2,1,0:T(8,128)(2,1)} custom-call(bf16[8,2,16,1920]{3,2,1,0:T(8,128)(2,1)S(1)} %get-tuple-element.27.refs_3_.refs_0_, bf16[256,640]{1,0:T(8,128)(2,1)S(1)} %get-tuple-element.28.refs_1_, bf16[8,2,32,640]{3,2,1,0:T(8,128)(2,1)S(1)} %copy-done.2, f32[1,640]{1,0:T(1,128)S(1)} %reshape.11.refs_1_.refs_3_, ...), custom_call_target="tpu_custom_call" | custom-call | flops 1258291200 | bytes 5734400 | tf_op jit(solution)/shard_map/pallas_call | solution.py:456
  83.0 5.4 %all-to-all-start.1 = ((bf16[8,32,640]{2,1,0:T(8,128)(2,1)}), bf16[8,32,640]{2,1,0:T(8,128)(2,1)S(1)}, u32[]{:S(2)}, u32[]{:S(2)}) async-start(bf16[8,32,640]{2,1,0:T(8,128)(2,1)} %shard_map.102), calls=%async_computation.1 | async-start | bytes 655360 | tf_op jit(solution)/shard_map/all_to_all | solution.py:582
  88.5 0.6 shard_map.104
  89.0 0.9 collective-permute-start.16
  90.0 2.1 %collective-permute-start.17 = (bf16[2,80,320]{2,1,0:T(8,128)(2,1)S(1)}, bf16[2,80,320]{2,1,0:T(8,128)(2,1)S(1)}, u32[]{:S(2)}, u32[]{:S(2)}) collective-permute-start(bf16[2,80,320]{2,1,0:T(8,128)(2,1)S(1)} %get-tuple-element.38), channel_id=1, source_target_pairs={{0,16},{4,68},{8,24},{12,76},{16,0},{20,84},{24,8},{28,92},{32,48}... | collective-permute-start | bytes 307208 | tf_op jit(solution)/shard_map/ppermute | solution.py:543
  92.0 2.6 %all-to-all-done.1.refs_0_ = bf16[8,32,640]{2,1,0:T(8,128)(2,1)S(1)} async-done(((bf16[8,32,640]{2,1,0:T(8,128)(2,1)}), bf16[8,32,640]{2,1,0:T(8,128)(2,1)S(1)}, u32[]{:S(2)}, u32[]{:S(2)}) %all-to-all-start.1) | async-done | bytes 327712 | tf_op jit(solution)/shard_map/all_to_all | solution.py:582
  94.6 2.0 %collective-permute-start.12 = (bf16[1,32,640]{2,1,0:T(8,128)(2,1)S(1)}, bf16[1,32,640]{2,1,0:T(8,128)(2,1)S(1)}, u32[]{:S(2)}, u32[]{:S(2)}) collective-permute-start(bf16[1,32,640]{2,1,0:T(8,128)(2,1)S(1)} %get-tuple-element.45), channel_id=1, source_target_pairs={{0,3},{1,0},{2,1},{3,2},{4,7},{5,4},{6,5},{7,6},{8,11},{9,8},{10,9... | collective-permute-start | bytes 122888 | tf_op jit(solution)/shard_map/ppermute | solution.py:577
  96.6 1.0 collective-permute-start.11
  97.6 0.5 collective-permute-done.18.refs_3_
  98.1 0.9 shard_map.105
  99.0 3.9 %all-to-all-start.2 = ((bf16[4,2,80,80]{3,2,1,0:T(8,128)(2,1)}), bf16[4,2,80,80]{3,2,1,0:T(8,128)(2,1)S(1)}, u32[]{:S(2)}, u32[]{:S(2)}) async-start(bf16[4,2,80,80]{3,2,1,0:T(8,128)(2,1)} %shard_map.105), calls=%async_computation.2 | async-start | bytes 327680 | tf_op jit(solution)/shard_map/all_to_all | solution.py:566
  102.9 5.8 %shard_map.103 = (bf16[8,32,640]{2,1,0:T(8,128)(2,1)}, f32[8,128]{1,0:T(8,128)S(1)}) custom-call(bf16[8,32,640]{2,1,0:T(8,128)(2,1)S(1)} %all-to-all-done.1.refs_0_, bf16[1,32,640]{2,1,0:T(8,128)(2,1)S(1)} %collective-permute-done.11.refs_1_, bf16[1,32,640]{2,1,0:T(8,128)(2,1)S(1)} %collective-permute-done.12.refs_2_, bf16[3,3,640,640]{3,2,1,0:T(8,128)(2,1)} %refs_3_.1), custom_call_target="tpu_custom_call" | custom-call | flops 1887436800 | bytes 7372800 | tf_op jit(solution)/shard_map/pallas_call | solution.py:124
  108.8 2.7 %all-to-all-done.2.refs_0_ = bf16[4,2,80,80]{3,2,1,0:T(8,128)(2,1)S(1)} async-done(((bf16[4,2,80,80]{3,2,1,0:T(8,128)(2,1)}), bf16[4,2,80,80]{3,2,1,0:T(8,128)(2,1)S(1)}, u32[]{:S(2)}, u32[]{:S(2)}) %all-to-all-start.2) | async-done | bytes 102432 | tf_op jit(solution)/shard_map/all_to_all | solution.py:566
  111.5 0.1 shard_map.106
  111.5 1.4 %collective-permute-start.19 = (bf16[80,80]{1,0:T(8,128)(2,1)S(1)}, bf16[80,80]{1,0:T(8,128)(2,1)S(1)}, u32[]{:S(2)}, u32[]{:S(2)}) collective-permute-start(bf16[80,80]{1,0:T(8,128)(2,1)S(1)} %get-tuple-element.42), channel_id=1, source_target_pairs={{0,128},{128,0},{1,129},{129,1},{2,130},{130,2},{3,131},{131,3},{4... | collective-permute-start | bytes 38408 | tf_op jit(solution)/shard_map/ppermute | solution.py:570
  112.9 2.5 %collective-permute-done.19.refs_1_ = bf16[80,80]{1,0:T(8,128)(2,1)S(1)} collective-permute-done((bf16[80,80]{1,0:T(8,128)(2,1)S(1)}, bf16[80,80]{1,0:T(8,128)(2,1)S(1)}, u32[]{:S(2)}, u32[]{:S(2)}) %collective-permute-start.19) | collective-permute-done | bytes 12832 | tf_op jit(solution)/shard_map/ppermute | solution.py:570
  115.4 0.7 shard_map.107
  (43 shorter events, 0.1 us)
Async XLA Ops:
  0.6 24.3 %copy-start.11 = (bf16[1,1,8,32,640]{4,3,2,1,0:T(8,128)(2,1)S(1)}, bf16[1,1,8,32,640]{4,3,2,1,0:T(8,128)(2,1)}, u32[]{:S(2)}) copy-start(bf16[1,1,8,32,640]{4,3,2,1,0:T(8,128)(2,1)} %param.7) | copy-start | bytes 983044
  0.6 24.3 %copy-start.12 = (bf16[1,1,8,32,640]{4,3,2,1,0:T(8,128)(2,1)S(1)}, bf16[1,1,8,32,640]{4,3,2,1,0:T(8,128)(2,1)}, u32[]{:S(2)}) copy-start(bf16[1,1,8,32,640]{4,3,2,1,0:T(8,128)(2,1)} %param.13) | copy-start | bytes 983044
  2.5 27.2 %collective-permute-start.5 = (bf16[288,640]{1,0:T(8,128)(2,1)}, bf16[288,640]{1,0:T(8,128)(2,1)S(1)}, u32[]{:S(2)}, u32[]{:S(2)}) collective-permute-start(bf16[288,640]{1,0:T(8,128)(2,1)} %shard_map.95.refs_0_), channel_id=1, source_target_pairs={{0,131},{4,132},{128,0},{132,5},{1,128},{5,133},{129,1},{133,6},{2... | collective-permute-start | bytes 1105928 | tf_op jit(solution)/shard_map/ppermute | solution.py:194
  8.4 21.3 %collective-permute-start.4 = (bf16[288,640]{1,0:T(8,128)(2,1)}, bf16[288,640]{1,0:T(8,128)(2,1)S(1)}, u32[]{:S(2)}, u32[]{:S(2)}) collective-permute-start(bf16[288,640]{1,0:T(8,128)(2,1)} %shard_map.95.refs_0_), channel_id=1, source_target_pairs={{0,96},{32,0},{64,32},{96,64},{1,97},{33,1},{65,33},{97,65},{2,98}... | collective-permute-start | bytes 1105928 | tf_op jit(solution)/shard_map/ppermute | solution.py:525
  11.5 18.3 %collective-permute-start.3 = (bf16[288,640]{1,0:T(8,128)(2,1)}, bf16[288,640]{1,0:T(8,128)(2,1)S(1)}, u32[]{:S(2)}, u32[]{:S(2)}) collective-permute-start(bf16[288,640]{1,0:T(8,128)(2,1)} %shard_map.95.refs_0_), channel_id=1, source_target_pairs={{0,64},{32,96},{64,0},{96,32},{1,65},{33,97},{65,1},{97,33},{2,66}... | collective-permute-start | bytes 1105928 | tf_op jit(solution)/shard_map/ppermute | solution.py:525
  12.1 17.7 %collective-permute-start.2 = (bf16[288,640]{1,0:T(8,128)(2,1)}, bf16[288,640]{1,0:T(8,128)(2,1)S(1)}, u32[]{:S(2)}, u32[]{:S(2)}) collective-permute-start(bf16[288,640]{1,0:T(8,128)(2,1)} %shard_map.95.refs_0_), channel_id=1, source_target_pairs={{0,32},{32,64},{64,96},{96,0},{1,33},{33,65},{65,97},{97,1},{2,34}... | collective-permute-start | bytes 1105928 | tf_op jit(solution)/shard_map/ppermute | solution.py:525
  13.9 5.0 %collective-permute-start.1 = (bf16[1,32,640]{2,1,0:T(8,128)(2,1)S(1)}, bf16[1,32,640]{2,1,0:T(8,128)(2,1)S(1)}, u32[]{:S(2)}, u32[]{:S(2)}) collective-permute-start(bf16[1,32,640]{2,1,0:T(8,128)(2,1)S(1)} %get-tuple-element.47), channel_id=1, source_target_pairs={{0,3},{1,0},{2,1},{3,2},{4,7},{5,4},{6,5},{7,6},{8,11},{9,8},{10,9... | collective-permute-start | bytes 122888 | tf_op jit(solution)/shard_map/ppermute | solution.py:577
  18.8 6.1 %collective-permute-start = (bf16[1,32,640]{2,1,0:T(8,128)(2,1)S(1)}, bf16[1,32,640]{2,1,0:T(8,128)(2,1)S(1)}, u32[]{:S(2)}, u32[]{:S(2)}) collective-permute-start(bf16[1,32,640]{2,1,0:T(8,128)(2,1)S(1)} %get-tuple-element.48), channel_id=1, source_target_pairs={{0,1},{1,2},{2,3},{3,0},{4,5},{5,6},{6,7},{7,4},{8,9},{9,10},{10,1... | collective-permute-start | bytes 122888 | tf_op jit(solution)/shard_map/ppermute | solution.py:576
  25.0 4.8 %copy-start.10 = (bf16[288,640]{1,0:T(8,128)(2,1)S(1)}, bf16[288,640]{1,0:T(8,128)(2,1)}, u32[]{:S(2)}) copy-start(bf16[288,640]{1,0:T(8,128)(2,1)} %shard_map.95.refs_0_) | copy-start | bytes 1105924
  29.7 1.4 %copy-start.6 = (bf16[8,2,32,640]{3,2,1,0:T(8,128)(2,1)}, bf16[8,2,32,640]{3,2,1,0:T(8,128)(2,1)S(1)}, u32[]{:S(2)}) copy-start(bf16[8,2,32,640]{3,2,1,0:T(8,128)(2,1)S(1)} %shard_map.94.refs_4_) | copy-start | bytes 1966084
  29.8 1.3 %copy-start.7 = (bf16[288,640]{1,0:T(8,128)(2,1)}, bf16[288,640]{1,0:T(8,128)(2,1)S(1)}, u32[]{:S(2)}) copy-start(bf16[288,640]{1,0:T(8,128)(2,1)S(1)} %collective-permute-done.5.refs_5_.refs_4_.refs_6_) | copy-start | bytes 1105924
  31.1 15.8 %collective-permute-start.8 = (bf16[3,288,640]{2,1,0:T(8,128)(2,1)}, bf16[3,288,640]{2,1,0:T(8,128)(2,1)S(1)}, u32[]{:S(2)}, u32[]{:S(2)}) collective-permute-start(bf16[3,288,640]{2,1,0:T(8,128)(2,1)} %get-tuple-element.25), channel_id=1, source_target_pairs={{0,131},{4,132},{128,0},{132,5},{1,128},{5,133},{129,1},{133,6},{2... | collective-permute-start | bytes 3317768 | tf_op jit(solution)/shard_map/ppermute | solution.py:194
  32.4 14.5 %all-to-all-start = ((bf16[8,2,32,640]{3,2,1,0:T(8,128)(2,1)}), bf16[8,2,32,640]{3,2,1,0:T(8,128)(2,1)S(1)}, u32[]{:S(2)}, u32[]{:S(2)}) async-start(bf16[8,2,32,640]{3,2,1,0:T(8,128)(2,1)} %copy-done.6), calls=%async_computation | async-start | bytes 1310720 | tf_op jit(solution)/shard_map/all_to_all | solution.py:582
  37.2 12.0 %copy-start.13 = (f32[640]{0:T(1024)S(1)}, f32[640]{0:T(1024)}, u32[]{:S(2)}) copy-start(f32[640]{0:T(1024)} %param.12) | copy-start | bytes 7684
  37.2 15.0 %collective-permute-start.6 = (bf16[4,288,640]{2,1,0:T(8,128)(2,1)S(1)}, bf16[4,288,640]{2,1,0:T(8,128)(2,1)}, u32[]{:S(2)}, u32[]{:S(2)}) collective-permute-start(bf16[4,288,640]{2,1,0:T(8,128)(2,1)S(1)} %get-tuple-element.24.refs_2_.refs_4_), channel_id=1, source_target_pairs={{0,4},{4,0},{1,5},{5,1},{2,6},{6,2},{3,7},{7,3},{8,12},{12,8},{9,1... | collective-permute-start | bytes 4423688 | tf_op jit(solution)/shard_map/ppermute | solution.py:198
  46.9 0.8 copy-start
  47.7 1.0 copy-start.3
  48.7 3.5 %collective-permute-start.9 = (bf16[3,288,640]{2,1,0:T(8,128)(2,1)}, bf16[3,288,640]{2,1,0:T(8,128)(2,1)S(1)}, u32[]{:S(2)}, u32[]{:S(2)}) collective-permute-start(bf16[3,288,640]{2,1,0:T(8,128)(2,1)} %shard_map.97.refs_6_.refs_8_), channel_id=1, source_target_pairs={{0,4},{4,0},{1,5},{5,1},{2,6},{6,2},{3,7},{7,3},{8,12},{12,8},{9,1... | collective-permute-start | bytes 3317768 | tf_op jit(solution)/shard_map/ppermute | solution.py:198
  48.7 3.5 %collective-permute-start.7 = (bf16[288,640]{1,0:T(8,128)(2,1)}, bf16[288,640]{1,0:T(8,128)(2,1)S(1)}, u32[]{:S(2)}, u32[]{:S(2)}) collective-permute-start(bf16[288,640]{1,0:T(8,128)(2,1)} %copy-done.7), channel_id=1, source_target_pairs={{0,4},{4,0},{1,5},{5,1},{2,6},{6,2},{3,7},{7,3},{8,12},{12,8},{9,1... | collective-permute-start | bytes 1105928 | tf_op jit(solution)/shard_map/ppermute | solution.py:198
  52.2 1.1 copy-start.1
  53.3 1.2 %copy-start.4 = (bf16[3,288,640]{2,1,0:T(8,128)(2,1)S(1)}, bf16[3,288,640]{2,1,0:T(8,128)(2,1)}, u32[]{:S(2)}) copy-start(bf16[3,288,640]{2,1,0:T(8,128)(2,1)} %shard_map.97.refs_6_.refs_8_) | copy-start | bytes 3317764
  54.5 1.0 copy-start.8
  55.5 3.2 %copy-start.2 = (bf16[8,2,32,640]{3,2,1,0:T(8,128)(2,1)S(1)}, bf16[8,2,32,640]{3,2,1,0:T(8,128)(2,1)}, u32[]{:S(2)}) copy-start(bf16[8,2,32,640]{3,2,1,0:T(8,128)(2,1)} %copy-done) | copy-start | bytes 1966084
  55.5 3.2 %copy-start.5 = (bf16[3,288,640]{2,1,0:T(8,128)(2,1)S(1)}, bf16[3,288,640]{2,1,0:T(8,128)(2,1)}, u32[]{:S(2)}) copy-start(bf16[3,288,640]{2,1,0:T(8,128)(2,1)} %shard_map.97.refs_6_.refs_8_) | copy-start | bytes 3317764
  55.5 3.2 %copy-start.9 = (bf16[288,640]{1,0:T(8,128)(2,1)S(1)}, bf16[288,640]{1,0:T(8,128)(2,1)}, u32[]{:S(2)}) copy-start(bf16[288,640]{1,0:T(8,128)(2,1)} %copy-done.7) | copy-start | bytes 1105924
  67.8 3.6 %collective-permute-start.10 = (bf16[4,4,80,640]{3,2,1,0:T(8,128)(2,1)S(1)}, bf16[4,4,80,640]{3,2,1,0:T(8,128)(2,1)S(1)}, u32[]{:S(2)}, u32[]{:S(2)}) collective-permute-start(bf16[4,4,80,640]{3,2,1,0:T(8,128)(2,1)S(1)} %get-tuple-element.30), channel_id=1, source_target_pairs={{0,4},{4,0},{1,5},{5,1},{2,6},{6,2},{3,7},{7,3},{8,12},{12,8},{9,1... | collective-permute-start | bytes 4915208 | tf_op jit(solution)/shard_map/ppermute | solution.py:198
  72.6 15.9 %collective-permute-start.13 = (bf16[4,80,640]{2,1,0:T(8,128)(2,1)}, bf16[4,80,640]{2,1,0:T(8,128)(2,1)S(1)}, u32[]{:S(2)}, u32[]{:S(2)}) collective-permute-start(bf16[4,80,640]{2,1,0:T(8,128)(2,1)} %get-tuple-element.33), channel_id=1, source_target_pairs={{0,32},{4,12},{8,40},{12,20},{16,48},{20,28},{24,56},{28,4},{32,64... | collective-permute-start | bytes 1228808 | tf_op jit(solution)/shard_map/ppermute | solution.py:543
  74.1 14.3 %collective-permute-start.14 = (bf16[4,80,640]{2,1,0:T(8,128)(2,1)}, bf16[4,80,640]{2,1,0:T(8,128)(2,1)S(1)}, u32[]{:S(2)}, u32[]{:S(2)}) collective-permute-start(bf16[4,80,640]{2,1,0:T(8,128)(2,1)} %get-tuple-element.34), channel_id=1, source_target_pairs={{0,64},{4,20},{8,72},{12,28},{16,80},{20,4},{24,88},{28,12},{32,96... | collective-permute-start | bytes 1228808 | tf_op jit(solution)/shard_map/ppermute | solution.py:543
  76.0 12.5 %collective-permute-start.15 = (bf16[4,80,640]{2,1,0:T(8,128)(2,1)}, bf16[4,80,640]{2,1,0:T(8,128)(2,1)S(1)}, u32[]{:S(2)}, u32[]{:S(2)}) collective-permute-start(bf16[4,80,640]{2,1,0:T(8,128)(2,1)} %get-tuple-element.35), channel_id=1, source_target_pairs={{0,96},{4,28},{8,104},{12,4},{16,112},{20,12},{24,120},{28,20},{32... | collective-permute-start | bytes 1228808 | tf_op jit(solution)/shard_map/ppermute | solution.py:543
  83.0 11.6 %all-to-all-start.1 = ((bf16[8,32,640]{2,1,0:T(8,128)(2,1)}), bf16[8,32,640]{2,1,0:T(8,128)(2,1)S(1)}, u32[]{:S(2)}, u32[]{:S(2)}) async-start(bf16[8,32,640]{2,1,0:T(8,128)(2,1)} %shard_map.102), calls=%async_computation.1 | async-start | bytes 655360 | tf_op jit(solution)/shard_map/all_to_all | solution.py:582
  89.0 8.6 %collective-permute-start.16 = (bf16[2,80,320]{2,1,0:T(8,128)(2,1)S(1)}, bf16[2,80,320]{2,1,0:T(8,128)(2,1)S(1)}, u32[]{:S(2)}, u32[]{:S(2)}) collective-permute-start(bf16[2,80,320]{2,1,0:T(8,128)(2,1)S(1)} %get-tuple-element.37), channel_id=1, source_target_pairs={{0,8},{4,36},{8,16},{12,44},{16,24},{20,52},{24,0},{28,60},{32,40}... | collective-permute-start | bytes 307208 | tf_op jit(solution)/shard_map/ppermute | solution.py:543
  90.0 7.7 %collective-permute-start.17 = (bf16[2,80,320]{2,1,0:T(8,128)(2,1)S(1)}, bf16[2,80,320]{2,1,0:T(8,128)(2,1)S(1)}, u32[]{:S(2)}, u32[]{:S(2)}) collective-permute-start(bf16[2,80,320]{2,1,0:T(8,128)(2,1)S(1)} %get-tuple-element.38), channel_id=1, source_target_pairs={{0,16},{4,68},{8,24},{12,76},{16,0},{20,84},{24,8},{28,92},{32,48}... | collective-permute-start | bytes 307208 | tf_op jit(solution)/shard_map/ppermute | solution.py:543
  92.0 6.1 %collective-permute-start.18 = (bf16[2,80,320]{2,1,0:T(8,128)(2,1)S(1)}, bf16[2,80,320]{2,1,0:T(8,128)(2,1)S(1)}, u32[]{:S(2)}, u32[]{:S(2)}) collective-permute-start(bf16[2,80,320]{2,1,0:T(8,128)(2,1)S(1)} %get-tuple-element.39), channel_id=1, source_target_pairs={{0,24},{4,100},{8,0},{12,108},{16,8},{20,116},{24,16},{28,124},{32... | collective-permute-start | bytes 307208 | tf_op jit(solution)/shard_map/ppermute | solution.py:543
  94.6 8.3 %collective-permute-start.12 = (bf16[1,32,640]{2,1,0:T(8,128)(2,1)S(1)}, bf16[1,32,640]{2,1,0:T(8,128)(2,1)S(1)}, u32[]{:S(2)}, u32[]{:S(2)}) collective-permute-start(bf16[1,32,640]{2,1,0:T(8,128)(2,1)S(1)} %get-tuple-element.45), channel_id=1, source_target_pairs={{0,3},{1,0},{2,1},{3,2},{4,7},{5,4},{6,5},{7,6},{8,11},{9,8},{10,9... | collective-permute-start | bytes 122888 | tf_op jit(solution)/shard_map/ppermute | solution.py:577
  96.6 6.3 %collective-permute-start.11 = (bf16[1,32,640]{2,1,0:T(8,128)(2,1)S(1)}, bf16[1,32,640]{2,1,0:T(8,128)(2,1)S(1)}, u32[]{:S(2)}, u32[]{:S(2)}) collective-permute-start(bf16[1,32,640]{2,1,0:T(8,128)(2,1)S(1)} %get-tuple-element.46), channel_id=1, source_target_pairs={{0,1},{1,2},{2,3},{3,0},{4,5},{5,6},{6,7},{7,4},{8,9},{9,10},{10,1... | collective-permute-start | bytes 122888 | tf_op jit(solution)/shard_map/ppermute | solution.py:576
  99.0 12.4 %all-to-all-start.2 = ((bf16[4,2,80,80]{3,2,1,0:T(8,128)(2,1)}), bf16[4,2,80,80]{3,2,1,0:T(8,128)(2,1)S(1)}, u32[]{:S(2)}, u32[]{:S(2)}) async-start(bf16[4,2,80,80]{3,2,1,0:T(8,128)(2,1)} %shard_map.105), calls=%async_computation.2 | async-start | bytes 327680 | tf_op jit(solution)/shard_map/all_to_all | solution.py:566
  111.5 3.9 %collective-permute-start.19 = (bf16[80,80]{1,0:T(8,128)(2,1)S(1)}, bf16[80,80]{1,0:T(8,128)(2,1)S(1)}, u32[]{:S(2)}, u32[]{:S(2)}) collective-permute-start(bf16[80,80]{1,0:T(8,128)(2,1)S(1)} %get-tuple-element.42), channel_id=1, source_target_pairs={{0,128},{128,0},{1,129},{129,1},{2,130},{130,2},{3,131},{131,3},{4... | collective-permute-start | bytes 38408 | tf_op jit(solution)/shard_map/ppermute | solution.py:570

commit v2 on v1

--- a/solution.py
+++ b/solution.py
@@ -68,25 +68,37 @@
 
 
 def kernel_copies(kernel_hbm, kernel_ref, sems):
-    return [
-        pltpu.make_async_copy(kernel_hbm.at[pl.ds(dy, 1)], kernel_ref.at[pl.ds(dy, 1)], sems.at[dy])
-        for dy in range(3)
+    copies = []
+    for dx in range(3):
+        tap = (pl.ds(0, 1), pl.ds(dx, 1))
+        copies.append(pltpu.make_async_copy(kernel_hbm.at[tap], kernel_ref.at[tap], sems.at[dx]))
+    for dy in (1, 2):
+        row = (pl.ds(dy, 1),)
+        copies.append(pltpu.make_async_copy(kernel_hbm.at[row], kernel_ref.at[row], sems.at[dy + 2]))
+    return copies
+
+
+def conv_forward_body(pos, low, high, images_hbm, grad_hbm, kernel_hbm, out, *scratch):
+    kernel_ref, shifts, sems, images, image_sems = scratch
+    inputs = [
+        pltpu.make_async_copy(images_hbm, images, image_sems.at[0]),
+        pltpu.make_async_copy(grad_hbm, out.at[:, 1], image_sems.at[1]),
     ]
-
-
-def conv_forward_body(pos, images, low, high, grad_out, kernel_hbm, out, *rest):
-    kernel_ref, shifts, sems = rest
     copies = kernel_copies(kernel_hbm, kernel_ref, sems)
-    for copy in copies:
+    for copy in inputs[:1] + copies + inputs[1:]:
         copy.start()
+    inputs[0].wait()
     shifted_columns(images, low, high, pos[4], shifts, (0, 1, 2))
     total = images[...].astype(F32).reshape(256, C)
-    for dy in range(3):
-        copies[dy].wait()
+    for dx in range(3):
+        copies[dx].wait()
+        total = total + mm(shifts[0:256, dx * C : (dx + 1) * C], kernel_ref[0, dx])
+    for dy in (1, 2):
+        copies[dy + 2].wait()
         taps = kernel_ref[dy].reshape(3 * C, C)
         total = total + mm(shifts[32 * dy : 32 * dy + 256, :], taps)
     out[:, 0] = total.astype(BF16).reshape(8, 32, C)
-    out[:, 1] = grad_out[...]
+    inputs[1].wait()
 
 
 def conv_backward_body(pos, images, low, high, kernel_hbm, out, token, kernel_ref, shifts, sems):
@@ -97,9 +109,12 @@
     shifted_columns(images, low, high, pos[4], shifts, (2, 1, 0))
     total = images[...].astype(F32).reshape(256, C)
     for dy in range(3):
-        copies[dy].wait()
         at = 32 * (2 - dy)
+        if dy > 0:
+            copies[dy + 2].wait()
         for dx in range(3):
+            if dy == 0:
+                copies[dx].wait()
             total = total + mm_nt(shifts[at : at + 256, dx * C : (dx + 1) * C], kernel_ref[dy, dx])
     out[...] = total.astype(BF16).reshape(8, 32, C)
 
@@ -111,13 +126,18 @@
     return call(
         conv_forward_body,
         [sds((8, 2, 32, C))],
-        4,
-        1,
-        CONV_SCRATCH + (pltpu.SemaphoreType.DMA((3,)),),
+        2,
+        3,
+        CONV_SCRATCH
+        + (
+            pltpu.SemaphoreType.DMA((5,)),
+            pltpu.VMEM((8, 32, C), BF16),
+            pltpu.SemaphoreType.DMA((2,)),
+        ),
         limit=48,
         flops=2 * 256 * 9 * C * C,
         moved=9 * C * C * 2,
-    )(images, low, high, grad_out, kernel)[0]
+    )(low, high, images, grad_out, kernel)[0]
 
 
 def conv_backward(images, low, high, kernel):
@@ -126,23 +146,24 @@
         [sds((8, 32, C)), sds((8, 128), F32)],
         3,
         1,
-        CONV_SCRATCH + (pltpu.SemaphoreType.DMA((3,)),),
+        CONV_SCRATCH + (pltpu.SemaphoreType.DMA((5,)),),
         limit=48,
         flops=2 * 256 * 9 * C * C,
         moved=9 * C * C * 2,
     )(images, low, high, kernel)
 
 
-def halves_body(pos, time, qkv, out, half, sems):
+def halves_body(pos, time, qkv, out, images, half, twin, top, bottom, sems):
     core = pos[3]
     rows = time.at[pl.ds(pl.multiple_of(112 * core, 16), 128)]
 
     def run(first, second):
-        copies = [
-            pltpu.make_async_copy(rows, half.at[0:128], sems.at[0]),
-            pltpu.make_async_copy(first, half.at[128:208], sems.at[1]),
-            pltpu.make_async_copy(second, half.at[208:288], sems.at[2]),
-        ]
+        moves = [(images.at[pl.ds(0, 1)], top), (images.at[pl.ds(7, 1)], bottom)]
+        for target in (half, twin):
+            moves.append((rows, target.at[0:128]))
+            moves.append((first, target.at[128:208]))
+            moves.append((second, target.at[208:288]))
+        copies = [pltpu.make_async_copy(a, b, sems.at[i]) for i, (a, b) in enumerate(moves)]
         for copy in copies:
             copy.start()
         for copy in copies:
@@ -157,9 +178,10 @@
         run(qkv.at[:, 2 * C : 3 * C], out)
 
 
-def halves_of(time, qkv, out):
-    dma = (pltpu.SemaphoreType.DMA((3,)),)
-    return call(halves_body, [sds((288, C))], 0, 3, dma, limit=62)(time, qkv, out)[0]
+def halves_of(time, qkv, out, images):
+    dma = (pltpu.SemaphoreType.DMA((8,)),)
+    outs = [sds((288, C))] * 2 + [sds((1, 32, C))] * 2
+    return call(halves_body, outs, 0, 4, dma, limit=62)(time, qkv, out, images)
 
 
 def gate(value, after):
@@ -169,6 +191,7 @@
         in_specs=[pl.BlockSpec(memory_space=pl.ANY)] * 2,
         out_specs=pl.BlockSpec(memory_space=pl.ANY),
         input_output_aliases={0: 0},
+        compiler_params=pltpu.CompilerParams(vmem_limit_bytes=MIB),
     )(value, after)
 
 
@@ -238,10 +261,11 @@
 
 
 def temporal_body(pos, tile, gain, *refs):
-    time_pieces, (temporal_out, normal_out) = refs[:6], refs[6:8]
-    time_ref, padded, sem = refs[8:]
-    copies = time_copies(pos, time_pieces, time_ref, sem)
-    for copy in copies:
+    pieces, (temporal_out, normal_out, time_ref, weight_ref) = refs[:6], refs[6:10]
+    padded, sem, weight_sem = refs[10:]
+    copies = time_copies(pos, pieces, time_ref, sem)
+    later_copies = projection_copies(pos, pieces, weight_ref, weight_sem)
+    for copy in copies + later_copies:
         copy.start()
     value = tile[:, 0].astype(F32)
     padded[0] = jnp.zeros((32, C), BF16)
@@ -258,32 +282,28 @@
     value = temporal.astype(F32)
     scale = lax.rsqrt(jnp.mean(value * value, axis=-1, keepdims=True) + 1e-06)
     normal_out[...] = (value * scale * gain[...]).astype(BF16)
-
-
-TIME_SCRATCH = (pltpu.VMEM((8, 240, C), BF16), pltpu.VMEM((10, 32, C), BF16))
-
-
-def temporal_step(tile, gain, time_pieces):
+    for copy in later_copies:
+        copy.wait()
+
+
+PADDED = (pltpu.VMEM((10, 32, C), BF16),)
+
+
+def temporal_step(tile, gain, pieces):
     return call(
         temporal_body,
-        [sds((256, C)), sds((256, C))],
+        [sds((256, C)), sds((256, C)), sds((8, 240, C)), sds((8, 80, 4 * C))],
         2,
         6,
-        TIME_SCRATCH + (pltpu.SemaphoreType.DMA((15,)),),
-        limit=20,
+        PADDED + (pltpu.SemaphoreType.DMA((15,)), pltpu.SemaphoreType.DMA((20,))),
+        limit=24,
         flops=2 * 256 * 3 * C * C,
         moved=3 * C * C * 2,
-    )(tile, gain, *time_pieces)
-
-
-def attention_body(pos, normal, tile, *refs):
-    weight_pieces, (grad_packed, mixed_out, send) = refs[:6], refs[6:9]
-    weight_ref, packed, grad_blend, blended, sem = refs[9:]
-    copies = projection_copies(pos, weight_pieces, weight_ref, sem)
-    for copy in copies:
-        copy.start()
-    for copy in copies:
-        copy.wait()
+    )(tile, gain, *pieces)
+
+
+def attention_body(pos, normal, tile, weight_ref, grad_packed, mixed_out, send, *scratch):
+    packed, grad_blend, blended = scratch
     weight = weight_ref[...].reshape(C, 4 * C)
     packed[...] = mm(normal[...], weight[:, : 3 * C]).astype(BF16).reshape(8, 2, 16, 3 * C)
     grad_blend[...] = mm_nt(tile[:, 1].reshape(256, C), weight[:, 3 * C :]).astype(BF16).reshape(8, 2, 16, C)
@@ -397,35 +417,25 @@
     )(normal, mixed, tile, grad_packed)[0]
 
 
-def attention_step(normal, tile, weight_pieces):
+def attention_step(normal, tile, weight):
     return call(
         attention_body,
         [sds((8, 2, 16, 3 * C)), sds((256, C)), sds(BLOCKS)],
-        2,
-        6,
+        3,
+        0,
         (
-            pltpu.VMEM((8, 80, 4 * C), BF16),
             pltpu.VMEM((8, 2, 16, 3 * C), BF16),
             pltpu.VMEM((8, 2, 16, C), BF16),
             pltpu.VMEM((8, 2, 16, C), BF16),
-            pltpu.SemaphoreType.DMA((20,)),
         ),
-        limit=36,
+        limit=32,
         flops=2 * 256 * 8 * C * C,
         moved=4 * C * C * 2,
-    )(normal, tile, *weight_pieces)
+    )(normal, tile, weight)
 
 
 def tile_gradient_body(pos, *refs):
-    grad_packed, temporal, tile, gain = refs[:4]
-    pieces, out = refs[4:10], refs[11]
-    weight_ref, time_ref, padded, sem, time_sem = refs[12:]
-    copies = projection_copies(pos, pieces, weight_ref, sem)
-    later_copies = time_copies(pos, pieces, time_ref, time_sem)
-    for copy in copies + later_copies:
-        copy.start()
-    for copy in copies:
-        copy.wait()
+    grad_packed, temporal, tile, gain, weight_ref, time_ref, _, out, padded = refs
     weight = weight_ref[...].reshape(C, 4 * C)[:, : 3 * C]
     grad_normal = mm_nt(grad_packed[...].reshape(256, 3 * C), weight)
     value = temporal[...].astype(F32)
@@ -437,8 +447,6 @@
     padded[0] = jnp.zeros((32, C), BF16)
     padded[1:9] = grad_temporal.reshape(8, 32, C)
     padded[9] = jnp.zeros((32, C), BF16)
-    for copy in later_copies:
-        copy.wait()
     taps = time_ref[...].reshape(3 * C, C)
     grad_act = jnp.zeros((256, C), F32)
     for k in range(3):
@@ -452,19 +460,17 @@
     out[...] = grad_spatial.astype(BF16).reshape(8, 32, C)
 
 
-def tile_gradient(grad_packed, temporal, tile, gain, weights, after):
+def tile_gradient(grad_packed, temporal, tile, gain, weight, time, after):
     return call(
         tile_gradient_body,
         [sds((8, 32, C))],
-        4,
-        7,
-        (pltpu.VMEM((8, 80, 4 * C), BF16),)
-        + TIME_SCRATCH
-        + (pltpu.SemaphoreType.DMA((20,)), pltpu.SemaphoreType.DMA((15,))),
-        limit=28,
+        6,
+        1,
+        PADDED,
+        limit=24,
         flops=2 * 256 * 6 * C * C,
         moved=7 * C * C * 2,
-    )(grad_packed, temporal, tile, gain, *weights, after)[0]
+    )(grad_packed, temporal, tile, gain, weight, time, after)[0]
 
 
 def pair_sum_body(pos, keep, other, own, *sends):
@@ -572,9 +578,9 @@
     return [grad.T for grad in grads]
 
 
-def edges(images):
-    low = lax.ppermute(images[7:8], "zh", [(i, (i + 1) % 4) for i in range(4)])
-    high = lax.ppermute(images[0:1], "zh", [(i, (i + 3) % 4) for i in range(4)])
+def edges(top, bottom):
+    low = lax.ppermute(bottom, "zh", [(i, (i + 1) % 4) for i in range(4)])
+    high = lax.ppermute(top, "zh", [(i, (i + 3) % 4) for i in range(4)])
     return low, high
 
 
@@ -585,23 +591,23 @@
 def shards(latents, space_kernel, time_kernel, qkv_weight, out_weight, norm_gain, grad_out):
     images, incoming = latents[0, 0], grad_out[0, 0]
     gain = norm_gain.reshape(1, C)
-    low, high = edges(images)
-    half = halves_of(time_kernel, qkv_weight, out_weight)
+    half, twin, top, bottom = halves_of(time_kernel, qkv_weight, out_weight, images)
     others = round_trip([half] * 3, "y")
-    near = across(half)
+    low, high = edges(top, bottom)
+    near = across(gate(twin, high))
     rows = conv_forward(images, low, high, incoming, space_kernel)
     tile = exchange(rows)
     own, three = four_of(half, others, rows, near)
     far = gate(across(three), tile)
     weights = [own, swapped(own), near, swapped(near), far, swapped(far)]
-    temporal, normal = temporal_step(tile, gain, weights)
-    grad_packed, mixed, send = attention_step(normal, tile, weights)
+    temporal, normal, time, weight = temporal_step(tile, gain, weights)
+    grad_packed, mixed, send = attention_step(normal, tile, weight)
     keep = own_gradient(normal, mixed, tile, grad_packed)
     summed = pair_sum(keep, send)
     grad_spatial = exchange(
-        tile_gradient(grad_packed, temporal, tile, gain, weights, summed[0])
+        tile_gradient(grad_packed, temporal, tile, gain, weight, time, summed[0])
     )
-    low, high = edges(grad_spatial)
+    low, high = edges(grad_spatial[0:1], grad_spatial[7:8])
     grad_latents, token = conv_backward(grad_spatial, low, high, space_kernel)
     grad_qkv, grad_outproj = reduce_grads(summed, token)
     return grad_latents[None, None], grad_qkv, grad_outproj

time: 118 us -> 111 us (0.941); the launches traced: 116 us -> 111 us
  local copies, waits for them, and re-layouts: 5.99 us -> 1.17 us
  waiting for transfers between devices: 32.7 us -> 36.4 us
  Pallas kernels: 36.7 us -> 33.3 us
    ppermute x4, starting transfers between devices: 4.53 us -> 10.6 us  [the longest x2 7.26 us: edges(): high = lax.ppermute(top, 'zh', [(i, (i + 3) % 4) for i in range(4)])]
    ppermute x2, starting transfers between devices: 7.27 us -> 2.27 us  [across(): return lax.ppermute(own, ('zl', 'c', 'zh'), pairs)]
    ppermute x6, waiting for transfers between devices: 0.52 us -> 5.28 us  [crosswise(): moved.append(lax.ppermute(sends[k], ('y', 'x', 'c'), pairs))]
    ppermute x3, waiting for transfers between devices: 0.01 us -> 4.36 us  [round_trip(): lax.ppermute(sends[k], axis, [(i, (i + k + 1) % 4) for i in range(4)])]
    ppermute x4, waiting for transfers between devices: 9.56 us -> 5.47 us  [the longest x2 5.46 us: edges(): low = lax.ppermute(bottom, 'zh', [(i, (i + 1) % 4) for i in range(4)])]
    unnamed x28 -> x12, local copies, waits for them, and re-layouts: 5.18 us -> 1.16 us
    all_to_all x2, waiting for transfers between devices: 12.1 us -> 9.54 us  [exchange(): return lax.all_to_all(rows, FRAME, split_axis=0, concat_axis=0, tiled=True)]
    pallas_call x1, Pallas kernels: 9.1 us -> 7.65 us  [attention_step(): call(attention_body, [sds((8, 2, 16, 3 * C)), sds((256, C)), sds(BLOCKS)]...]
  transfers between devices with their start and end apart: 23 -> 23, of which waited for: 9 -> 12; matrix products, arithmetic and copies ran while one was open for 1% -> 0% of each run, Pallas kernels for 17% -> 16%
where the time goes in v2:
time: 111 us
  starting transfers between devices  39.3 us (35%)
  waiting for transfers between devices  36.4 us (33%)
  Pallas kernels  33.3 us (30%)
  local copies, waits for them, and re-layouts  1.17 us (1%)
    all_to_all x2, starting transfers between devices, exchange(): return lax.all_to_all(rows, FRAME, split_axis=0, concat_axis=0, tiled=True)  10.2 us
    all_to_all x2, waiting for transfers between devices, exchange(): return lax.all_to_all(rows, FRAME, split_axis=0, concat_axis=0, tiled=True)  9.54 us
    pallas_call x1, Pallas kernels, attention_step(): call(attention_body, [sds((8, 2, 16, 3 * C)), sds((256, C)), sds(BLOCKS)]...  7.65 us
    ppermute x2, starting transfers between devices, edges(): high = lax.ppermute(top, 'zh', [(i, (i + 3) % 4) for i in range(4)])  7.26 us
    ppermute x6, starting transfers between devices, crosswise(): moved.append(lax.ppermute(sends[k], ('y', 'x', 'c'), pairs))  6.84 us
    pallas_call x1, Pallas kernels, conv_backward(): call(conv_backward_body, [sds((8, 32, C)), sds((8, 128), F32)], 3, 1, CON...  5.77 us
    pallas_call x1, Pallas kernels, conv_forward(): call(conv_forward_body, [sds((8, 2, 32, C))], 2, 3, CONV_SCRATCH + (pltpu...  5.47 us
    ppermute x2, waiting for transfers between devices, edges(): low = lax.ppermute(bottom, 'zh', [(i, (i + 1) % 4) for i in range(4)])  5.46 us
  transfers between devices with their start and end apart: 23, of which 12 were waited for; matrix products, arithmetic and copies ran while one was open for 0% of the time, Pallas kernels for 16%

profile of v2, /device:TPU:6, one launch (start us, length us, event | category | flops | bytes accessed | tf_op | source)
XLA Modules:
  0.0 110.9 jit_solution(10267882718630481076)
XLA Ops:
  0.7 2.3 %shard_map.94 = (bf16[288,640]{1,0:T(8,128)(2,1)}, bf16[288,640]{1,0:T(8,128)(2,1)}, bf16[1,32,640]{2,1,0:T(8,128)(2,1)}, bf16[1,32,640]{2,1,0:T(8,128)(2,1)}) custom-call(bf16[240,640]{1,0:T(8,128)(2,1)} %refs_0_.1, bf16[80,1920]{1,0:T(8,128)(2,1)} %refs_1_.1, bf16[80,640]{1,0:T(8,128)(2,1)} %refs_2_.1, bf16[8,32,640]{2,1,0:T(8,128)(2,1)} %bitcast.5), custom_call_target="tpu_custom_call" | custom-call | tf_op jit(solution)/shard_map/pallas_call | solution.py:184
  2.9 6.4 %collective-permute-start.1 = (bf16[1,32,640]{2,1,0:T(8,128)(2,1)}, bf16[1,32,640]{2,1,0:T(8,128)(2,1)S(1)}, u32[]{:S(2)}, u32[]{:S(2)}) collective-permute-start(bf16[1,32,640]{2,1,0:T(8,128)(2,1)} %get-tuple-element.31), channel_id=1, source_target_pairs={{0,3},{1,0},{2,1},{3,2},{4,7},{5,4},{6,5},{7,6},{8,11},{9,8},{10,9... | collective-permute-start | bytes 122888 | tf_op jit(solution)/shard_map/ppermute | solution.py:583
  9.3 3.0 %collective-permute-start.4 = (bf16[288,640]{1,0:T(8,128)(2,1)}, bf16[288,640]{1,0:T(8,128)(2,1)S(1)}, u32[]{:S(2)}, u32[]{:S(2)}) collective-permute-start(bf16[288,640]{1,0:T(8,128)(2,1)} %get-tuple-element.32.refs_0_), channel_id=1, source_target_pairs={{0,96},{32,0},{64,32},{96,64},{1,97},{33,1},{65,33},{97,65},{2,98}... | collective-permute-start | bytes 1105928 | tf_op jit(solution)/shard_map/ppermute | solution.py:531
  12.3 0.6 collective-permute-start.3
  12.9 1.0 collective-permute-start.2
  13.9 1.3 %collective-permute-start.5 = (bf16[288,640]{1,0:T(8,128)(2,1)}, bf16[288,640]{1,0:T(8,128)(2,1)S(1)}, u32[]{:S(2)}, u32[]{:S(2)}) collective-permute-start(bf16[288,640]{1,0:T(8,128)(2,1)} %shard_map.96), channel_id=1, source_target_pairs={{0,131},{4,132},{128,0},{132,5},{1,128},{5,133},{129,1},{133,6},{2... | collective-permute-start | bytes 1105928 | tf_op jit(solution)/shard_map/ppermute | solution.py:217
  15.2 1.2 %collective-permute-start = (bf16[1,32,640]{2,1,0:T(8,128)(2,1)}, bf16[1,32,640]{2,1,0:T(8,128)(2,1)S(1)}, u32[]{:S(2)}, u32[]{:S(2)}) collective-permute-start(bf16[1,32,640]{2,1,0:T(8,128)(2,1)} %get-tuple-element.30), channel_id=1, source_target_pairs={{0,1},{1,2},{2,3},{3,0},{4,5},{5,6},{6,7},{7,4},{8,9},{9,10},{10,1... | collective-permute-start | bytes 122888 | tf_op jit(solution)/shard_map/ppermute | solution.py:582
  16.4 5.5 %collective-permute-done.refs_0_ = bf16[1,32,640]{2,1,0:T(8,128)(2,1)S(1)} collective-permute-done((bf16[1,32,640]{2,1,0:T(8,128)(2,1)}, bf16[1,32,640]{2,1,0:T(8,128)(2,1)S(1)}, u32[]{:S(2)}, u32[]{:S(2)}) %collective-permute-start) | collective-permute-done | bytes 40992 | tf_op jit(solution)/shard_map/ppermute | solution.py:582
  21.9 5.5 %shard_map.95.refs_4_ = bf16[8,2,32,640]{3,2,1,0:T(8,128)(2,1)} custom-call(bf16[1,32,640]{2,1,0:T(8,128)(2,1)S(1)} %collective-permute-done.refs_0_, bf16[1,32,640]{2,1,0:T(8,128)(2,1)S(1)} %collective-permute-done.1.refs_1_.b, bf16[8,32,640]{2,1,0:T(8,128)(2,1)S(1)} %bitcast.6, bf16[8,32,640]{2,1,0:T(8,128)(2,1)S(1)} %bitcast.7, ...), custom_call_target="tpu_custom_call" | custom-call | flops 1887436800 | bytes 7372800 | tf_op jit(solution)/shard_map/pallas_call | solution.py:126
  27.4 0.8 collective-permute-done.4.refs_3_
  28.1 3.6 %collective-permute-done.2.refs_1_ = bf16[288,640]{1,0:T(8,128)(2,1)S(1)} collective-permute-done((bf16[288,640]{1,0:T(8,128)(2,1)}, bf16[288,640]{1,0:T(8,128)(2,1)S(1)}, u32[]{:S(2)}, u32[]{:S(2)}) %collective-permute-start.2) | collective-permute-done | bytes 368672 | tf_op jit(solution)/shard_map/ppermute | solution.py:531
  31.7 0.2 shard_map.97
  31.9 1.1 %copy-done = bf16[4,288,640]{2,1,0:T(8,128)(2,1)} copy-done((bf16[4,288,640]{2,1,0:T(8,128)(2,1)}, bf16[4,288,640]{2,1,0:T(8,128)(2,1)S(1)}, u32[]{:S(2)}) %copy-start) | copy-done | bytes 1474584
  33.1 1.0 collective-permute-start.8
  34.1 4.8 %all-to-all-start = ((bf16[8,2,32,640]{3,2,1,0:T(8,128)(2,1)}), bf16[8,2,32,640]{3,2,1,0:T(8,128)(2,1)S(1)}, u32[]{:S(2)}, u32[]{:S(2)}) async-start(bf16[8,2,32,640]{3,2,1,0:T(8,128)(2,1)} %shard_map.95.refs_4_), calls=%async_computation | async-start | bytes 1310720 | tf_op jit(solution)/shard_map/all_to_all | solution.py:588
  38.9 0.1 collective-permute-start.6
  39.0 9.5 %all-to-all-done.b.refs_0_.refs_1_.refs_2_ = bf16[8,2,32,640]{3,2,1,0:T(8,128)(2,1)S(1)} async-done(((bf16[8,2,32,640]{3,2,1,0:T(8,128)(2,1)}), bf16[8,2,32,640]{3,2,1,0:T(8,128)(2,1)S(1)}, u32[]{:S(2)}, u32[]{:S(2)}) %all-to-all-start) | async-done | bytes 655392 | tf_op jit(solution)/shard_map/all_to_all | solution.py:588
  48.6 0.1 collective-permute-start.9
  48.7 0.4 collective-permute-start.7
  49.1 2.8 %collective-permute-done.7.refs_5_ = bf16[288,640]{1,0:T(8,128)(2,1)S(1)} collective-permute-done((bf16[288,640]{1,0:T(8,128)(2,1)S(1)}, bf16[288,640]{1,0:T(8,128)(2,1)S(1)}, u32[]{:S(2)}, u32[]{:S(2)}) %collective-permute-start.7) | collective-permute-done | bytes 368672 | tf_op jit(solution)/shard_map/ppermute | solution.py:221
  51.8 3.8 %shard_map.99 = (bf16[256,640]{1,0:T(8,128)(2,1)S(1)}, bf16[256,640]{1,0:T(8,128)(2,1)S(1)}, bf16[8,240,640]{2,1,0:T(8,128)(2,1)S(1)}, bf16[8,80,2560]{2,1,0:T(8,128)(2,1)S(1)}) custom-call(bf16[8,2,32,640]{3,2,1,0:T(8,128)(2,1)S(1)} %all-to-all-done.b.refs_0_.refs_1_.refs_2_, f32[1,640]{1,0:T(1,128)S(1)} %reshape.9.refs_1_.refs_3_, ...), custom_call_target="tpu_custom_call" | custom-call | flops 629145600 | bytes 2457600 | tf_op jit(solution)/shard_map/pallas_call | solution.py:293
  55.7 7.6 %shard_map.100 = (bf16[8,2,16,1920]{3,2,1,0:T(8,128)(2,1)S(1)}, bf16[256,640]{1,0:T(8,128)(2,1)S(1)}, bf16[4,4,80,640]{3,2,1,0:T(8,128)(2,1)S(1)}) custom-call(bf16[256,640]{1,0:T(8,128)(2,1)S(1)} %get-tuple-element.36.refs_0_, bf16[8,2,32,640]{3,2,1,0:T(8,128)(2,1)S(1)} %all-to-all-done.b.refs_0_.refs_1_.refs_2_, ...), custom_call_target="tpu_custom_call" | custom-call | flops 1677721600 | bytes 3276800 | tf_op jit(solution)/shard_map/pallas_call | solution.py:421
  63.3 0.1 collective-permute-start.10
  63.4 1.1 %shard_map.101.refs_0_ = bf16[4,4,80,640]{3,2,1,0:T(8,128)(2,1)S(1)} custom-call(bf16[256,640]{1,0:T(8,128)(2,1)S(1)} %get-tuple-element.36.refs_0_, bf16[256,640]{1,0:T(8,128)(2,1)S(1)} %get-tuple-element.41.refs_1_, bf16[8,2,32,640]{3,2,1,0:T(8,128)(2,1)S(1)} %all-to-all-done.b.refs_0_.refs_1_.refs_2_, ...), custom_call_target="tpu_custom_call" | custom-call | flops 419430400 | bytes 1638400 | tf_op jit(solution)/shard_map/pallas_call | solution.py:409
  64.6 2.4 %collective-permute-done.10.refs_1_ = bf16[4,4,80,640]{3,2,1,0:T(8,128)(2,1)S(1)} collective-permute-done((bf16[4,4,80,640]{3,2,1,0:T(8,128)(2,1)S(1)}, bf16[4,4,80,640]{3,2,1,0:T(8,128)(2,1)S(1)}, u32[]{:S(2)}, u32[]{:S(2)}) %collective-permute-start.10) | collective-permute-done | bytes 1638432 | tf_op jit(solution)/shard_map/ppermute | solution.py:221
  66.9 1.0 shard_map.102
  68.0 2.1 %collective-permute-start.14 = (bf16[4,80,640]{2,1,0:T(8,128)(2,1)S(1)}, bf16[4,80,640]{2,1,0:T(8,128)(2,1)S(1)}, u32[]{:S(2)}, u32[]{:S(2)}) collective-permute-start(bf16[4,80,640]{2,1,0:T(8,128)(2,1)S(1)} %get-tuple-element.46), channel_id=1, source_target_pairs={{0,64},{4,20},{8,72},{12,28},{16,80},{20,4},{24,88},{28,12},{32,96... | collective-permute-start | bytes 1228808 | tf_op jit(solution)/shard_map/ppermute | solution.py:549
  70.0 1.2 %collective-permute-start.15 = (bf16[4,80,640]{2,1,0:T(8,128)(2,1)S(1)}, bf16[4,80,640]{2,1,0:T(8,128)(2,1)S(1)}, u32[]{:S(2)}, u32[]{:S(2)}) collective-permute-start(bf16[4,80,640]{2,1,0:T(8,128)(2,1)S(1)} %get-tuple-element.47), channel_id=1, source_target_pairs={{0,96},{4,28},{8,104},{12,4},{16,112},{20,12},{24,120},{28,20},{32... | collective-permute-start | bytes 1228808 | tf_op jit(solution)/shard_map/ppermute | solution.py:549
  71.2 3.7 %shard_map.103 = bf16[8,32,640]{2,1,0:T(8,128)(2,1)} custom-call(bf16[8,2,16,1920]{3,2,1,0:T(8,128)(2,1)S(1)} %get-tuple-element.38.refs_3_.refs_0_, bf16[256,640]{1,0:T(8,128)(2,1)S(1)} %get-tuple-element.39.refs_1_, bf16[8,2,32,640]{3,2,1,0:T(8,128)(2,1)S(1)} %all-to-all-done.b.refs_0_.refs_1_.refs_2_, f32[1,640]{1,0:T(1,128)S(1)} %reshape.9.refs_1_.refs_3_, ...), custom_call_target="tpu_custom_call" | custom-call | flops 1258291200 | bytes 5734400 | tf_op jit(solution)/shard_map/pallas_call | solution.py:464
  74.9 5.4 %all-to-all-start.1 = ((bf16[8,32,640]{2,1,0:T(8,128)(2,1)}), bf16[8,32,640]{2,1,0:T(8,128)(2,1)S(1)}, u32[]{:S(2)}, u32[]{:S(2)}) async-start(bf16[8,32,640]{2,1,0:T(8,128)(2,1)} %shard_map.103), calls=%async_computation.1 | async-start | bytes 655360 | tf_op jit(solution)/shard_map/all_to_all | solution.py:588
  80.4 1.4 %collective-permute-done.13.refs_1_ = bf16[4,80,640]{2,1,0:T(8,128)(2,1)S(1)} collective-permute-done((bf16[4,80,640]{2,1,0:T(8,128)(2,1)}, bf16[4,80,640]{2,1,0:T(8,128)(2,1)S(1)}, u32[]{:S(2)}, u32[]{:S(2)}) %collective-permute-start.13) | collective-permute-done | bytes 409632 | tf_op jit(solution)/shard_map/ppermute | solution.py:549
  81.7 0.7 collective-permute-done.15.refs_3_
  82.4 0.6 shard_map.105
  83.0 2.2 %collective-permute-start.16 = (bf16[2,80,320]{2,1,0:T(8,128)(2,1)S(1)}, bf16[2,80,320]{2,1,0:T(8,128)(2,1)S(1)}, u32[]{:S(2)}, u32[]{:S(2)}) collective-permute-start(bf16[2,80,320]{2,1,0:T(8,128)(2,1)S(1)} %get-tuple-element.49), channel_id=1, source_target_pairs={{0,8},{4,36},{8,16},{12,44},{16,24},{20,52},{24,0},{28,60},{32,40}... | collective-permute-start | bytes 307208 | tf_op jit(solution)/shard_map/ppermute | solution.py:549
  85.1 0.8 collective-permute-start.17
  85.9 0.7 collective-permute-start.18
  86.6 0.9 collective-permute-start.12
  87.5 2.2 %collective-permute-start.11 = (bf16[1,32,640]{2,1,0:T(8,128)(2,1)S(1)}, bf16[1,32,640]{2,1,0:T(8,128)(2,1)S(1)}, u32[]{:S(2)}, u32[]{:S(2)}) collective-permute-start(bf16[1,32,640]{2,1,0:T(8,128)(2,1)S(1)} %get-tuple-element.58), channel_id=1, source_target_pairs={{0,1},{1,2},{2,3},{3,0},{4,5},{5,6},{6,7},{7,4},{8,9},{9,10},{10,1... | collective-permute-start | bytes 122888 | tf_op jit(solution)/shard_map/ppermute | solution.py:582
  89.6 2.0 %collective-permute-done.17.refs_2_ = bf16[2,80,320]{2,1,0:T(8,128)(2,1)S(1)} collective-permute-done((bf16[2,80,320]{2,1,0:T(8,128)(2,1)S(1)}, bf16[2,80,320]{2,1,0:T(8,128)(2,1)S(1)}, u32[]{:S(2)}, u32[]{:S(2)}) %collective-permute-start.17) | collective-permute-done | bytes 102432 | tf_op jit(solution)/shard_map/ppermute | solution.py:549
  91.6 1.2 %collective-permute-done.18.refs_3_ = bf16[2,80,320]{2,1,0:T(8,128)(2,1)S(1)} collective-permute-done((bf16[2,80,320]{2,1,0:T(8,128)(2,1)S(1)}, bf16[2,80,320]{2,1,0:T(8,128)(2,1)S(1)}, u32[]{:S(2)}, u32[]{:S(2)}) %collective-permute-start.18) | collective-permute-done | bytes 102432 | tf_op jit(solution)/shard_map/ppermute | solution.py:549
  92.8 0.9 shard_map.106
  93.7 3.3 %all-to-all-start.2 = ((bf16[4,2,80,80]{3,2,1,0:T(8,128)(2,1)}), bf16[4,2,80,80]{3,2,1,0:T(8,128)(2,1)S(1)}, u32[]{:S(2)}, u32[]{:S(2)}) async-start(bf16[4,2,80,80]{3,2,1,0:T(8,128)(2,1)} %shard_map.106), calls=%async_computation.2 | async-start | bytes 327680 | tf_op jit(solution)/shard_map/all_to_all | solution.py:572
  97.1 5.8 %shard_map.104 = (bf16[8,32,640]{2,1,0:T(8,128)(2,1)}, f32[8,128]{1,0:T(8,128)S(1)}) custom-call(bf16[8,32,640]{2,1,0:T(8,128)(2,1)S(1)} %all-to-all-done.1.refs_0_, bf16[1,32,640]{2,1,0:T(8,128)(2,1)S(1)} %collective-permute-done.11.refs_1_, bf16[1,32,640]{2,1,0:T(8,128)(2,1)S(1)} %collective-permute-done.12.refs_2_, bf16[3,3,640,640]{3,2,1,0:T(8,128)(2,1)} %refs_3_.1), custom_call_target="tpu_custom_call" | custom-call | flops 1887436800 | bytes 7372800 | tf_op jit(solution)/shard_map/pallas_call | solution.py:144
  102.9 3.4 %all-to-all-done.2.refs_0_ = bf16[4,2,80,80]{3,2,1,0:T(8,128)(2,1)S(1)} async-done(((bf16[4,2,80,80]{3,2,1,0:T(8,128)(2,1)}), bf16[4,2,80,80]{3,2,1,0:T(8,128)(2,1)S(1)}, u32[]{:S(2)}, u32[]{:S(2)}) %all-to-all-start.2) | async-done | bytes 102432 | tf_op jit(solution)/shard_map/all_to_all | solution.py:572
  106.3 0.1 shard_map.107
  106.3 0.6 collective-permute-start.19
  106.9 3.3 %collective-permute-done.19.refs_1_ = bf16[80,80]{1,0:T(8,128)(2,1)S(1)} collective-permute-done((bf16[80,80]{1,0:T(8,128)(2,1)S(1)}, bf16[80,80]{1,0:T(8,128)(2,1)S(1)}, u32[]{:S(2)}, u32[]{:S(2)}) %collective-permute-start.19) | collective-permute-done | bytes 12832 | tf_op jit(solution)/shard_map/ppermute | solution.py:576
  110.2 0.7 shard_map.108
  (27 shorter events, 0.1 us)
Async XLA Ops:
  0.6 21.2 %copy-start.2 = (bf16[1,1,8,32,640]{4,3,2,1,0:T(8,128)(2,1)S(1)}, bf16[1,1,8,32,640]{4,3,2,1,0:T(8,128)(2,1)}, u32[]{:S(2)}) copy-start(bf16[1,1,8,32,640]{4,3,2,1,0:T(8,128)(2,1)} %param.7) | copy-start | bytes 983044
  0.6 21.2 %copy-start.4 = (bf16[1,1,8,32,640]{4,3,2,1,0:T(8,128)(2,1)S(1)}, bf16[1,1,8,32,640]{4,3,2,1,0:T(8,128)(2,1)}, u32[]{:S(2)}) copy-start(bf16[1,1,8,32,640]{4,3,2,1,0:T(8,128)(2,1)} %param.13) | copy-start | bytes 983044
  2.9 11.0 %collective-permute-start.1 = (bf16[1,32,640]{2,1,0:T(8,128)(2,1)}, bf16[1,32,640]{2,1,0:T(8,128)(2,1)S(1)}, u32[]{:S(2)}, u32[]{:S(2)}) collective-permute-start(bf16[1,32,640]{2,1,0:T(8,128)(2,1)} %get-tuple-element.31), channel_id=1, source_target_pairs={{0,3},{1,0},{2,1},{3,2},{4,7},{5,4},{6,5},{7,6},{8,11},{9,8},{10,9... | collective-permute-start | bytes 122888 | tf_op jit(solution)/shard_map/ppermute | solution.py:583
  9.3 18.8 %collective-permute-start.4 = (bf16[288,640]{1,0:T(8,128)(2,1)}, bf16[288,640]{1,0:T(8,128)(2,1)S(1)}, u32[]{:S(2)}, u32[]{:S(2)}) collective-permute-start(bf16[288,640]{1,0:T(8,128)(2,1)} %get-tuple-element.32.refs_0_), channel_id=1, source_target_pairs={{0,96},{32,0},{64,32},{96,64},{1,97},{33,1},{65,33},{97,65},{2,98}... | collective-permute-start | bytes 1105928 | tf_op jit(solution)/shard_map/ppermute | solution.py:531
  12.3 15.8 %collective-permute-start.3 = (bf16[288,640]{1,0:T(8,128)(2,1)}, bf16[288,640]{1,0:T(8,128)(2,1)S(1)}, u32[]{:S(2)}, u32[]{:S(2)}) collective-permute-start(bf16[288,640]{1,0:T(8,128)(2,1)} %get-tuple-element.32.refs_0_), channel_id=1, source_target_pairs={{0,64},{32,96},{64,0},{96,32},{1,65},{33,97},{65,1},{97,33},{2,66}... | collective-permute-start | bytes 1105928 | tf_op jit(solution)/shard_map/ppermute | solution.py:531
  12.9 18.8 %collective-permute-start.2 = (bf16[288,640]{1,0:T(8,128)(2,1)}, bf16[288,640]{1,0:T(8,128)(2,1)S(1)}, u32[]{:S(2)}, u32[]{:S(2)}) collective-permute-start(bf16[288,640]{1,0:T(8,128)(2,1)} %get-tuple-element.32.refs_0_), channel_id=1, source_target_pairs={{0,32},{32,64},{64,96},{96,0},{1,33},{33,65},{65,97},{97,1},{2,34}... | collective-permute-start | bytes 1105928 | tf_op jit(solution)/shard_map/ppermute | solution.py:531
  13.9 17.8 %collective-permute-start.5 = (bf16[288,640]{1,0:T(8,128)(2,1)}, bf16[288,640]{1,0:T(8,128)(2,1)S(1)}, u32[]{:S(2)}, u32[]{:S(2)}) collective-permute-start(bf16[288,640]{1,0:T(8,128)(2,1)} %shard_map.96), channel_id=1, source_target_pairs={{0,131},{4,132},{128,0},{132,5},{1,128},{5,133},{129,1},{133,6},{2... | collective-permute-start | bytes 1105928 | tf_op jit(solution)/shard_map/ppermute | solution.py:217
  15.2 6.7 %collective-permute-start = (bf16[1,32,640]{2,1,0:T(8,128)(2,1)}, bf16[1,32,640]{2,1,0:T(8,128)(2,1)S(1)}, u32[]{:S(2)}, u32[]{:S(2)}) collective-permute-start(bf16[1,32,640]{2,1,0:T(8,128)(2,1)} %get-tuple-element.30), channel_id=1, source_target_pairs={{0,1},{1,2},{2,3},{3,0},{4,5},{5,6},{6,7},{7,4},{8,9},{9,10},{10,1... | collective-permute-start | bytes 122888 | tf_op jit(solution)/shard_map/ppermute | solution.py:582
  21.9 9.8 %copy-start.3 = (bf16[288,640]{1,0:T(8,128)(2,1)S(1)}, bf16[288,640]{1,0:T(8,128)(2,1)}, u32[]{:S(2)}) copy-start(bf16[288,640]{1,0:T(8,128)(2,1)} %get-tuple-element.32.refs_0_) | copy-start | bytes 1105924
  31.9 1.1 %copy-start = (bf16[4,288,640]{2,1,0:T(8,128)(2,1)}, bf16[4,288,640]{2,1,0:T(8,128)(2,1)S(1)}, u32[]{:S(2)}) copy-start(bf16[4,288,640]{2,1,0:T(8,128)(2,1)S(1)} %get-tuple-element.34.refs_2_) | copy-start | bytes 4423684
  33.1 15.5 %collective-permute-start.8 = (bf16[3,288,640]{2,1,0:T(8,128)(2,1)S(1)}, bf16[3,288,640]{2,1,0:T(8,128)(2,1)S(1)}, u32[]{:S(2)}, u32[]{:S(2)}) collective-permute-start(bf16[3,288,640]{2,1,0:T(8,128)(2,1)S(1)} %get-tuple-element.35), channel_id=1, source_target_pairs={{0,131},{4,132},{128,0},{132,5},{1,128},{5,133},{129,1},{133,6},{2... | collective-permute-start | bytes 3317768 | tf_op jit(solution)/shard_map/ppermute | solution.py:217
  34.1 14.5 %all-to-all-start = ((bf16[8,2,32,640]{3,2,1,0:T(8,128)(2,1)}), bf16[8,2,32,640]{3,2,1,0:T(8,128)(2,1)S(1)}, u32[]{:S(2)}, u32[]{:S(2)}) async-start(bf16[8,2,32,640]{3,2,1,0:T(8,128)(2,1)} %shard_map.95.refs_4_), calls=%async_computation | async-start | bytes 1310720 | tf_op jit(solution)/shard_map/all_to_all | solution.py:588
  38.9 10.2 %copy-start.5 = (f32[640]{0:T(1024)S(1)}, f32[640]{0:T(1024)}, u32[]{:S(2)}) copy-start(f32[640]{0:T(1024)} %param.12) | copy-start | bytes 7684
  38.9 13.0 %collective-permute-start.6 = (bf16[4,288,640]{2,1,0:T(8,128)(2,1)}, bf16[4,288,640]{2,1,0:T(8,128)(2,1)}, u32[]{:S(2)}, u32[]{:S(2)}) collective-permute-start(bf16[4,288,640]{2,1,0:T(8,128)(2,1)} %copy-done), channel_id=1, source_target_pairs={{0,4},{4,0},{1,5},{5,1},{2,6},{6,2},{3,7},{7,3},{8,12},{12,8},{9,1... | collective-permute-start | bytes 4423688 | tf_op jit(solution)/shard_map/ppermute | solution.py:221
  48.6 3.3 %copy-start.1 = (bf16[4,288,640]{2,1,0:T(8,128)(2,1)S(1)}, bf16[4,288,640]{2,1,0:T(8,128)(2,1)}, u32[]{:S(2)}) copy-start(bf16[4,288,640]{2,1,0:T(8,128)(2,1)} %copy-done) | copy-start | bytes 4423684
  48.6 3.3 %collective-permute-start.9 = (bf16[3,288,640]{2,1,0:T(8,128)(2,1)S(1)}, bf16[3,288,640]{2,1,0:T(8,128)(2,1)S(1)}, u32[]{:S(2)}, u32[]{:S(2)}) collective-permute-start(bf16[3,288,640]{2,1,0:T(8,128)(2,1)S(1)} %shard_map.98.refs_6_), channel_id=1, source_target_pairs={{0,4},{4,0},{1,5},{5,1},{2,6},{6,2},{3,7},{7,3},{8,12},{12,8},{9,1... | collective-permute-start | bytes 3317768 | tf_op jit(solution)/shard_map/ppermute | solution.py:221
  48.7 3.2 %collective-permute-start.7 = (bf16[288,640]{1,0:T(8,128)(2,1)S(1)}, bf16[288,640]{1,0:T(8,128)(2,1)S(1)}, u32[]{:S(2)}, u32[]{:S(2)}) collective-permute-start(bf16[288,640]{1,0:T(8,128)(2,1)S(1)} %collective-permute-done.5.refs_5_.refs_4_), channel_id=1, source_target_pairs={{0,4},{4,0},{1,5},{5,1},{2,6},{6,2},{3,7},{7,3},{8,12},{12,8},{9,1... | collective-permute-start | bytes 1105928 | tf_op jit(solution)/shard_map/ppermute | solution.py:221
  63.3 3.6 %collective-permute-start.10 = (bf16[4,4,80,640]{3,2,1,0:T(8,128)(2,1)S(1)}, bf16[4,4,80,640]{3,2,1,0:T(8,128)(2,1)S(1)}, u32[]{:S(2)}, u32[]{:S(2)}) collective-permute-start(bf16[4,4,80,640]{3,2,1,0:T(8,128)(2,1)S(1)} %get-tuple-element.42), channel_id=1, source_target_pairs={{0,4},{4,0},{1,5},{5,1},{2,6},{6,2},{3,7},{7,3},{8,12},{12,8},{9,1... | collective-permute-start | bytes 4915208 | tf_op jit(solution)/shard_map/ppermute | solution.py:221
  68.0 13.8 %collective-permute-start.13 = (bf16[4,80,640]{2,1,0:T(8,128)(2,1)}, bf16[4,80,640]{2,1,0:T(8,128)(2,1)S(1)}, u32[]{:S(2)}, u32[]{:S(2)}) collective-permute-start(bf16[4,80,640]{2,1,0:T(8,128)(2,1)} %get-tuple-element.45), channel_id=1, source_target_pairs={{0,32},{4,12},{8,40},{12,20},{16,48},{20,28},{24,56},{28,4},{32,64... | collective-permute-start | bytes 1228808 | tf_op jit(solution)/shard_map/ppermute | solution.py:549
  68.0 13.8 %collective-permute-start.14 = (bf16[4,80,640]{2,1,0:T(8,128)(2,1)S(1)}, bf16[4,80,640]{2,1,0:T(8,128)(2,1)S(1)}, u32[]{:S(2)}, u32[]{:S(2)}) collective-permute-start(bf16[4,80,640]{2,1,0:T(8,128)(2,1)S(1)} %get-tuple-element.46), channel_id=1, source_target_pairs={{0,64},{4,20},{8,72},{12,28},{16,80},{20,4},{24,88},{28,12},{32,96... | collective-permute-start | bytes 1228808 | tf_op jit(solution)/shard_map/ppermute | solution.py:549
  70.0 12.4 %collective-permute-start.15 = (bf16[4,80,640]{2,1,0:T(8,128)(2,1)S(1)}, bf16[4,80,640]{2,1,0:T(8,128)(2,1)S(1)}, u32[]{:S(2)}, u32[]{:S(2)}) collective-permute-start(bf16[4,80,640]{2,1,0:T(8,128)(2,1)S(1)} %get-tuple-element.47), channel_id=1, source_target_pairs={{0,96},{4,28},{8,104},{12,4},{16,112},{20,12},{24,120},{28,20},{32... | collective-permute-start | bytes 1228808 | tf_op jit(solution)/shard_map/ppermute | solution.py:549
  74.9 11.6 %all-to-all-start.1 = ((bf16[8,32,640]{2,1,0:T(8,128)(2,1)}), bf16[8,32,640]{2,1,0:T(8,128)(2,1)S(1)}, u32[]{:S(2)}, u32[]{:S(2)}) async-start(bf16[8,32,640]{2,1,0:T(8,128)(2,1)} %shard_map.103), calls=%async_computation.1 | async-start | bytes 655360 | tf_op jit(solution)/shard_map/all_to_all | solution.py:588
  83.0 6.6 %collective-permute-start.16 = (bf16[2,80,320]{2,1,0:T(8,128)(2,1)S(1)}, bf16[2,80,320]{2,1,0:T(8,128)(2,1)S(1)}, u32[]{:S(2)}, u32[]{:S(2)}) collective-permute-start(bf16[2,80,320]{2,1,0:T(8,128)(2,1)S(1)} %get-tuple-element.49), channel_id=1, source_target_pairs={{0,8},{4,36},{8,16},{12,44},{16,24},{20,52},{24,0},{28,60},{32,40}... | collective-permute-start | bytes 307208 | tf_op jit(solution)/shard_map/ppermute | solution.py:549
  85.1 6.5 %collective-permute-start.17 = (bf16[2,80,320]{2,1,0:T(8,128)(2,1)S(1)}, bf16[2,80,320]{2,1,0:T(8,128)(2,1)S(1)}, u32[]{:S(2)}, u32[]{:S(2)}) collective-permute-start(bf16[2,80,320]{2,1,0:T(8,128)(2,1)S(1)} %get-tuple-element.50), channel_id=1, source_target_pairs={{0,16},{4,68},{8,24},{12,76},{16,0},{20,84},{24,8},{28,92},{32,48}... | collective-permute-start | bytes 307208 | tf_op jit(solution)/shard_map/ppermute | solution.py:549
  85.9 6.9 %collective-permute-start.18 = (bf16[2,80,320]{2,1,0:T(8,128)(2,1)S(1)}, bf16[2,80,320]{2,1,0:T(8,128)(2,1)S(1)}, u32[]{:S(2)}, u32[]{:S(2)}) collective-permute-start(bf16[2,80,320]{2,1,0:T(8,128)(2,1)S(1)} %get-tuple-element.51), channel_id=1, source_target_pairs={{0,24},{4,100},{8,0},{12,108},{16,8},{20,116},{24,16},{28,124},{32... | collective-permute-start | bytes 307208 | tf_op jit(solution)/shard_map/ppermute | solution.py:549
  86.6 10.5 %collective-permute-start.12 = (bf16[1,32,640]{2,1,0:T(8,128)(2,1)S(1)}, bf16[1,32,640]{2,1,0:T(8,128)(2,1)S(1)}, u32[]{:S(2)}, u32[]{:S(2)}) collective-permute-start(bf16[1,32,640]{2,1,0:T(8,128)(2,1)S(1)} %get-tuple-element.57), channel_id=1, source_target_pairs={{0,3},{1,0},{2,1},{3,2},{4,7},{5,4},{6,5},{7,6},{8,11},{9,8},{10,9... | collective-permute-start | bytes 122888 | tf_op jit(solution)/shard_map/ppermute | solution.py:583
  87.5 9.6 %collective-permute-start.11 = (bf16[1,32,640]{2,1,0:T(8,128)(2,1)S(1)}, bf16[1,32,640]{2,1,0:T(8,128)(2,1)S(1)}, u32[]{:S(2)}, u32[]{:S(2)}) collective-permute-start(bf16[1,32,640]{2,1,0:T(8,128)(2,1)S(1)} %get-tuple-element.58), channel_id=1, source_target_pairs={{0,1},{1,2},{2,3},{3,0},{4,5},{5,6},{6,7},{7,4},{8,9},{9,10},{10,1... | collective-permute-start | bytes 122888 | tf_op jit(solution)/shard_map/ppermute | solution.py:582
  93.7 12.5 %all-to-all-start.2 = ((bf16[4,2,80,80]{3,2,1,0:T(8,128)(2,1)}), bf16[4,2,80,80]{3,2,1,0:T(8,128)(2,1)S(1)}, u32[]{:S(2)}, u32[]{:S(2)}) async-start(bf16[4,2,80,80]{3,2,1,0:T(8,128)(2,1)} %shard_map.106), calls=%async_computation.2 | async-start | bytes 327680 | tf_op jit(solution)/shard_map/all_to_all | solution.py:572
  106.3 3.9 %collective-permute-start.19 = (bf16[80,80]{1,0:T(8,128)(2,1)S(1)}, bf16[80,80]{1,0:T(8,128)(2,1)S(1)}, u32[]{:S(2)}, u32[]{:S(2)}) collective-permute-start(bf16[80,80]{1,0:T(8,128)(2,1)S(1)} %get-tuple-element.54), channel_id=1, source_target_pairs={{0,128},{128,0},{1,129},{129,1},{2,130},{130,2},{3,131},{131,3},{4... | collective-permute-start | bytes 38408 | tf_op jit(solution)/shard_map/ppermute | solution.py:576

commit v3 on v2

--- a/solution.py
+++ b/solution.py
@@ -321,33 +321,45 @@
     def merged(both):
         return jnp.where(first_head, both[:128], both[128:]).astype(BF16)
 
-    for half in range(2):
-        for pair in range(5):
-            at = pair * 128
-
-            def part(ref, offset):
-                return ref[:, half, :, offset + at : offset + at + 128].reshape(128, 128)
-
-            queries = two_heads(part(packed, 0))
-            keys = part(packed, C)
-            values = part(packed, 2 * C)
-            scores = jnp.where(same_pixel, mm_nt(queries, keys) * HEAD_DIM**-0.5, -1e30)
-            expons = jnp.exp(scores - jnp.max(scores, axis=-1, keepdims=True))
-            probs = expons * (1.0 / jnp.sum(expons, axis=-1, keepdims=True))
-            rounded = probs.astype(BF16)
-            blended[:, half, :, at : at + 128] = merged(mm(rounded, values)).reshape(8, 16, 128)
-            upper = two_heads(part(grad_blend, 0))
-            grad_probs = mm_nt(upper, values)
-            inner = jnp.sum(grad_probs * probs, axis=-1, keepdims=True)
-            grad_scores = (probs * (grad_probs - inner) * HEAD_DIM**-0.5).astype(BF16)
-            results = (
-                merged(mm(grad_scores, keys)),
-                mm_tn(grad_scores, queries).astype(BF16),
-                mm_tn(rounded, upper).astype(BF16),
-            )
-            for i, result in enumerate(results):
-                lanes = slice(i * C + at, i * C + at + 128)
-                grad_packed[:, half, :, lanes] = result.reshape(8, 16, 128)
+    blocks = [(half, pair * 128) for pair in range(5) for half in range(2)]
+
+    def parts(ref, offset):
+        return [
+            ref[:, half, :, offset + at : offset + at + 128].reshape(128, 128)
+            for half, at in blocks
+        ]
+
+    def each(function, *lists):
+        return [function(*values) for values in zip(*lists)]
+
+    def row_sum(values):
+        return jnp.sum(values, axis=-1, keepdims=True)
+
+    queries = each(two_heads, parts(packed, 0))
+    keys, values = parts(packed, C), parts(packed, 2 * C)
+    upper = each(two_heads, parts(grad_blend, 0))
+    scores = each(mm_nt, queries, keys)
+    grad_probs = each(mm_nt, upper, values)
+    scores = each(lambda s: jnp.where(same_pixel, s * HEAD_DIM**-0.5, -1e30), scores)
+    largest = each(lambda s: jnp.max(s, axis=-1, keepdims=True), scores)
+    expons = each(lambda s, top: jnp.exp(s - top), scores, largest)
+    probs = each(lambda e, total: e * (1.0 / total), expons, each(row_sum, expons))
+    rounded = each(lambda p: p.astype(BF16), probs)
+    inner = each(lambda g, p: row_sum(g * p), grad_probs, probs)
+    grad_scores = each(
+        lambda p, g, i: (p * (g - i) * HEAD_DIM**-0.5).astype(BF16), probs, grad_probs, inner
+    )
+    mixed = each(lambda p, v: merged(mm(p, v)), rounded, values)
+    results = (
+        each(lambda g, k: merged(mm(g, k)), grad_scores, keys),
+        each(lambda g, q: mm_tn(g, q).astype(BF16), grad_scores, queries),
+        each(lambda p, u: mm_tn(p, u).astype(BF16), rounded, upper),
+    )
+    for n, (half, at) in enumerate(blocks):
+        blended[:, half, :, at : at + 128] = mixed[n].reshape(8, 16, 128)
+        for i in range(3):
+            lanes = slice(i * C + at, i * C + at + 128)
+            grad_packed[:, half, :, lanes] = results[i][n].reshape(8, 16, 128)
 
     mixed_out[...] = blended[...].reshape(256, C)
     weight_gradient(1 - pos[3], normal, mixed_out, tile, grad_packed, send)

time: 111 us -> 108 us (0.973)
  Pallas kernels: 33.3 us -> 30.1 us
    pallas_call x1, Pallas kernels: 7.65 us -> 4.45 us  [attention_step(): call(attention_body, [sds((8, 2, 16, 3 * C)), sds((256, C)), sds(BLOCKS)]...]
where the time goes in v3:
time: 108 us
  starting transfers between devices  39.2 us (36%)
  waiting for transfers between devices  36.4 us (34%)
  Pallas kernels  30.1 us (28%)
  local copies, waits for them, and re-layouts  1.17 us (1%)
    all_to_all x2, starting transfers between devices, exchange(): return lax.all_to_all(rows, FRAME, split_axis=0, concat_axis=0, tiled=True)  10.2 us
    all_to_all x2, waiting for transfers between devices, exchange(): return lax.all_to_all(rows, FRAME, split_axis=0, concat_axis=0, tiled=True)  9.54 us
    ppermute x2, starting transfers between devices, edges(): high = lax.ppermute(top, 'zh', [(i, (i + 3) % 4) for i in range(4)])  7.26 us
    ppermute x6, starting transfers between devices, crosswise(): moved.append(lax.ppermute(sends[k], ('y', 'x', 'c'), pairs))  6.82 us
    pallas_call x1, Pallas kernels, conv_backward(): call(conv_backward_body, [sds((8, 32, C)), sds((8, 128), F32)], 3, 1, CON...  5.77 us
    pallas_call x1, Pallas kernels, conv_forward(): call(conv_forward_body, [sds((8, 2, 32, C))], 2, 3, CONV_SCRATCH + (pltpu...  5.47 us
    ppermute x2, waiting for transfers between devices, edges(): low = lax.ppermute(bottom, 'zh', [(i, (i + 1) % 4) for i in range(4)])  5.46 us
    ppermute x6, waiting for transfers between devices, crosswise(): moved.append(lax.ppermute(sends[k], ('y', 'x', 'c'), pairs))  5.3 us
  transfers between devices with their start and end apart: 23, of which 12 were waited for; matrix products, arithmetic and copies ran while one was open for 0% of the time, Pallas kernels for 16%

profile of v3, /device:TPU:6, one launch (start us, length us, event | category | flops | bytes accessed | tf_op | source)
XLA Modules:
  0.0 107.7 jit_solution(5126771574885745096)
XLA Ops:
  0.7 2.3 %shard_map.94 = (bf16[288,640]{1,0:T(8,128)(2,1)}, bf16[288,640]{1,0:T(8,128)(2,1)}, bf16[1,32,640]{2,1,0:T(8,128)(2,1)}, bf16[1,32,640]{2,1,0:T(8,128)(2,1)}) custom-call(bf16[240,640]{1,0:T(8,128)(2,1)} %refs_0_.1, bf16[80,1920]{1,0:T(8,128)(2,1)} %refs_1_.1, bf16[80,640]{1,0:T(8,128)(2,1)} %refs_2_.1, bf16[8,32,640]{2,1,0:T(8,128)(2,1)} %bitcast.5), custom_call_target="tpu_custom_call" | custom-call | tf_op jit(solution)/shard_map/pallas_call | solution.py:184
  2.9 6.4 %collective-permute-start.1 = (bf16[1,32,640]{2,1,0:T(8,128)(2,1)}, bf16[1,32,640]{2,1,0:T(8,128)(2,1)S(1)}, u32[]{:S(2)}, u32[]{:S(2)}) collective-permute-start(bf16[1,32,640]{2,1,0:T(8,128)(2,1)} %get-tuple-element.31), channel_id=1, source_target_pairs={{0,3},{1,0},{2,1},{3,2},{4,7},{5,4},{6,5},{7,6},{8,11},{9,8},{10,9... | collective-permute-start | bytes 122888 | tf_op jit(solution)/shard_map/ppermute | solution.py:595
  9.3 3.0 %collective-permute-start.4 = (bf16[288,640]{1,0:T(8,128)(2,1)}, bf16[288,640]{1,0:T(8,128)(2,1)S(1)}, u32[]{:S(2)}, u32[]{:S(2)}) collective-permute-start(bf16[288,640]{1,0:T(8,128)(2,1)} %get-tuple-element.32.refs_0_), channel_id=1, source_target_pairs={{0,96},{32,0},{64,32},{96,64},{1,97},{33,1},{65,33},{97,65},{2,98}... | collective-permute-start | bytes 1105928 | tf_op jit(solution)/shard_map/ppermute | solution.py:543
  12.3 0.6 collective-permute-start.3
  12.9 1.0 collective-permute-start.2
  13.9 1.3 %collective-permute-start.5 = (bf16[288,640]{1,0:T(8,128)(2,1)}, bf16[288,640]{1,0:T(8,128)(2,1)S(1)}, u32[]{:S(2)}, u32[]{:S(2)}) collective-permute-start(bf16[288,640]{1,0:T(8,128)(2,1)} %shard_map.96), channel_id=1, source_target_pairs={{0,131},{4,132},{128,0},{132,5},{1,128},{5,133},{129,1},{133,6},{2... | collective-permute-start | bytes 1105928 | tf_op jit(solution)/shard_map/ppermute | solution.py:217
  15.2 1.2 %collective-permute-start = (bf16[1,32,640]{2,1,0:T(8,128)(2,1)}, bf16[1,32,640]{2,1,0:T(8,128)(2,1)S(1)}, u32[]{:S(2)}, u32[]{:S(2)}) collective-permute-start(bf16[1,32,640]{2,1,0:T(8,128)(2,1)} %get-tuple-element.30), channel_id=1, source_target_pairs={{0,1},{1,2},{2,3},{3,0},{4,5},{5,6},{6,7},{7,4},{8,9},{9,10},{10,1... | collective-permute-start | bytes 122888 | tf_op jit(solution)/shard_map/ppermute | solution.py:594
  16.4 5.5 %collective-permute-done.refs_0_ = bf16[1,32,640]{2,1,0:T(8,128)(2,1)S(1)} collective-permute-done((bf16[1,32,640]{2,1,0:T(8,128)(2,1)}, bf16[1,32,640]{2,1,0:T(8,128)(2,1)S(1)}, u32[]{:S(2)}, u32[]{:S(2)}) %collective-permute-start) | collective-permute-done | bytes 40992 | tf_op jit(solution)/shard_map/ppermute | solution.py:594
  21.9 5.5 %shard_map.95.refs_4_ = bf16[8,2,32,640]{3,2,1,0:T(8,128)(2,1)} custom-call(bf16[1,32,640]{2,1,0:T(8,128)(2,1)S(1)} %collective-permute-done.refs_0_, bf16[1,32,640]{2,1,0:T(8,128)(2,1)S(1)} %collective-permute-done.1.refs_1_.b, bf16[8,32,640]{2,1,0:T(8,128)(2,1)S(1)} %bitcast.6, bf16[8,32,640]{2,1,0:T(8,128)(2,1)S(1)} %bitcast.7, ...), custom_call_target="tpu_custom_call" | custom-call | flops 1887436800 | bytes 7372800 | tf_op jit(solution)/shard_map/pallas_call | solution.py:126
  27.4 0.8 collective-permute-done.4.refs_3_
  28.1 3.6 %collective-permute-done.2.refs_1_ = bf16[288,640]{1,0:T(8,128)(2,1)S(1)} collective-permute-done((bf16[288,640]{1,0:T(8,128)(2,1)}, bf16[288,640]{1,0:T(8,128)(2,1)S(1)}, u32[]{:S(2)}, u32[]{:S(2)}) %collective-permute-start.2) | collective-permute-done | bytes 368672 | tf_op jit(solution)/shard_map/ppermute | solution.py:543
  31.7 0.2 shard_map.97
  31.9 1.1 %copy-done = bf16[4,288,640]{2,1,0:T(8,128)(2,1)} copy-done((bf16[4,288,640]{2,1,0:T(8,128)(2,1)}, bf16[4,288,640]{2,1,0:T(8,128)(2,1)S(1)}, u32[]{:S(2)}) %copy-start) | copy-done | bytes 1474584
  33.1 1.0 collective-permute-start.8
  34.1 4.8 %all-to-all-start = ((bf16[8,2,32,640]{3,2,1,0:T(8,128)(2,1)}), bf16[8,2,32,640]{3,2,1,0:T(8,128)(2,1)S(1)}, u32[]{:S(2)}, u32[]{:S(2)}) async-start(bf16[8,2,32,640]{3,2,1,0:T(8,128)(2,1)} %shard_map.95.refs_4_), calls=%async_computation | async-start | bytes 1310720 | tf_op jit(solution)/shard_map/all_to_all | solution.py:600
  38.9 0.1 collective-permute-start.6
  39.0 9.5 %all-to-all-done.b.refs_0_.refs_1_.refs_2_ = bf16[8,2,32,640]{3,2,1,0:T(8,128)(2,1)S(1)} async-done(((bf16[8,2,32,640]{3,2,1,0:T(8,128)(2,1)}), bf16[8,2,32,640]{3,2,1,0:T(8,128)(2,1)S(1)}, u32[]{:S(2)}, u32[]{:S(2)}) %all-to-all-start) | async-done | bytes 655392 | tf_op jit(solution)/shard_map/all_to_all | solution.py:600
  48.6 0.1 collective-permute-start.9
  48.7 0.4 collective-permute-start.7
  49.1 2.8 %collective-permute-done.7.refs_5_ = bf16[288,640]{1,0:T(8,128)(2,1)S(1)} collective-permute-done((bf16[288,640]{1,0:T(8,128)(2,1)S(1)}, bf16[288,640]{1,0:T(8,128)(2,1)S(1)}, u32[]{:S(2)}, u32[]{:S(2)}) %collective-permute-start.7) | collective-permute-done | bytes 368672 | tf_op jit(solution)/shard_map/ppermute | solution.py:221
  51.8 3.8 %shard_map.99 = (bf16[256,640]{1,0:T(8,128)(2,1)S(1)}, bf16[256,640]{1,0:T(8,128)(2,1)S(1)}, bf16[8,240,640]{2,1,0:T(8,128)(2,1)S(1)}, bf16[8,80,2560]{2,1,0:T(8,128)(2,1)S(1)}) custom-call(bf16[8,2,32,640]{3,2,1,0:T(8,128)(2,1)S(1)} %all-to-all-done.b.refs_0_.refs_1_.refs_2_, f32[1,640]{1,0:T(1,128)S(1)} %reshape.9.refs_1_.refs_3_, ...), custom_call_target="tpu_custom_call" | custom-call | flops 629145600 | bytes 2457600 | tf_op jit(solution)/shard_map/pallas_call | solution.py:293
  55.7 4.4 %shard_map.100 = (bf16[8,2,16,1920]{3,2,1,0:T(8,128)(2,1)S(1)}, bf16[256,640]{1,0:T(8,128)(2,1)S(1)}, bf16[4,4,80,640]{3,2,1,0:T(8,128)(2,1)S(1)}) custom-call(bf16[256,640]{1,0:T(8,128)(2,1)S(1)} %get-tuple-element.36.refs_0_, bf16[8,2,32,640]{3,2,1,0:T(8,128)(2,1)S(1)} %all-to-all-done.b.refs_0_.refs_1_.refs_2_, ...), custom_call_target="tpu_custom_call" | custom-call | flops 1677721600 | bytes 3276800 | tf_op jit(solution)/shard_map/pallas_call | solution.py:433
  60.1 0.1 collective-permute-start.10
  60.2 1.1 %shard_map.101.refs_0_ = bf16[4,4,80,640]{3,2,1,0:T(8,128)(2,1)S(1)} custom-call(bf16[256,640]{1,0:T(8,128)(2,1)S(1)} %get-tuple-element.36.refs_0_, bf16[256,640]{1,0:T(8,128)(2,1)S(1)} %get-tuple-element.41.refs_1_, bf16[8,2,32,640]{3,2,1,0:T(8,128)(2,1)S(1)} %all-to-all-done.b.refs_0_.refs_1_.refs_2_, ...), custom_call_target="tpu_custom_call" | custom-call | flops 419430400 | bytes 1638400 | tf_op jit(solution)/shard_map/pallas_call | solution.py:421
  61.4 2.4 %collective-permute-done.10.refs_1_ = bf16[4,4,80,640]{3,2,1,0:T(8,128)(2,1)S(1)} collective-permute-done((bf16[4,4,80,640]{3,2,1,0:T(8,128)(2,1)S(1)}, bf16[4,4,80,640]{3,2,1,0:T(8,128)(2,1)S(1)}, u32[]{:S(2)}, u32[]{:S(2)}) %collective-permute-start.10) | collective-permute-done | bytes 1638432 | tf_op jit(solution)/shard_map/ppermute | solution.py:221
  63.7 1.0 shard_map.102
  64.8 2.1 %collective-permute-start.14 = (bf16[4,80,640]{2,1,0:T(8,128)(2,1)S(1)}, bf16[4,80,640]{2,1,0:T(8,128)(2,1)S(1)}, u32[]{:S(2)}, u32[]{:S(2)}) collective-permute-start(bf16[4,80,640]{2,1,0:T(8,128)(2,1)S(1)} %get-tuple-element.46), channel_id=1, source_target_pairs={{0,64},{4,20},{8,72},{12,28},{16,80},{20,4},{24,88},{28,12},{32,96... | collective-permute-start | bytes 1228808 | tf_op jit(solution)/shard_map/ppermute | solution.py:561
  66.8 1.2 %collective-permute-start.15 = (bf16[4,80,640]{2,1,0:T(8,128)(2,1)S(1)}, bf16[4,80,640]{2,1,0:T(8,128)(2,1)S(1)}, u32[]{:S(2)}, u32[]{:S(2)}) collective-permute-start(bf16[4,80,640]{2,1,0:T(8,128)(2,1)S(1)} %get-tuple-element.47), channel_id=1, source_target_pairs={{0,96},{4,28},{8,104},{12,4},{16,112},{20,12},{24,120},{28,20},{32... | collective-permute-start | bytes 1228808 | tf_op jit(solution)/shard_map/ppermute | solution.py:561
  68.0 3.7 %shard_map.103 = bf16[8,32,640]{2,1,0:T(8,128)(2,1)} custom-call(bf16[8,2,16,1920]{3,2,1,0:T(8,128)(2,1)S(1)} %get-tuple-element.38.refs_3_.refs_0_, bf16[256,640]{1,0:T(8,128)(2,1)S(1)} %get-tuple-element.39.refs_1_, bf16[8,2,32,640]{3,2,1,0:T(8,128)(2,1)S(1)} %all-to-all-done.b.refs_0_.refs_1_.refs_2_, f32[1,640]{1,0:T(1,128)S(1)} %reshape.9.refs_1_.refs_3_, ...), custom_call_target="tpu_custom_call" | custom-call | flops 1258291200 | bytes 5734400 | tf_op jit(solution)/shard_map/pallas_call | solution.py:476
  71.7 5.4 %all-to-all-start.1 = ((bf16[8,32,640]{2,1,0:T(8,128)(2,1)}), bf16[8,32,640]{2,1,0:T(8,128)(2,1)S(1)}, u32[]{:S(2)}, u32[]{:S(2)}) async-start(bf16[8,32,640]{2,1,0:T(8,128)(2,1)} %shard_map.103), calls=%async_computation.1 | async-start | bytes 655360 | tf_op jit(solution)/shard_map/all_to_all | solution.py:600
  77.1 1.4 %collective-permute-done.13.refs_1_ = bf16[4,80,640]{2,1,0:T(8,128)(2,1)S(1)} collective-permute-done((bf16[4,80,640]{2,1,0:T(8,128)(2,1)}, bf16[4,80,640]{2,1,0:T(8,128)(2,1)S(1)}, u32[]{:S(2)}, u32[]{:S(2)}) %collective-permute-start.13) | collective-permute-done | bytes 409632 | tf_op jit(solution)/shard_map/ppermute | solution.py:561
  78.5 0.7 collective-permute-done.15.refs_3_
  79.2 0.6 shard_map.105
  79.8 2.1 %collective-permute-start.16 = (bf16[2,80,320]{2,1,0:T(8,128)(2,1)S(1)}, bf16[2,80,320]{2,1,0:T(8,128)(2,1)S(1)}, u32[]{:S(2)}, u32[]{:S(2)}) collective-permute-start(bf16[2,80,320]{2,1,0:T(8,128)(2,1)S(1)} %get-tuple-element.49), channel_id=1, source_target_pairs={{0,8},{4,36},{8,16},{12,44},{16,24},{20,52},{24,0},{28,60},{32,40}... | collective-permute-start | bytes 307208 | tf_op jit(solution)/shard_map/ppermute | solution.py:561
  81.9 0.8 collective-permute-start.17
  82.7 0.7 collective-permute-start.18
  83.4 0.9 collective-permute-start.12
  84.2 2.1 %collective-permute-start.11 = (bf16[1,32,640]{2,1,0:T(8,128)(2,1)S(1)}, bf16[1,32,640]{2,1,0:T(8,128)(2,1)S(1)}, u32[]{:S(2)}, u32[]{:S(2)}) collective-permute-start(bf16[1,32,640]{2,1,0:T(8,128)(2,1)S(1)} %get-tuple-element.58), channel_id=1, source_target_pairs={{0,1},{1,2},{2,3},{3,0},{4,5},{5,6},{6,7},{7,4},{8,9},{9,10},{10,1... | collective-permute-start | bytes 122888 | tf_op jit(solution)/shard_map/ppermute | solution.py:594
  86.4 2.0 %collective-permute-done.17.refs_2_ = bf16[2,80,320]{2,1,0:T(8,128)(2,1)S(1)} collective-permute-done((bf16[2,80,320]{2,1,0:T(8,128)(2,1)S(1)}, bf16[2,80,320]{2,1,0:T(8,128)(2,1)S(1)}, u32[]{:S(2)}, u32[]{:S(2)}) %collective-permute-start.17) | collective-permute-done | bytes 102432 | tf_op jit(solution)/shard_map/ppermute | solution.py:561
  88.4 1.2 %collective-permute-done.18.refs_3_ = bf16[2,80,320]{2,1,0:T(8,128)(2,1)S(1)} collective-permute-done((bf16[2,80,320]{2,1,0:T(8,128)(2,1)S(1)}, bf16[2,80,320]{2,1,0:T(8,128)(2,1)S(1)}, u32[]{:S(2)}, u32[]{:S(2)}) %collective-permute-start.18) | collective-permute-done | bytes 102432 | tf_op jit(solution)/shard_map/ppermute | solution.py:561
  89.6 0.9 shard_map.106
  90.5 3.3 %all-to-all-start.2 = ((bf16[4,2,80,80]{3,2,1,0:T(8,128)(2,1)}), bf16[4,2,80,80]{3,2,1,0:T(8,128)(2,1)S(1)}, u32[]{:S(2)}, u32[]{:S(2)}) async-start(bf16[4,2,80,80]{3,2,1,0:T(8,128)(2,1)} %shard_map.106), calls=%async_computation.2 | async-start | bytes 327680 | tf_op jit(solution)/shard_map/all_to_all | solution.py:584
  93.9 5.8 %shard_map.104 = (bf16[8,32,640]{2,1,0:T(8,128)(2,1)}, f32[8,128]{1,0:T(8,128)S(1)}) custom-call(bf16[8,32,640]{2,1,0:T(8,128)(2,1)S(1)} %all-to-all-done.1.refs_0_, bf16[1,32,640]{2,1,0:T(8,128)(2,1)S(1)} %collective-permute-done.11.refs_1_, bf16[1,32,640]{2,1,0:T(8,128)(2,1)S(1)} %collective-permute-done.12.refs_2_, bf16[3,3,640,640]{3,2,1,0:T(8,128)(2,1)} %refs_3_.1), custom_call_target="tpu_custom_call" | custom-call | flops 1887436800 | bytes 7372800 | tf_op jit(solution)/shard_map/pallas_call | solution.py:144
  99.7 3.4 %all-to-all-done.2.refs_0_ = bf16[4,2,80,80]{3,2,1,0:T(8,128)(2,1)S(1)} async-done(((bf16[4,2,80,80]{3,2,1,0:T(8,128)(2,1)}), bf16[4,2,80,80]{3,2,1,0:T(8,128)(2,1)S(1)}, u32[]{:S(2)}, u32[]{:S(2)}) %all-to-all-start.2) | async-done | bytes 102432 | tf_op jit(solution)/shard_map/all_to_all | solution.py:584
  103.0 0.1 shard_map.107
  103.1 0.6 collective-permute-start.19
  103.7 3.3 %collective-permute-done.19.refs_1_ = bf16[80,80]{1,0:T(8,128)(2,1)S(1)} collective-permute-done((bf16[80,80]{1,0:T(8,128)(2,1)S(1)}, bf16[80,80]{1,0:T(8,128)(2,1)S(1)}, u32[]{:S(2)}, u32[]{:S(2)}) %collective-permute-start.19) | collective-permute-done | bytes 12832 | tf_op jit(solution)/shard_map/ppermute | solution.py:588
  107.0 0.7 shard_map.108
  (27 shorter events, 0.1 us)
Async XLA Ops:
  0.6 21.2 %copy-start.2 = (bf16[1,1,8,32,640]{4,3,2,1,0:T(8,128)(2,1)S(1)}, bf16[1,1,8,32,640]{4,3,2,1,0:T(8,128)(2,1)}, u32[]{:S(2)}) copy-start(bf16[1,1,8,32,640]{4,3,2,1,0:T(8,128)(2,1)} %param.7) | copy-start | bytes 983044
  0.6 21.2 %copy-start.4 = (bf16[1,1,8,32,640]{4,3,2,1,0:T(8,128)(2,1)S(1)}, bf16[1,1,8,32,640]{4,3,2,1,0:T(8,128)(2,1)}, u32[]{:S(2)}) copy-start(bf16[1,1,8,32,640]{4,3,2,1,0:T(8,128)(2,1)} %param.13) | copy-start | bytes 983044
  2.9 11.0 %collective-permute-start.1 = (bf16[1,32,640]{2,1,0:T(8,128)(2,1)}, bf16[1,32,640]{2,1,0:T(8,128)(2,1)S(1)}, u32[]{:S(2)}, u32[]{:S(2)}) collective-permute-start(bf16[1,32,640]{2,1,0:T(8,128)(2,1)} %get-tuple-element.31), channel_id=1, source_target_pairs={{0,3},{1,0},{2,1},{3,2},{4,7},{5,4},{6,5},{7,6},{8,11},{9,8},{10,9... | collective-permute-start | bytes 122888 | tf_op jit(solution)/shard_map/ppermute | solution.py:595
  9.3 18.8 %collective-permute-start.4 = (bf16[288,640]{1,0:T(8,128)(2,1)}, bf16[288,640]{1,0:T(8,128)(2,1)S(1)}, u32[]{:S(2)}, u32[]{:S(2)}) collective-permute-start(bf16[288,640]{1,0:T(8,128)(2,1)} %get-tuple-element.32.refs_0_), channel_id=1, source_target_pairs={{0,96},{32,0},{64,32},{96,64},{1,97},{33,1},{65,33},{97,65},{2,98}... | collective-permute-start | bytes 1105928 | tf_op jit(solution)/shard_map/ppermute | solution.py:543
  12.3 15.8 %collective-permute-start.3 = (bf16[288,640]{1,0:T(8,128)(2,1)}, bf16[288,640]{1,0:T(8,128)(2,1)S(1)}, u32[]{:S(2)}, u32[]{:S(2)}) collective-permute-start(bf16[288,640]{1,0:T(8,128)(2,1)} %get-tuple-element.32.refs_0_), channel_id=1, source_target_pairs={{0,64},{32,96},{64,0},{96,32},{1,65},{33,97},{65,1},{97,33},{2,66}... | collective-permute-start | bytes 1105928 | tf_op jit(solution)/shard_map/ppermute | solution.py:543
  12.9 18.8 %collective-permute-start.2 = (bf16[288,640]{1,0:T(8,128)(2,1)}, bf16[288,640]{1,0:T(8,128)(2,1)S(1)}, u32[]{:S(2)}, u32[]{:S(2)}) collective-permute-start(bf16[288,640]{1,0:T(8,128)(2,1)} %get-tuple-element.32.refs_0_), channel_id=1, source_target_pairs={{0,32},{32,64},{64,96},{96,0},{1,33},{33,65},{65,97},{97,1},{2,34}... | collective-permute-start | bytes 1105928 | tf_op jit(solution)/shard_map/ppermute | solution.py:543
  13.9 17.8 %collective-permute-start.5 = (bf16[288,640]{1,0:T(8,128)(2,1)}, bf16[288,640]{1,0:T(8,128)(2,1)S(1)}, u32[]{:S(2)}, u32[]{:S(2)}) collective-permute-start(bf16[288,640]{1,0:T(8,128)(2,1)} %shard_map.96), channel_id=1, source_target_pairs={{0,131},{4,132},{128,0},{132,5},{1,128},{5,133},{129,1},{133,6},{2... | collective-permute-start | bytes 1105928 | tf_op jit(solution)/shard_map/ppermute | solution.py:217
  15.2 6.7 %collective-permute-start = (bf16[1,32,640]{2,1,0:T(8,128)(2,1)}, bf16[1,32,640]{2,1,0:T(8,128)(2,1)S(1)}, u32[]{:S(2)}, u32[]{:S(2)}) collective-permute-start(bf16[1,32,640]{2,1,0:T(8,128)(2,1)} %get-tuple-element.30), channel_id=1, source_target_pairs={{0,1},{1,2},{2,3},{3,0},{4,5},{5,6},{6,7},{7,4},{8,9},{9,10},{10,1... | collective-permute-start | bytes 122888 | tf_op jit(solution)/shard_map/ppermute | solution.py:594
  21.9 9.8 %copy-start.3 = (bf16[288,640]{1,0:T(8,128)(2,1)S(1)}, bf16[288,640]{1,0:T(8,128)(2,1)}, u32[]{:S(2)}) copy-start(bf16[288,640]{1,0:T(8,128)(2,1)} %get-tuple-element.32.refs_0_) | copy-start | bytes 1105924
  31.9 1.1 %copy-start = (bf16[4,288,640]{2,1,0:T(8,128)(2,1)}, bf16[4,288,640]{2,1,0:T(8,128)(2,1)S(1)}, u32[]{:S(2)}) copy-start(bf16[4,288,640]{2,1,0:T(8,128)(2,1)S(1)} %get-tuple-element.34.refs_2_) | copy-start | bytes 4423684
  33.1 15.5 %collective-permute-start.8 = (bf16[3,288,640]{2,1,0:T(8,128)(2,1)S(1)}, bf16[3,288,640]{2,1,0:T(8,128)(2,1)S(1)}, u32[]{:S(2)}, u32[]{:S(2)}) collective-permute-start(bf16[3,288,640]{2,1,0:T(8,128)(2,1)S(1)} %get-tuple-element.35), channel_id=1, source_target_pairs={{0,131},{4,132},{128,0},{132,5},{1,128},{5,133},{129,1},{133,6},{2... | collective-permute-start | bytes 3317768 | tf_op jit(solution)/shard_map/ppermute | solution.py:217
  34.1 14.5 %all-to-all-start = ((bf16[8,2,32,640]{3,2,1,0:T(8,128)(2,1)}), bf16[8,2,32,640]{3,2,1,0:T(8,128)(2,1)S(1)}, u32[]{:S(2)}, u32[]{:S(2)}) async-start(bf16[8,2,32,640]{3,2,1,0:T(8,128)(2,1)} %shard_map.95.refs_4_), calls=%async_computation | async-start | bytes 1310720 | tf_op jit(solution)/shard_map/all_to_all | solution.py:600
  38.9 10.2 %copy-start.5 = (f32[640]{0:T(1024)S(1)}, f32[640]{0:T(1024)}, u32[]{:S(2)}) copy-start(f32[640]{0:T(1024)} %param.12) | copy-start | bytes 7684
  38.9 13.0 %collective-permute-start.6 = (bf16[4,288,640]{2,1,0:T(8,128)(2,1)}, bf16[4,288,640]{2,1,0:T(8,128)(2,1)}, u32[]{:S(2)}, u32[]{:S(2)}) collective-permute-start(bf16[4,288,640]{2,1,0:T(8,128)(2,1)} %copy-done), channel_id=1, source_target_pairs={{0,4},{4,0},{1,5},{5,1},{2,6},{6,2},{3,7},{7,3},{8,12},{12,8},{9,1... | collective-permute-start | bytes 4423688 | tf_op jit(solution)/shard_map/ppermute | solution.py:221
  48.6 3.3 %copy-start.1 = (bf16[4,288,640]{2,1,0:T(8,128)(2,1)S(1)}, bf16[4,288,640]{2,1,0:T(8,128)(2,1)}, u32[]{:S(2)}) copy-start(bf16[4,288,640]{2,1,0:T(8,128)(2,1)} %copy-done) | copy-start | bytes 4423684
  48.6 3.3 %collective-permute-start.9 = (bf16[3,288,640]{2,1,0:T(8,128)(2,1)S(1)}, bf16[3,288,640]{2,1,0:T(8,128)(2,1)S(1)}, u32[]{:S(2)}, u32[]{:S(2)}) collective-permute-start(bf16[3,288,640]{2,1,0:T(8,128)(2,1)S(1)} %shard_map.98.refs_6_), channel_id=1, source_target_pairs={{0,4},{4,0},{1,5},{5,1},{2,6},{6,2},{3,7},{7,3},{8,12},{12,8},{9,1... | collective-permute-start | bytes 3317768 | tf_op jit(solution)/shard_map/ppermute | solution.py:221
  48.7 3.2 %collective-permute-start.7 = (bf16[288,640]{1,0:T(8,128)(2,1)S(1)}, bf16[288,640]{1,0:T(8,128)(2,1)S(1)}, u32[]{:S(2)}, u32[]{:S(2)}) collective-permute-start(bf16[288,640]{1,0:T(8,128)(2,1)S(1)} %collective-permute-done.5.refs_5_.refs_4_), channel_id=1, source_target_pairs={{0,4},{4,0},{1,5},{5,1},{2,6},{6,2},{3,7},{7,3},{8,12},{12,8},{9,1... | collective-permute-start | bytes 1105928 | tf_op jit(solution)/shard_map/ppermute | solution.py:221
  60.1 3.6 %collective-permute-start.10 = (bf16[4,4,80,640]{3,2,1,0:T(8,128)(2,1)S(1)}, bf16[4,4,80,640]{3,2,1,0:T(8,128)(2,1)S(1)}, u32[]{:S(2)}, u32[]{:S(2)}) collective-permute-start(bf16[4,4,80,640]{3,2,1,0:T(8,128)(2,1)S(1)} %get-tuple-element.42), channel_id=1, source_target_pairs={{0,4},{4,0},{1,5},{5,1},{2,6},{6,2},{3,7},{7,3},{8,12},{12,8},{9,1... | collective-permute-start | bytes 4915208 | tf_op jit(solution)/shard_map/ppermute | solution.py:221
  64.8 13.8 %collective-permute-start.13 = (bf16[4,80,640]{2,1,0:T(8,128)(2,1)}, bf16[4,80,640]{2,1,0:T(8,128)(2,1)S(1)}, u32[]{:S(2)}, u32[]{:S(2)}) collective-permute-start(bf16[4,80,640]{2,1,0:T(8,128)(2,1)} %get-tuple-element.45), channel_id=1, source_target_pairs={{0,32},{4,12},{8,40},{12,20},{16,48},{20,28},{24,56},{28,4},{32,64... | collective-permute-start | bytes 1228808 | tf_op jit(solution)/shard_map/ppermute | solution.py:561
  64.8 13.8 %collective-permute-start.14 = (bf16[4,80,640]{2,1,0:T(8,128)(2,1)S(1)}, bf16[4,80,640]{2,1,0:T(8,128)(2,1)S(1)}, u32[]{:S(2)}, u32[]{:S(2)}) collective-permute-start(bf16[4,80,640]{2,1,0:T(8,128)(2,1)S(1)} %get-tuple-element.46), channel_id=1, source_target_pairs={{0,64},{4,20},{8,72},{12,28},{16,80},{20,4},{24,88},{28,12},{32,96... | collective-permute-start | bytes 1228808 | tf_op jit(solution)/shard_map/ppermute | solution.py:561
  66.8 12.4 %collective-permute-start.15 = (bf16[4,80,640]{2,1,0:T(8,128)(2,1)S(1)}, bf16[4,80,640]{2,1,0:T(8,128)(2,1)S(1)}, u32[]{:S(2)}, u32[]{:S(2)}) collective-permute-start(bf16[4,80,640]{2,1,0:T(8,128)(2,1)S(1)} %get-tuple-element.47), channel_id=1, source_target_pairs={{0,96},{4,28},{8,104},{12,4},{16,112},{20,12},{24,120},{28,20},{32... | collective-permute-start | bytes 1228808 | tf_op jit(solution)/shard_map/ppermute | solution.py:561
  71.7 11.6 %all-to-all-start.1 = ((bf16[8,32,640]{2,1,0:T(8,128)(2,1)}), bf16[8,32,640]{2,1,0:T(8,128)(2,1)S(1)}, u32[]{:S(2)}, u32[]{:S(2)}) async-start(bf16[8,32,640]{2,1,0:T(8,128)(2,1)} %shard_map.103), calls=%async_computation.1 | async-start | bytes 655360 | tf_op jit(solution)/shard_map/all_to_all | solution.py:600
  79.8 6.6 %collective-permute-start.16 = (bf16[2,80,320]{2,1,0:T(8,128)(2,1)S(1)}, bf16[2,80,320]{2,1,0:T(8,128)(2,1)S(1)}, u32[]{:S(2)}, u32[]{:S(2)}) collective-permute-start(bf16[2,80,320]{2,1,0:T(8,128)(2,1)S(1)} %get-tuple-element.49), channel_id=1, source_target_pairs={{0,8},{4,36},{8,16},{12,44},{16,24},{20,52},{24,0},{28,60},{32,40}... | collective-permute-start | bytes 307208 | tf_op jit(solution)/shard_map/ppermute | solution.py:561
  81.9 6.5 %collective-permute-start.17 = (bf16[2,80,320]{2,1,0:T(8,128)(2,1)S(1)}, bf16[2,80,320]{2,1,0:T(8,128)(2,1)S(1)}, u32[]{:S(2)}, u32[]{:S(2)}) collective-permute-start(bf16[2,80,320]{2,1,0:T(8,128)(2,1)S(1)} %get-tuple-element.50), channel_id=1, source_target_pairs={{0,16},{4,68},{8,24},{12,76},{16,0},{20,84},{24,8},{28,92},{32,48}... | collective-permute-start | bytes 307208 | tf_op jit(solution)/shard_map/ppermute | solution.py:561
  82.7 6.9 %collective-permute-start.18 = (bf16[2,80,320]{2,1,0:T(8,128)(2,1)S(1)}, bf16[2,80,320]{2,1,0:T(8,128)(2,1)S(1)}, u32[]{:S(2)}, u32[]{:S(2)}) collective-permute-start(bf16[2,80,320]{2,1,0:T(8,128)(2,1)S(1)} %get-tuple-element.51), channel_id=1, source_target_pairs={{0,24},{4,100},{8,0},{12,108},{16,8},{20,116},{24,16},{28,124},{32... | collective-permute-start | bytes 307208 | tf_op jit(solution)/shard_map/ppermute | solution.py:561
  83.4 10.5 %collective-permute-start.12 = (bf16[1,32,640]{2,1,0:T(8,128)(2,1)S(1)}, bf16[1,32,640]{2,1,0:T(8,128)(2,1)S(1)}, u32[]{:S(2)}, u32[]{:S(2)}) collective-permute-start(bf16[1,32,640]{2,1,0:T(8,128)(2,1)S(1)} %get-tuple-element.57), channel_id=1, source_target_pairs={{0,3},{1,0},{2,1},{3,2},{4,7},{5,4},{6,5},{7,6},{8,11},{9,8},{10,9... | collective-permute-start | bytes 122888 | tf_op jit(solution)/shard_map/ppermute | solution.py:595
  84.2 9.6 %collective-permute-start.11 = (bf16[1,32,640]{2,1,0:T(8,128)(2,1)S(1)}, bf16[1,32,640]{2,1,0:T(8,128)(2,1)S(1)}, u32[]{:S(2)}, u32[]{:S(2)}) collective-permute-start(bf16[1,32,640]{2,1,0:T(8,128)(2,1)S(1)} %get-tuple-element.58), channel_id=1, source_target_pairs={{0,1},{1,2},{2,3},{3,0},{4,5},{5,6},{6,7},{7,4},{8,9},{9,10},{10,1... | collective-permute-start | bytes 122888 | tf_op jit(solution)/shard_map/ppermute | solution.py:594
  90.5 12.5 %all-to-all-start.2 = ((bf16[4,2,80,80]{3,2,1,0:T(8,128)(2,1)}), bf16[4,2,80,80]{3,2,1,0:T(8,128)(2,1)S(1)}, u32[]{:S(2)}, u32[]{:S(2)}) async-start(bf16[4,2,80,80]{3,2,1,0:T(8,128)(2,1)} %shard_map.106), calls=%async_computation.2 | async-start | bytes 327680 | tf_op jit(solution)/shard_map/all_to_all | solution.py:584
  103.1 3.9 %collective-permute-start.19 = (bf16[80,80]{1,0:T(8,128)(2,1)S(1)}, bf16[80,80]{1,0:T(8,128)(2,1)S(1)}, u32[]{:S(2)}, u32[]{:S(2)}) collective-permute-start(bf16[80,80]{1,0:T(8,128)(2,1)S(1)} %get-tuple-element.54), channel_id=1, source_target_pairs={{0,128},{128,0},{1,129},{129,1},{2,130},{130,2},{3,131},{131,3},{4... | collective-permute-start | bytes 38408 | tf_op jit(solution)/shard_map/ppermute | solution.py:588

commit v4 on v3

--- a/solution.py
+++ b/solution.py
@@ -195,17 +195,30 @@
     )(value, after)
 
 
-def four_body(pos, own, *refs):
-    others, four, three = refs[:3], refs[-2], refs[-1]
-    four[pos[1]] = own[...]
-    for k in range(3):
-        four[(pos[1] + 3 - k) % 4] = others[k][...]
-        three[k] = others[k][...]
+def four_body(own, first, second, third, *refs):
+    four, three, sems = refs[-3:]
+    y = lax.axis_index("y")
+    copies = [pltpu.make_async_copy(own, four.at[y], sems.at[3])]
+    for k, other in enumerate((first, second, third)):
+        copies.append(pltpu.make_async_copy(other, four.at[(y + 3 - k) % 4], sems.at[k]))
+    for copy in copies:
+        copy.start()
+    for k, other in enumerate((first, second, third)):
+        three[k] = other[...]
+    for copy in copies:
+        copy.wait()
 
 
 def four_of(own, others, *after):
-    outs = [sds((4,) + own.shape), sds((3,) + own.shape)]
-    return call(four_body, outs, 4, len(after))(own, *others, *after)
+    vmem, anywhere = pl.BlockSpec(memory_space=pltpu.VMEM), pl.BlockSpec(memory_space=pl.ANY)
+    return pl.pallas_call(
+        four_body,
+        out_shape=[sds((4,) + own.shape), sds((3,) + own.shape)],
+        in_specs=[vmem] * 4 + [anywhere] * len(after),
+        out_specs=[pl.BlockSpec(memory_space=pltpu.HBM), vmem],
+        scratch_shapes=[pltpu.SemaphoreType.DMA((4,))],
+        compiler_params=pltpu.CompilerParams(vmem_limit_bytes=12 * MIB),
+    )(own, *others, *after)
 
 
 def across(own):

time: 108 us -> 109 us (level)
  no operation moved by 1% of the time
where the time goes in v4:
time: 109 us; the launch traced here: 108 us
  starting transfers between devices  39.3 us (36%)
  waiting for transfers between devices  36.4 us (33%)
  Pallas kernels  30.6 us (28%)
  local copies, waits for them, and re-layouts  1.17 us (1%)
    all_to_all x2, starting transfers between devices, exchange(): return lax.all_to_all(rows, FRAME, split_axis=0, concat_axis=0, tiled=True)  10.2 us
    all_to_all x2, waiting for transfers between devices, exchange(): return lax.all_to_all(rows, FRAME, split_axis=0, concat_axis=0, tiled=True)  9.54 us
    ppermute x2, starting transfers between devices, edges(): high = lax.ppermute(top, 'zh', [(i, (i + 3) % 4) for i in range(4)])  7.26 us
    ppermute x6, starting transfers between devices, crosswise(): moved.append(lax.ppermute(sends[k], ('y', 'x', 'c'), pairs))  6.84 us
    pallas_call x1, Pallas kernels, conv_backward(): call(conv_backward_body, [sds((8, 32, C)), sds((8, 128), F32)], 3, 1, CON...  5.77 us
    pallas_call x1, Pallas kernels, conv_forward(): call(conv_forward_body, [sds((8, 2, 32, C))], 2, 3, CONV_SCRATCH + (pltpu...  5.47 us
    ppermute x2, waiting for transfers between devices, edges(): low = lax.ppermute(bottom, 'zh', [(i, (i + 1) % 4) for i in range(4)])  5.46 us
    ppermute x6, waiting for transfers between devices, crosswise(): moved.append(lax.ppermute(sends[k], ('y', 'x', 'c'), pairs))  5.28 us
  transfers between devices with their start and end apart: 23, of which 12 were waited for; matrix products, arithmetic and copies ran while one was open for 0% of the time, Pallas kernels for 16%

profile of v4, /device:TPU:6, one launch (start us, length us, event | category | flops | bytes accessed | tf_op | source)
XLA Modules:
  0.0 108.2 jit_solution(8395631108991148572)
XLA Ops:
  0.7 2.3 %shard_map.94 = (bf16[288,640]{1,0:T(8,128)(2,1)}, bf16[288,640]{1,0:T(8,128)(2,1)}, bf16[1,32,640]{2,1,0:T(8,128)(2,1)}, bf16[1,32,640]{2,1,0:T(8,128)(2,1)}) custom-call(bf16[240,640]{1,0:T(8,128)(2,1)} %refs_0_.1, bf16[80,1920]{1,0:T(8,128)(2,1)} %refs_1_.1, bf16[80,640]{1,0:T(8,128)(2,1)} %refs_2_.1, bf16[8,32,640]{2,1,0:T(8,128)(2,1)} %bitcast.5), custom_call_target="tpu_custom_call" | custom-call | tf_op jit(solution)/shard_map/pallas_call | solution.py:184
  2.9 6.4 %collective-permute-start.1 = (bf16[1,32,640]{2,1,0:T(8,128)(2,1)}, bf16[1,32,640]{2,1,0:T(8,128)(2,1)S(1)}, u32[]{:S(2)}, u32[]{:S(2)}) collective-permute-start(bf16[1,32,640]{2,1,0:T(8,128)(2,1)} %get-tuple-element.31), channel_id=1, source_target_pairs={{0,3},{1,0},{2,1},{3,2},{4,7},{5,4},{6,5},{7,6},{8,11},{9,8},{10,9... | collective-permute-start | bytes 122888 | tf_op jit(solution)/shard_map/ppermute | solution.py:608
  9.3 3.0 %collective-permute-start.4 = (bf16[288,640]{1,0:T(8,128)(2,1)}, bf16[288,640]{1,0:T(8,128)(2,1)S(1)}, u32[]{:S(2)}, u32[]{:S(2)}) collective-permute-start(bf16[288,640]{1,0:T(8,128)(2,1)} %get-tuple-element.32.own), channel_id=1, source_target_pairs={{0,96},{32,0},{64,32},{96,64},{1,97},{33,1},{65,33},{97,65},{2,98}... | collective-permute-start | bytes 1105928 | tf_op jit(solution)/shard_map/ppermute | solution.py:556
  12.3 0.6 collective-permute-start.3
  12.9 1.0 collective-permute-start.2
  13.9 1.3 %collective-permute-start.5 = (bf16[288,640]{1,0:T(8,128)(2,1)}, bf16[288,640]{1,0:T(8,128)(2,1)S(1)}, u32[]{:S(2)}, u32[]{:S(2)}) collective-permute-start(bf16[288,640]{1,0:T(8,128)(2,1)} %shard_map.96), channel_id=1, source_target_pairs={{0,131},{4,132},{128,0},{132,5},{1,128},{5,133},{129,1},{133,6},{2... | collective-permute-start | bytes 1105928 | tf_op jit(solution)/shard_map/ppermute | solution.py:230
  15.2 1.2 %collective-permute-start = (bf16[1,32,640]{2,1,0:T(8,128)(2,1)}, bf16[1,32,640]{2,1,0:T(8,128)(2,1)S(1)}, u32[]{:S(2)}, u32[]{:S(2)}) collective-permute-start(bf16[1,32,640]{2,1,0:T(8,128)(2,1)} %get-tuple-element.30), channel_id=1, source_target_pairs={{0,1},{1,2},{2,3},{3,0},{4,5},{5,6},{6,7},{7,4},{8,9},{9,10},{10,1... | collective-permute-start | bytes 122888 | tf_op jit(solution)/shard_map/ppermute | solution.py:607
  16.4 5.5 %collective-permute-done.refs_0_ = bf16[1,32,640]{2,1,0:T(8,128)(2,1)S(1)} collective-permute-done((bf16[1,32,640]{2,1,0:T(8,128)(2,1)}, bf16[1,32,640]{2,1,0:T(8,128)(2,1)S(1)}, u32[]{:S(2)}, u32[]{:S(2)}) %collective-permute-start) | collective-permute-done | bytes 40992 | tf_op jit(solution)/shard_map/ppermute | solution.py:607
  21.9 5.5 %shard_map.95.refs_0_ = bf16[8,2,32,640]{3,2,1,0:T(8,128)(2,1)} custom-call(bf16[1,32,640]{2,1,0:T(8,128)(2,1)S(1)} %collective-permute-done.refs_0_, bf16[1,32,640]{2,1,0:T(8,128)(2,1)S(1)} %collective-permute-done.1.refs_1_.b, bf16[8,32,640]{2,1,0:T(8,128)(2,1)S(1)} %bitcast.6, bf16[8,32,640]{2,1,0:T(8,128)(2,1)S(1)} %bitcast.7, ...), custom_call_target="tpu_custom_call" | custom-call | flops 1887436800 | bytes 7372800 | tf_op jit(solution)/shard_map/pallas_call | solution.py:126
  27.4 0.8 collective-permute-done.4.third
  28.1 3.6 %collective-permute-done.2.first = bf16[288,640]{1,0:T(8,128)(2,1)S(1)} collective-permute-done((bf16[288,640]{1,0:T(8,128)(2,1)}, bf16[288,640]{1,0:T(8,128)(2,1)S(1)}, u32[]{:S(2)}, u32[]{:S(2)}) %collective-permute-start.2) | collective-permute-done | bytes 368672 | tf_op jit(solution)/shard_map/ppermute | solution.py:556
  31.7 0.7 shard_map.97
  32.5 1.1 %copy-done = bf16[4,288,640]{2,1,0:T(8,128)(2,1)} copy-done((bf16[4,288,640]{2,1,0:T(8,128)(2,1)}, bf16[4,288,640]{2,1,0:T(8,128)(2,1)S(1)}, u32[]{:S(2)}) %copy-start) | copy-done | bytes 1474584
  33.6 1.0 collective-permute-start.8
  34.6 4.8 %all-to-all-start = ((bf16[8,2,32,640]{3,2,1,0:T(8,128)(2,1)}), bf16[8,2,32,640]{3,2,1,0:T(8,128)(2,1)S(1)}, u32[]{:S(2)}, u32[]{:S(2)}) async-start(bf16[8,2,32,640]{3,2,1,0:T(8,128)(2,1)} %shard_map.95.refs_0_), calls=%async_computation | async-start | bytes 1310720 | tf_op jit(solution)/shard_map/all_to_all | solution.py:613
  39.4 0.1 collective-permute-start.6
  39.6 9.5 %all-to-all-done.b.refs_0_.refs_1_.refs_2_ = bf16[8,2,32,640]{3,2,1,0:T(8,128)(2,1)S(1)} async-done(((bf16[8,2,32,640]{3,2,1,0:T(8,128)(2,1)}), bf16[8,2,32,640]{3,2,1,0:T(8,128)(2,1)S(1)}, u32[]{:S(2)}, u32[]{:S(2)}) %all-to-all-start) | async-done | bytes 655392 | tf_op jit(solution)/shard_map/all_to_all | solution.py:613
  49.1 0.1 collective-permute-start.9
  49.2 0.4 collective-permute-start.7
  49.6 2.8 %collective-permute-done.7.refs_5_ = bf16[288,640]{1,0:T(8,128)(2,1)S(1)} collective-permute-done((bf16[288,640]{1,0:T(8,128)(2,1)S(1)}, bf16[288,640]{1,0:T(8,128)(2,1)S(1)}, u32[]{:S(2)}, u32[]{:S(2)}) %collective-permute-start.7) | collective-permute-done | bytes 368672 | tf_op jit(solution)/shard_map/ppermute | solution.py:234
  52.4 3.8 %shard_map.99 = (bf16[256,640]{1,0:T(8,128)(2,1)S(1)}, bf16[256,640]{1,0:T(8,128)(2,1)S(1)}, bf16[8,240,640]{2,1,0:T(8,128)(2,1)S(1)}, bf16[8,80,2560]{2,1,0:T(8,128)(2,1)S(1)}) custom-call(bf16[8,2,32,640]{3,2,1,0:T(8,128)(2,1)S(1)} %all-to-all-done.b.refs_0_.refs_1_.refs_2_, f32[1,640]{1,0:T(1,128)S(1)} %reshape.9.refs_1_.refs_3_, ...), custom_call_target="tpu_custom_call" | custom-call | flops 629145600 | bytes 2457600 | tf_op jit(solution)/shard_map/pallas_call | solution.py:306
  56.2 4.4 %shard_map.100 = (bf16[8,2,16,1920]{3,2,1,0:T(8,128)(2,1)S(1)}, bf16[256,640]{1,0:T(8,128)(2,1)S(1)}, bf16[4,4,80,640]{3,2,1,0:T(8,128)(2,1)S(1)}) custom-call(bf16[256,640]{1,0:T(8,128)(2,1)S(1)} %get-tuple-element.36.refs_0_, bf16[8,2,32,640]{3,2,1,0:T(8,128)(2,1)S(1)} %all-to-all-done.b.refs_0_.refs_1_.refs_2_, ...), custom_call_target="tpu_custom_call" | custom-call | flops 1677721600 | bytes 3276800 | tf_op jit(solution)/shard_map/pallas_call | solution.py:446
  60.6 0.1 collective-permute-start.10
  60.7 1.1 %shard_map.101.refs_0_ = bf16[4,4,80,640]{3,2,1,0:T(8,128)(2,1)S(1)} custom-call(bf16[256,640]{1,0:T(8,128)(2,1)S(1)} %get-tuple-element.36.refs_0_, bf16[256,640]{1,0:T(8,128)(2,1)S(1)} %get-tuple-element.41.refs_1_, bf16[8,2,32,640]{3,2,1,0:T(8,128)(2,1)S(1)} %all-to-all-done.b.refs_0_.refs_1_.refs_2_, ...), custom_call_target="tpu_custom_call" | custom-call | flops 419430400 | bytes 1638400 | tf_op jit(solution)/shard_map/pallas_call | solution.py:434
  61.9 2.4 %collective-permute-done.10.refs_1_ = bf16[4,4,80,640]{3,2,1,0:T(8,128)(2,1)S(1)} collective-permute-done((bf16[4,4,80,640]{3,2,1,0:T(8,128)(2,1)S(1)}, bf16[4,4,80,640]{3,2,1,0:T(8,128)(2,1)S(1)}, u32[]{:S(2)}, u32[]{:S(2)}) %collective-permute-start.10) | collective-permute-done | bytes 1638432 | tf_op jit(solution)/shard_map/ppermute | solution.py:234
  64.2 1.0 shard_map.102
  65.3 2.1 %collective-permute-start.14 = (bf16[4,80,640]{2,1,0:T(8,128)(2,1)S(1)}, bf16[4,80,640]{2,1,0:T(8,128)(2,1)S(1)}, u32[]{:S(2)}, u32[]{:S(2)}) collective-permute-start(bf16[4,80,640]{2,1,0:T(8,128)(2,1)S(1)} %get-tuple-element.46), channel_id=1, source_target_pairs={{0,64},{4,20},{8,72},{12,28},{16,80},{20,4},{24,88},{28,12},{32,96... | collective-permute-start | bytes 1228808 | tf_op jit(solution)/shard_map/ppermute | solution.py:574
  67.4 1.2 %collective-permute-start.15 = (bf16[4,80,640]{2,1,0:T(8,128)(2,1)S(1)}, bf16[4,80,640]{2,1,0:T(8,128)(2,1)S(1)}, u32[]{:S(2)}, u32[]{:S(2)}) collective-permute-start(bf16[4,80,640]{2,1,0:T(8,128)(2,1)S(1)} %get-tuple-element.47), channel_id=1, source_target_pairs={{0,96},{4,28},{8,104},{12,4},{16,112},{20,12},{24,120},{28,20},{32... | collective-permute-start | bytes 1228808 | tf_op jit(solution)/shard_map/ppermute | solution.py:574
  68.6 3.7 %shard_map.103 = bf16[8,32,640]{2,1,0:T(8,128)(2,1)} custom-call(bf16[8,2,16,1920]{3,2,1,0:T(8,128)(2,1)S(1)} %get-tuple-element.38.refs_3_.refs_0_, bf16[256,640]{1,0:T(8,128)(2,1)S(1)} %get-tuple-element.39.refs_1_, bf16[8,2,32,640]{3,2,1,0:T(8,128)(2,1)S(1)} %all-to-all-done.b.refs_0_.refs_1_.refs_2_, f32[1,640]{1,0:T(1,128)S(1)} %reshape.9.refs_1_.refs_3_, ...), custom_call_target="tpu_custom_call" | custom-call | flops 1258291200 | bytes 5734400 | tf_op jit(solution)/shard_map/pallas_call | solution.py:489
  72.2 5.4 %all-to-all-start.1 = ((bf16[8,32,640]{2,1,0:T(8,128)(2,1)}), bf16[8,32,640]{2,1,0:T(8,128)(2,1)S(1)}, u32[]{:S(2)}, u32[]{:S(2)}) async-start(bf16[8,32,640]{2,1,0:T(8,128)(2,1)} %shard_map.103), calls=%async_computation.1 | async-start | bytes 655360 | tf_op jit(solution)/shard_map/all_to_all | solution.py:613
  77.7 1.4 %collective-permute-done.13.refs_1_ = bf16[4,80,640]{2,1,0:T(8,128)(2,1)S(1)} collective-permute-done((bf16[4,80,640]{2,1,0:T(8,128)(2,1)}, bf16[4,80,640]{2,1,0:T(8,128)(2,1)S(1)}, u32[]{:S(2)}, u32[]{:S(2)}) %collective-permute-start.13) | collective-permute-done | bytes 409632 | tf_op jit(solution)/shard_map/ppermute | solution.py:574
  79.0 0.7 collective-permute-done.15.refs_3_
  79.7 0.6 shard_map.105
  80.3 2.2 %collective-permute-start.16 = (bf16[2,80,320]{2,1,0:T(8,128)(2,1)S(1)}, bf16[2,80,320]{2,1,0:T(8,128)(2,1)S(1)}, u32[]{:S(2)}, u32[]{:S(2)}) collective-permute-start(bf16[2,80,320]{2,1,0:T(8,128)(2,1)S(1)} %get-tuple-element.49), channel_id=1, source_target_pairs={{0,8},{4,36},{8,16},{12,44},{16,24},{20,52},{24,0},{28,60},{32,40}... | collective-permute-start | bytes 307208 | tf_op jit(solution)/shard_map/ppermute | solution.py:574
  82.5 0.8 collective-permute-start.17
  83.2 0.7 collective-permute-start.18
  83.9 0.9 collective-permute-start.12
  84.8 2.1 %collective-permute-start.11 = (bf16[1,32,640]{2,1,0:T(8,128)(2,1)S(1)}, bf16[1,32,640]{2,1,0:T(8,128)(2,1)S(1)}, u32[]{:S(2)}, u32[]{:S(2)}) collective-permute-start(bf16[1,32,640]{2,1,0:T(8,128)(2,1)S(1)} %get-tuple-element.58), channel_id=1, source_target_pairs={{0,1},{1,2},{2,3},{3,0},{4,5},{5,6},{6,7},{7,4},{8,9},{9,10},{10,1... | collective-permute-start | bytes 122888 | tf_op jit(solution)/shard_map/ppermute | solution.py:607
  86.9 2.0 %collective-permute-done.17.refs_2_ = bf16[2,80,320]{2,1,0:T(8,128)(2,1)S(1)} collective-permute-done((bf16[2,80,320]{2,1,0:T(8,128)(2,1)S(1)}, bf16[2,80,320]{2,1,0:T(8,128)(2,1)S(1)}, u32[]{:S(2)}, u32[]{:S(2)}) %collective-permute-start.17) | collective-permute-done | bytes 102432 | tf_op jit(solution)/shard_map/ppermute | solution.py:574
  88.9 1.2 %collective-permute-done.18.refs_3_ = bf16[2,80,320]{2,1,0:T(8,128)(2,1)S(1)} collective-permute-done((bf16[2,80,320]{2,1,0:T(8,128)(2,1)S(1)}, bf16[2,80,320]{2,1,0:T(8,128)(2,1)S(1)}, u32[]{:S(2)}, u32[]{:S(2)}) %collective-permute-start.18) | collective-permute-done | bytes 102432 | tf_op jit(solution)/shard_map/ppermute | solution.py:574
  90.2 0.9 shard_map.106
  91.1 3.3 %all-to-all-start.2 = ((bf16[4,2,80,80]{3,2,1,0:T(8,128)(2,1)}), bf16[4,2,80,80]{3,2,1,0:T(8,128)(2,1)S(1)}, u32[]{:S(2)}, u32[]{:S(2)}) async-start(bf16[4,2,80,80]{3,2,1,0:T(8,128)(2,1)} %shard_map.106), calls=%async_computation.2 | async-start | bytes 327680 | tf_op jit(solution)/shard_map/all_to_all | solution.py:597
  94.4 5.8 %shard_map.104 = (bf16[8,32,640]{2,1,0:T(8,128)(2,1)}, f32[8,128]{1,0:T(8,128)S(1)}) custom-call(bf16[8,32,640]{2,1,0:T(8,128)(2,1)S(1)} %all-to-all-done.1.refs_0_, bf16[1,32,640]{2,1,0:T(8,128)(2,1)S(1)} %collective-permute-done.11.refs_1_, bf16[1,32,640]{2,1,0:T(8,128)(2,1)S(1)} %collective-permute-done.12.refs_2_, bf16[3,3,640,640]{3,2,1,0:T(8,128)(2,1)} %refs_3_.1), custom_call_target="tpu_custom_call" | custom-call | flops 1887436800 | bytes 7372800 | tf_op jit(solution)/shard_map/pallas_call | solution.py:144
  100.2 3.4 %all-to-all-done.2.refs_0_ = bf16[4,2,80,80]{3,2,1,0:T(8,128)(2,1)S(1)} async-done(((bf16[4,2,80,80]{3,2,1,0:T(8,128)(2,1)}), bf16[4,2,80,80]{3,2,1,0:T(8,128)(2,1)S(1)}, u32[]{:S(2)}, u32[]{:S(2)}) %all-to-all-start.2) | async-done | bytes 102432 | tf_op jit(solution)/shard_map/all_to_all | solution.py:597
  103.6 0.1 shard_map.107
  103.6 0.6 collective-permute-start.19
  104.2 3.3 %collective-permute-done.19.refs_1_ = bf16[80,80]{1,0:T(8,128)(2,1)S(1)} collective-permute-done((bf16[80,80]{1,0:T(8,128)(2,1)S(1)}, bf16[80,80]{1,0:T(8,128)(2,1)S(1)}, u32[]{:S(2)}, u32[]{:S(2)}) %collective-permute-start.19) | collective-permute-done | bytes 12832 | tf_op jit(solution)/shard_map/ppermute | solution.py:601
  107.5 0.7 shard_map.108
  (27 shorter events, 0.1 us)
Async XLA Ops:
  0.6 21.2 %copy-start.2 = (bf16[1,1,8,32,640]{4,3,2,1,0:T(8,128)(2,1)S(1)}, bf16[1,1,8,32,640]{4,3,2,1,0:T(8,128)(2,1)}, u32[]{:S(2)}) copy-start(bf16[1,1,8,32,640]{4,3,2,1,0:T(8,128)(2,1)} %param.7) | copy-start | bytes 983044
  0.6 21.2 %copy-start.4 = (bf16[1,1,8,32,640]{4,3,2,1,0:T(8,128)(2,1)S(1)}, bf16[1,1,8,32,640]{4,3,2,1,0:T(8,128)(2,1)}, u32[]{:S(2)}) copy-start(bf16[1,1,8,32,640]{4,3,2,1,0:T(8,128)(2,1)} %param.13) | copy-start | bytes 983044
  2.9 11.0 %collective-permute-start.1 = (bf16[1,32,640]{2,1,0:T(8,128)(2,1)}, bf16[1,32,640]{2,1,0:T(8,128)(2,1)S(1)}, u32[]{:S(2)}, u32[]{:S(2)}) collective-permute-start(bf16[1,32,640]{2,1,0:T(8,128)(2,1)} %get-tuple-element.31), channel_id=1, source_target_pairs={{0,3},{1,0},{2,1},{3,2},{4,7},{5,4},{6,5},{7,6},{8,11},{9,8},{10,9... | collective-permute-start | bytes 122888 | tf_op jit(solution)/shard_map/ppermute | solution.py:608
  9.3 18.8 %collective-permute-start.4 = (bf16[288,640]{1,0:T(8,128)(2,1)}, bf16[288,640]{1,0:T(8,128)(2,1)S(1)}, u32[]{:S(2)}, u32[]{:S(2)}) collective-permute-start(bf16[288,640]{1,0:T(8,128)(2,1)} %get-tuple-element.32.own), channel_id=1, source_target_pairs={{0,96},{32,0},{64,32},{96,64},{1,97},{33,1},{65,33},{97,65},{2,98}... | collective-permute-start | bytes 1105928 | tf_op jit(solution)/shard_map/ppermute | solution.py:556
  12.3 15.8 %collective-permute-start.3 = (bf16[288,640]{1,0:T(8,128)(2,1)}, bf16[288,640]{1,0:T(8,128)(2,1)S(1)}, u32[]{:S(2)}, u32[]{:S(2)}) collective-permute-start(bf16[288,640]{1,0:T(8,128)(2,1)} %get-tuple-element.32.own), channel_id=1, source_target_pairs={{0,64},{32,96},{64,0},{96,32},{1,65},{33,97},{65,1},{97,33},{2,66}... | collective-permute-start | bytes 1105928 | tf_op jit(solution)/shard_map/ppermute | solution.py:556
  12.9 18.8 %collective-permute-start.2 = (bf16[288,640]{1,0:T(8,128)(2,1)}, bf16[288,640]{1,0:T(8,128)(2,1)S(1)}, u32[]{:S(2)}, u32[]{:S(2)}) collective-permute-start(bf16[288,640]{1,0:T(8,128)(2,1)} %get-tuple-element.32.own), channel_id=1, source_target_pairs={{0,32},{32,64},{64,96},{96,0},{1,33},{33,65},{65,97},{97,1},{2,34}... | collective-permute-start | bytes 1105928 | tf_op jit(solution)/shard_map/ppermute | solution.py:556
  13.9 17.8 %collective-permute-start.5 = (bf16[288,640]{1,0:T(8,128)(2,1)}, bf16[288,640]{1,0:T(8,128)(2,1)S(1)}, u32[]{:S(2)}, u32[]{:S(2)}) collective-permute-start(bf16[288,640]{1,0:T(8,128)(2,1)} %shard_map.96), channel_id=1, source_target_pairs={{0,131},{4,132},{128,0},{132,5},{1,128},{5,133},{129,1},{133,6},{2... | collective-permute-start | bytes 1105928 | tf_op jit(solution)/shard_map/ppermute | solution.py:230
  15.2 6.7 %collective-permute-start = (bf16[1,32,640]{2,1,0:T(8,128)(2,1)}, bf16[1,32,640]{2,1,0:T(8,128)(2,1)S(1)}, u32[]{:S(2)}, u32[]{:S(2)}) collective-permute-start(bf16[1,32,640]{2,1,0:T(8,128)(2,1)} %get-tuple-element.30), channel_id=1, source_target_pairs={{0,1},{1,2},{2,3},{3,0},{4,5},{5,6},{6,7},{7,4},{8,9},{9,10},{10,1... | collective-permute-start | bytes 122888 | tf_op jit(solution)/shard_map/ppermute | solution.py:607
  21.9 9.8 %copy-start.3 = (bf16[288,640]{1,0:T(8,128)(2,1)S(1)}, bf16[288,640]{1,0:T(8,128)(2,1)}, u32[]{:S(2)}) copy-start(bf16[288,640]{1,0:T(8,128)(2,1)} %get-tuple-element.32.own) | copy-start | bytes 1105924
  32.5 1.1 %copy-start = (bf16[4,288,640]{2,1,0:T(8,128)(2,1)}, bf16[4,288,640]{2,1,0:T(8,128)(2,1)S(1)}, u32[]{:S(2)}) copy-start(bf16[4,288,640]{2,1,0:T(8,128)(2,1)S(1)} %get-tuple-element.34.refs_2_) | copy-start | bytes 4423684
  33.6 15.5 %collective-permute-start.8 = (bf16[3,288,640]{2,1,0:T(8,128)(2,1)S(1)}, bf16[3,288,640]{2,1,0:T(8,128)(2,1)S(1)}, u32[]{:S(2)}, u32[]{:S(2)}) collective-permute-start(bf16[3,288,640]{2,1,0:T(8,128)(2,1)S(1)} %get-tuple-element.35), channel_id=1, source_target_pairs={{0,131},{4,132},{128,0},{132,5},{1,128},{5,133},{129,1},{133,6},{2... | collective-permute-start | bytes 3317768 | tf_op jit(solution)/shard_map/ppermute | solution.py:230
  34.6 14.5 %all-to-all-start = ((bf16[8,2,32,640]{3,2,1,0:T(8,128)(2,1)}), bf16[8,2,32,640]{3,2,1,0:T(8,128)(2,1)S(1)}, u32[]{:S(2)}, u32[]{:S(2)}) async-start(bf16[8,2,32,640]{3,2,1,0:T(8,128)(2,1)} %shard_map.95.refs_0_), calls=%async_computation | async-start | bytes 1310720 | tf_op jit(solution)/shard_map/all_to_all | solution.py:613
  39.4 10.2 %copy-start.5 = (f32[640]{0:T(1024)S(1)}, f32[640]{0:T(1024)}, u32[]{:S(2)}) copy-start(f32[640]{0:T(1024)} %param.12) | copy-start | bytes 7684
  39.4 13.0 %collective-permute-start.6 = (bf16[4,288,640]{2,1,0:T(8,128)(2,1)}, bf16[4,288,640]{2,1,0:T(8,128)(2,1)}, u32[]{:S(2)}, u32[]{:S(2)}) collective-permute-start(bf16[4,288,640]{2,1,0:T(8,128)(2,1)} %copy-done), channel_id=1, source_target_pairs={{0,4},{4,0},{1,5},{5,1},{2,6},{6,2},{3,7},{7,3},{8,12},{12,8},{9,1... | collective-permute-start | bytes 4423688 | tf_op jit(solution)/shard_map/ppermute | solution.py:234
  49.1 3.3 %copy-start.1 = (bf16[4,288,640]{2,1,0:T(8,128)(2,1)S(1)}, bf16[4,288,640]{2,1,0:T(8,128)(2,1)}, u32[]{:S(2)}) copy-start(bf16[4,288,640]{2,1,0:T(8,128)(2,1)} %copy-done) | copy-start | bytes 4423684
  49.1 3.3 %collective-permute-start.9 = (bf16[3,288,640]{2,1,0:T(8,128)(2,1)S(1)}, bf16[3,288,640]{2,1,0:T(8,128)(2,1)S(1)}, u32[]{:S(2)}, u32[]{:S(2)}) collective-permute-start(bf16[3,288,640]{2,1,0:T(8,128)(2,1)S(1)} %shard_map.98.refs_6_), channel_id=1, source_target_pairs={{0,4},{4,0},{1,5},{5,1},{2,6},{6,2},{3,7},{7,3},{8,12},{12,8},{9,1... | collective-permute-start | bytes 3317768 | tf_op jit(solution)/shard_map/ppermute | solution.py:234
  49.2 3.2 %collective-permute-start.7 = (bf16[288,640]{1,0:T(8,128)(2,1)S(1)}, bf16[288,640]{1,0:T(8,128)(2,1)S(1)}, u32[]{:S(2)}, u32[]{:S(2)}) collective-permute-start(bf16[288,640]{1,0:T(8,128)(2,1)S(1)} %collective-permute-done.5.refs_1_.refs_4_), channel_id=1, source_target_pairs={{0,4},{4,0},{1,5},{5,1},{2,6},{6,2},{3,7},{7,3},{8,12},{12,8},{9,1... | collective-permute-start | bytes 1105928 | tf_op jit(solution)/shard_map/ppermute | solution.py:234
  60.6 3.6 %collective-permute-start.10 = (bf16[4,4,80,640]{3,2,1,0:T(8,128)(2,1)S(1)}, bf16[4,4,80,640]{3,2,1,0:T(8,128)(2,1)S(1)}, u32[]{:S(2)}, u32[]{:S(2)}) collective-permute-start(bf16[4,4,80,640]{3,2,1,0:T(8,128)(2,1)S(1)} %get-tuple-element.42), channel_id=1, source_target_pairs={{0,4},{4,0},{1,5},{5,1},{2,6},{6,2},{3,7},{7,3},{8,12},{12,8},{9,1... | collective-permute-start | bytes 4915208 | tf_op jit(solution)/shard_map/ppermute | solution.py:234
  65.3 13.8 %collective-permute-start.13 = (bf16[4,80,640]{2,1,0:T(8,128)(2,1)}, bf16[4,80,640]{2,1,0:T(8,128)(2,1)S(1)}, u32[]{:S(2)}, u32[]{:S(2)}) collective-permute-start(bf16[4,80,640]{2,1,0:T(8,128)(2,1)} %get-tuple-element.45), channel_id=1, source_target_pairs={{0,32},{4,12},{8,40},{12,20},{16,48},{20,28},{24,56},{28,4},{32,64... | collective-permute-start | bytes 1228808 | tf_op jit(solution)/shard_map/ppermute | solution.py:574
  65.3 13.8 %collective-permute-start.14 = (bf16[4,80,640]{2,1,0:T(8,128)(2,1)S(1)}, bf16[4,80,640]{2,1,0:T(8,128)(2,1)S(1)}, u32[]{:S(2)}, u32[]{:S(2)}) collective-permute-start(bf16[4,80,640]{2,1,0:T(8,128)(2,1)S(1)} %get-tuple-element.46), channel_id=1, source_target_pairs={{0,64},{4,20},{8,72},{12,28},{16,80},{20,4},{24,88},{28,12},{32,96... | collective-permute-start | bytes 1228808 | tf_op jit(solution)/shard_map/ppermute | solution.py:574
  67.4 12.4 %collective-permute-start.15 = (bf16[4,80,640]{2,1,0:T(8,128)(2,1)S(1)}, bf16[4,80,640]{2,1,0:T(8,128)(2,1)S(1)}, u32[]{:S(2)}, u32[]{:S(2)}) collective-permute-start(bf16[4,80,640]{2,1,0:T(8,128)(2,1)S(1)} %get-tuple-element.47), channel_id=1, source_target_pairs={{0,96},{4,28},{8,104},{12,4},{16,112},{20,12},{24,120},{28,20},{32... | collective-permute-start | bytes 1228808 | tf_op jit(solution)/shard_map/ppermute | solution.py:574
  72.2 11.6 %all-to-all-start.1 = ((bf16[8,32,640]{2,1,0:T(8,128)(2,1)}), bf16[8,32,640]{2,1,0:T(8,128)(2,1)S(1)}, u32[]{:S(2)}, u32[]{:S(2)}) async-start(bf16[8,32,640]{2,1,0:T(8,128)(2,1)} %shard_map.103), calls=%async_computation.1 | async-start | bytes 655360 | tf_op jit(solution)/shard_map/all_to_all | solution.py:613
  80.3 6.6 %collective-permute-start.16 = (bf16[2,80,320]{2,1,0:T(8,128)(2,1)S(1)}, bf16[2,80,320]{2,1,0:T(8,128)(2,1)S(1)}, u32[]{:S(2)}, u32[]{:S(2)}) collective-permute-start(bf16[2,80,320]{2,1,0:T(8,128)(2,1)S(1)} %get-tuple-element.49), channel_id=1, source_target_pairs={{0,8},{4,36},{8,16},{12,44},{16,24},{20,52},{24,0},{28,60},{32,40}... | collective-permute-start | bytes 307208 | tf_op jit(solution)/shard_map/ppermute | solution.py:574
  82.5 6.5 %collective-permute-start.17 = (bf16[2,80,320]{2,1,0:T(8,128)(2,1)S(1)}, bf16[2,80,320]{2,1,0:T(8,128)(2,1)S(1)}, u32[]{:S(2)}, u32[]{:S(2)}) collective-permute-start(bf16[2,80,320]{2,1,0:T(8,128)(2,1)S(1)} %get-tuple-element.50), channel_id=1, source_target_pairs={{0,16},{4,68},{8,24},{12,76},{16,0},{20,84},{24,8},{28,92},{32,48}... | collective-permute-start | bytes 307208 | tf_op jit(solution)/shard_map/ppermute | solution.py:574
  83.2 6.9 %collective-permute-start.18 = (bf16[2,80,320]{2,1,0:T(8,128)(2,1)S(1)}, bf16[2,80,320]{2,1,0:T(8,128)(2,1)S(1)}, u32[]{:S(2)}, u32[]{:S(2)}) collective-permute-start(bf16[2,80,320]{2,1,0:T(8,128)(2,1)S(1)} %get-tuple-element.51), channel_id=1, source_target_pairs={{0,24},{4,100},{8,0},{12,108},{16,8},{20,116},{24,16},{28,124},{32... | collective-permute-start | bytes 307208 | tf_op jit(solution)/shard_map/ppermute | solution.py:574
  83.9 10.5 %collective-permute-start.12 = (bf16[1,32,640]{2,1,0:T(8,128)(2,1)S(1)}, bf16[1,32,640]{2,1,0:T(8,128)(2,1)S(1)}, u32[]{:S(2)}, u32[]{:S(2)}) collective-permute-start(bf16[1,32,640]{2,1,0:T(8,128)(2,1)S(1)} %get-tuple-element.57), channel_id=1, source_target_pairs={{0,3},{1,0},{2,1},{3,2},{4,7},{5,4},{6,5},{7,6},{8,11},{9,8},{10,9... | collective-permute-start | bytes 122888 | tf_op jit(solution)/shard_map/ppermute | solution.py:608
  84.8 9.6 %collective-permute-start.11 = (bf16[1,32,640]{2,1,0:T(8,128)(2,1)S(1)}, bf16[1,32,640]{2,1,0:T(8,128)(2,1)S(1)}, u32[]{:S(2)}, u32[]{:S(2)}) collective-permute-start(bf16[1,32,640]{2,1,0:T(8,128)(2,1)S(1)} %get-tuple-element.58), channel_id=1, source_target_pairs={{0,1},{1,2},{2,3},{3,0},{4,5},{5,6},{6,7},{7,4},{8,9},{9,10},{10,1... | collective-permute-start | bytes 122888 | tf_op jit(solution)/shard_map/ppermute | solution.py:607
  91.1 12.5 %all-to-all-start.2 = ((bf16[4,2,80,80]{3,2,1,0:T(8,128)(2,1)}), bf16[4,2,80,80]{3,2,1,0:T(8,128)(2,1)S(1)}, u32[]{:S(2)}, u32[]{:S(2)}) async-start(bf16[4,2,80,80]{3,2,1,0:T(8,128)(2,1)} %shard_map.106), calls=%async_computation.2 | async-start | bytes 327680 | tf_op jit(solution)/shard_map/all_to_all | solution.py:597
  103.6 3.9 %collective-permute-start.19 = (bf16[80,80]{1,0:T(8,128)(2,1)S(1)}, bf16[80,80]{1,0:T(8,128)(2,1)S(1)}, u32[]{:S(2)}, u32[]{:S(2)}) collective-permute-start(bf16[80,80]{1,0:T(8,128)(2,1)S(1)} %get-tuple-element.54), channel_id=1, source_target_pairs={{0,128},{128,0},{1,129},{129,1},{2,130},{130,2},{3,131},{131,3},{4... | collective-permute-start | bytes 38408 | tf_op jit(solution)/shard_map/ppermute | solution.py:601
